TPU v7x, 128 devices: a whole 4x4x4 slice. The times are simulated.
128 devices in a mesh: mode: 8 (over x, core), mer: 16 (over z, y).
Axes of the slice: x: 4, y: 4, z: 4, core: 2. Of those that a mesh axis runs over, the one named last changes fastest.
Arguments:
- cotangent: float32 [9, 9, 262144], P(None, None, ('mer', 'mode')), may hold values from -6 to 6
- checkpoint: float32 [9, 9, 262144], P(None, None, ('mer', 'mode')), may hold values from -0.25 to 0.25
- mass: float32 [9, 9, 256], P(None, None, 'mer'), may hold values from 0.5 to 2
- inv_radius_sq: float32 [9, 9, 256], P(None, None, 'mer'), may hold values from 0.25 to 4
- derivative: float32 [9, 9], replicated, may hold values from -2 to 2
Outputs:
- sensitivity: float32 [9, 9, 262144], P(None, None, ('mer', 'mode'))
All inputs are finite; a program needn't handle non-finite values.
Results may differ from a plain program's by a relative error of at most 0.0001.
Values sent between devices are 32-bit elements; how exact they have to be, the bound alone decides.
A program may use at most 128 MiB of HBM per device.

v0:
```python
import math

import jax
import jax.numpy as jnp
from jax import lax
from jax.sharding import PartitionSpec as P

NODE = 9
RADIAL = 8
ITERS = 4


STEP_RATE = 1.0
AZIMUTH_WEIGHT = 4.0
PENALTY = 1.0
HIGHEST = lax.Precision.HIGHEST


def padded_2(cells, sides, width):
    for axis, dim in sides:
        count = lax.axis_size(axis)
        ends = count - 1
        head = lax.slice_in_dim(cells, 0, width, axis=dim)
        tail = lax.slice_in_dim(cells, cells.shape[dim] - width, cells.shape[dim], axis=dim)
        cells = jnp.concatenate(
            [
                lax.ppermute(tail, axis, [(i, (i + 1) % count) for i in range(ends)]),
                cells,
                lax.ppermute(head, axis, [((i + 1) % count, i) for i in range(ends)]),
            ],
            axis=dim,
        )
    return cells


def plane_angles(group_total, local_modes, plane_total):
    shape_full = (group_total, 2, local_modes, plane_total)
    group_ids = lax.broadcasted_iota(jnp.int32, shape_full, 0)
    part_ids = lax.broadcasted_iota(jnp.int32, shape_full, 1)
    inner_ids = lax.broadcasted_iota(jnp.int32, shape_full, 2)
    plane_ids = lax.broadcasted_iota(jnp.int32, shape_full, 3)
    mode_order = group_ids * local_modes + inner_ids
    phase_index = mode_order * plane_ids % plane_total
    angles = phase_index.astype(jnp.float32) * (2.0 * math.pi / plane_total)
    return (part_ids, mode_order, angles)


def plane_table(group_total, local_modes, plane_total):
    part_ids, mode_order, angles = plane_angles(group_total, local_modes, plane_total)
    values = jnp.where(part_ids == 0, jnp.cos(angles), -jnp.sin(angles))
    return values.reshape(group_total * 2 * local_modes, plane_total)


def turned_table(group_total, local_modes, plane_total):
    part_ids, mode_order, angles = plane_angles(group_total, local_modes, plane_total)
    fraction = mode_order.astype(jnp.float32) / (group_total * local_modes)
    values = jnp.where(part_ids == 0, -fraction * jnp.sin(angles), -fraction * jnp.cos(angles))
    return values.reshape(group_total * 2 * local_modes, plane_total)


def shards(cotangent, checkpoint, mass, inv_radius_sq, derivative):
    group_total = lax.axis_size("mode")
    mode_group = lax.axis_index("mode")
    place = lax.axis_index("mer")
    place_total = lax.axis_size("mer")
    elem_dev = mass.shape[2]
    axial_dev = elem_dev // RADIAL
    width = cotangent.shape[2]
    local_modes = width // (elem_dev * 2)
    mode_total = local_modes * group_total
    coeff_total = 2 * mode_total
    plane_total = 2 * mode_total
    elem_sub = elem_dev // group_total
    plane_rows = NODE * NODE * elem_sub
    lane_axial = RADIAL * 2 * local_modes
    lane_inner = 2 * local_modes
    stiffness = jnp.dot(
        derivative.T, derivative, precision=HIGHEST, preferred_element_type=jnp.float32
    )
    mode_number = mode_group * local_modes + jnp.arange(local_modes, dtype=jnp.int32)
    mode_fraction = mode_number.astype(jnp.float32) / mode_total
    spectral_weight = jnp.where(mode_number == 0, 1.0 / plane_total, 2.0 / plane_total).astype(
        jnp.float32
    )
    weight_full = jnp.tile(spectral_weight, elem_dev * 2)
    factor = (
        STEP_RATE + AZIMUTH_WEIGHT * mode_fraction * mode_fraction * inv_radius_sq[..., None, None]
    )
    diagonal = jnp.broadcast_to(
        mass[..., None, None] * factor, (NODE, NODE, elem_dev, 2, local_modes)
    ).reshape(NODE, NODE, width)
    mass_full = jnp.broadcast_to(mass[..., None], (NODE, NODE, elem_dev, 2 * local_modes)).reshape(
        NODE, NODE, width
    )
    transform = plane_table(group_total, local_modes, plane_total)
    both_tables = jnp.concatenate(
        [transform, turned_table(group_total, local_modes, plane_total)], axis=1
    )
    below_mask = (place > 0).astype(jnp.float32)
    above_mask = (place < place_total - 1).astype(jnp.float32)

    def operate(field):
        result = diagonal * field
        result = result + jnp.einsum("ab,bjl->ajl", stiffness, field, precision=HIGHEST)
        result = result + jnp.einsum("ab,ibl->ial", stiffness, field, precision=HIGHEST)
        field_four = field.reshape(NODE, NODE, axial_dev, lane_axial)
        jump_axial = field_four[:, NODE - 1, :-1, :] - field_four[:, 0, 1:, :]
        rims = jnp.stack([field_four[:, 0, 0, :], field_four[:, NODE - 1, axial_dev - 1, :]])
        padded = padded_2(rims, (("mer", 0),), 1)
        lower_edge = below_mask * (rims[0] - padded[0])
        upper_edge = above_mask * (rims[1] - padded[3])
        top_rows = jnp.concatenate(
            [PENALTY * jump_axial, (PENALTY * upper_edge)[:, None, :]], axis=1
        )
        bottom_rows = jnp.concatenate(
            [(PENALTY * lower_edge)[:, None, :], -PENALTY * jump_axial], axis=1
        )
        middle = jnp.zeros((NODE, NODE - 2, axial_dev, lane_axial), jnp.float32)
        axial_fix = jnp.concatenate([bottom_rows[:, None], middle, top_rows[:, None]], axis=1)
        field_five = field.reshape(NODE, NODE, axial_dev, RADIAL, lane_inner)
        jump_radial = field_five[NODE - 1, :, :, :-1, :] - field_five[0, :, :, 1:, :]
        edge_zero = jnp.zeros((NODE, axial_dev, 1, lane_inner), jnp.float32)
        outer_rows = jnp.concatenate([PENALTY * jump_radial, edge_zero], axis=2)
        inner_rows = jnp.concatenate([edge_zero, -PENALTY * jump_radial], axis=2)
        middle_radial = jnp.zeros((NODE - 2, NODE, axial_dev, RADIAL, lane_inner), jnp.float32)
        radial_fix = jnp.concatenate([inner_rows[None], middle_radial, outer_rows[None]], axis=0)
        return result + axial_fix.reshape(NODE, NODE, width) + radial_fix.reshape(NODE, NODE, width)

    def per_mode_dot(first, second):
        return jnp.sum((first * second).reshape(NODE * NODE * elem_dev * 2, local_modes), axis=0)

    def spread(values):
        return jnp.tile(values, elem_dev * 2)

    def squared_norm(residual):
        return lax.psum(per_mode_dot(residual, residual), "mer")

    def conjugate_solve(rhs):
        solution = jnp.zeros_like(rhs)
        residual = rhs
        direction = rhs
        norm_now = squared_norm(residual)
        for sweep in range(ITERS):
            applied = operate(direction)
            curvature_sum = lax.psum(per_mode_dot(direction, applied), "mer")
            step_size = spread(norm_now / curvature_sum)
            solution = solution + step_size * direction
            residual = residual - step_size * applied
            norm_next = squared_norm(residual)
            direction = residual + spread(norm_next / norm_now) * direction
            norm_now = norm_next
        return solution

    def to_planes(state, extras):
        fields = [state] + extras
        stack_count = len(fields)
        blocks = jnp.stack(fields).reshape(stack_count, NODE, NODE, elem_dev, 2 * local_modes)
        arrived = lax.all_to_all(blocks, "mode", split_axis=3, concat_axis=4, tiled=True)
        flat_rows = arrived.reshape(stack_count, plane_rows, coeff_total)
        paired = jnp.dot(
            flat_rows[0], both_tables, precision=HIGHEST, preferred_element_type=jnp.float32
        )
        pieces = [paired[:, :plane_total], paired[:, plane_total:]]
        if stack_count > 1:
            rest = lax.dot_general(
                flat_rows[1:],
                transform,
                (((2,), (0,)), ((), ())),
                precision=HIGHEST,
                preferred_element_type=jnp.float32,
            )
            pieces = pieces + [rest[0]]
        return jnp.stack(pieces)

    def to_modes(physical, table):
        stack_count = physical.shape[0]
        projected = lax.dot_general(
            physical,
            table,
            (((2,), (1,)), ((), ())),
            precision=HIGHEST,
            preferred_element_type=jnp.float32,
        )
        projected = projected.reshape(stack_count, NODE, NODE, elem_sub, coeff_total)
        arrived = lax.all_to_all(projected, "mode", split_axis=4, concat_axis=3, tiled=True)
        return arrived.reshape(stack_count, NODE, NODE, width)

    def finish(weighted, state_planes, turned_planes, adjoint_planes):
        joined = jnp.concatenate(
            [turned_planes * adjoint_planes, state_planes * adjoint_planes], axis=1
        )
        returned = to_modes(joined[None], both_tables)
        return STEP_RATE * weighted - returned[0]

    first_planes = to_planes(checkpoint, [])
    nonlinear = weight_full * to_modes((first_planes[0] * first_planes[1])[None], transform)[0]
    next_state = conjugate_solve(mass_full * (STEP_RATE * checkpoint - nonlinear))
    multiplier = conjugate_solve(cotangent)
    weighted = mass_full * multiplier
    later_planes = to_planes(next_state, [weight_full * weighted])
    adjoint = finish(weighted, later_planes[0], later_planes[1], later_planes[2])
    multiplier = conjugate_solve(adjoint)
    weighted = mass_full * multiplier
    early_planes = to_planes(checkpoint, [weight_full * weighted])
    adjoint = finish(weighted, early_planes[0], early_planes[1], early_planes[2])
    return adjoint


def solution(mesh):
    return jax.shard_map(
        shards,
        mesh=mesh,
        in_specs=(
            P(None, None, ("mer", "mode")),
            P(None, None, ("mer", "mode")),
            P(None, None, "mer"),
            P(None, None, "mer"),
            P(),
        ),
        out_specs=P(None, None, ("mer", "mode")),
        check_vma=False,
    )
```

profile of v0, /device:TPU:1, one launch (start us, length us, event | category | flops | bytes accessed | tf_op | source)
XLA Modules:
  0.0 1506.5 jit_solution(1952679150022136807)
XLA Ops:
  33.6 19.8 %negate_select_fusion.5 = (f32[1024,1024]{1,0:T(8,128)}, f32[1024,1024]{1,0:T(8,128)}) fusion(s32[1024]{0:T(1024)S(1)} %add.406, pred[1024]{0:T(1024)(128)(4,1)S(1)} %copy-done.36, f32[1024]{0:T(1024)S(1)} %copy-done.35), kind=kLoop, calls=%fused_computation.21 | loop fusion | flops 19922944 | bytes 8397824 | tf_op jit(solution)/shard_map/jit(_where)/select_n | solution.py:50
  53.4 18.1 %negate_select_fusion.4 = f32[8,2,64,1024]{3,2,1,0:T(8,128)} fusion(s32[8,2,64]{2,1,0:T(2,128)S(1)} %copy-done.32, pred[2]{0:T(512)(128)(4,1)S(1)} %copy-done.38), kind=kLoop, calls=%fused_computation.17 | loop fusion | flops 16777216 | bytes 4198402 | tf_op jit(solution)/shard_map/jit(_where)/select_n | solution.py:50
  98.4 15.0 reshape.1551
  136.1 18.8 %reshape.1552 = f32[1024,1,9,2,9]{4,3,2,1,0:T(2,128)} reshape(f32[8,20736]{1,0:T(8,128)S(1)} %reduce) | data formatting | bytes 1327104
  215.1 36.4 %all-reduce.31 = (f32[64]{0:T(128)}, f32[64]{0:T(128)}, f32[64]{0:T(128)}, f32[64]{0:T(128)}) all-reduce(f32[64]{0:T(128)S(1)} %copy-done.39, f32[64]{0:T(128)} %reduce_sum.217, f32[64]{0:T(128)} %reduce_sum.224, f32[64]{0:T(128)} %reduce_sum.225), channel_id=1, replica_groups=mesh['mode'=8,'mer'=16] {'mer'}, use_global_device_ids=true, to_apply=%region_1.2 | all-reduce | flops 256 | bytes 2048 | tf_op jit(solution)/shard_map/psum | solution.py:136
  272.4 29.1 %all-reduce.30 = (f32[64]{0:T(128)}, f32[64]{0:T(128)}) all-reduce(f32[64]{0:T(128)S(1)} %reduce_sum.218, f32[64]{0:T(128)} %reduce_sum.226), channel_id=1, replica_groups=mesh['mode'=8,'mer'=16] {'mer'}, use_global_device_ids=true, to_apply=%region_5.6 | all-reduce | flops 128 | bytes 1024 | tf_op jit(solution)/shard_map/psum | solution.py:136
  381.5 31.6 %all-reduce.29 = (f32[64]{0:T(128)}, f32[64]{0:T(128)}) all-reduce(f32[64]{0:T(128)} %reduce_sum.219, f32[64]{0:T(128)S(1)} %reduce_sum.227), channel_id=1, replica_groups=mesh['mode'=8,'mer'=16] {'mer'}, use_global_device_ids=true, to_apply=%region_7.8 | all-reduce | flops 128 | bytes 1024 | tf_op jit(solution)/shard_map/psum | solution.py:145
  436.7 29.3 %all-reduce.28 = (f32[64]{0:T(128)}, f32[64]{0:T(128)}) all-reduce(f32[64]{0:T(128)S(1)} %reduce_sum.220, f32[64]{0:T(128)} %reduce_sum.228), channel_id=1, replica_groups=mesh['mode'=8,'mer'=16] {'mer'}, use_global_device_ids=true, to_apply=%region_9.10 | all-reduce | flops 128 | bytes 1024 | tf_op jit(solution)/shard_map/psum | solution.py:136
  546.5 31.6 %all-reduce.27 = (f32[64]{0:T(128)}, f32[64]{0:T(128)}) all-reduce(f32[64]{0:T(128)} %reduce_sum.221, f32[64]{0:T(128)S(1)} %reduce_sum.229), channel_id=1, replica_groups=mesh['mode'=8,'mer'=16] {'mer'}, use_global_device_ids=true, to_apply=%region_11.12 | all-reduce | flops 128 | bytes 1024 | tf_op jit(solution)/shard_map/psum | solution.py:145
  599.4 29.6 %all-reduce.26 = (f32[64]{0:T(128)}, f32[64]{0:T(128)}) all-reduce(f32[64]{0:T(128)S(1)} %reduce_sum.222, f32[64]{0:T(128)} %reduce_sum.230), channel_id=1, replica_groups=mesh['mode'=8,'mer'=16] {'mer'}, use_global_device_ids=true, to_apply=%region_13.14 | all-reduce | flops 128 | bytes 1024 | tf_op jit(solution)/shard_map/psum | solution.py:136
  707.9 31.2 %all-reduce.25 = (f32[64]{0:T(128)}, f32[64]{0:T(128)}) all-reduce(f32[64]{0:T(128)S(1)} %reduce_sum.223, f32[64]{0:T(128)} %reduce_sum.231), channel_id=1, replica_groups=mesh['mode'=8,'mer'=16] {'mer'}, use_global_device_ids=true, to_apply=%region_15.16 | all-reduce | flops 128 | bytes 1024 | tf_op jit(solution)/shard_map/psum | solution.py:145
  760.4 77.4 %all_to_all.90 = f32[2,9,9,16,128]{4,0,2,1,3:T(2,128)S(1)} all-to-all(f32[2,9,9,16,128]{4,0,2,1,3:T(2,128)S(1)} %pad_maximum_fusion.8), channel_id=1, replica_groups=mesh['mode'=8,'mer'=16] {'mode'}, dimensions={3} | all-to-all | bytes 2654208 | tf_op jit(solution)/shard_map/all_to_all | solution.py:158
  875.8 14.4 reshape.1553
  906.7 18.7 %reshape.1554 = f32[1024,1,9,2,9]{4,3,2,1,0:T(2,128)} reshape(f32[8,20736]{1,0:T(8,128)S(1)} %reduce.1) | data formatting | bytes 1327104
  969.3 31.5 %all-reduce.24 = (f32[64]{0:T(128)}, f32[64]{0:T(128)}) all-reduce(f32[64]{0:T(128)S(1)} %reduce_sum.232, f32[64]{0:T(128)} %reduce_sum.233), channel_id=1, replica_groups=mesh['mode'=8,'mer'=16] {'mer'}, use_global_device_ids=true, to_apply=%region_33.34 | all-reduce | flops 128 | bytes 1024 | tf_op jit(solution)/shard_map/psum | solution.py:136
  1008.1 28.7 %psum.186 = f32[64]{0:T(128)S(1)} all-reduce(f32[64]{0:T(128)S(1)} %reduce_sum.234), channel_id=1, replica_groups=mesh['mode'=8,'mer'=16] {'mer'}, use_global_device_ids=true, to_apply=%region_37.38 | all-reduce | flops 64 | bytes 512 | tf_op jit(solution)/shard_map/psum | solution.py:136
  1070.7 30.3 %psum.187 = f32[64]{0:T(128)} all-reduce(f32[64]{0:T(128)S(1)} %reduce_sum.235), channel_id=1, replica_groups=mesh['mode'=8,'mer'=16] {'mer'}, use_global_device_ids=true, to_apply=%region_39.40 | all-reduce | flops 64 | bytes 512 | tf_op jit(solution)/shard_map/psum | solution.py:145
  1112.5 29.7 %psum.188 = f32[64]{0:T(128)} all-reduce(f32[64]{0:T(128)S(1)} %reduce_sum.236), channel_id=1, replica_groups=mesh['mode'=8,'mer'=16] {'mer'}, use_global_device_ids=true, to_apply=%region_41.42 | all-reduce | flops 64 | bytes 512 | tf_op jit(solution)/shard_map/psum | solution.py:136
  1182.5 30.3 %psum.189 = f32[64]{0:T(128)} all-reduce(f32[64]{0:T(128)S(1)} %reduce_sum.237), channel_id=1, replica_groups=mesh['mode'=8,'mer'=16] {'mer'}, use_global_device_ids=true, to_apply=%region_43.44 | all-reduce | flops 64 | bytes 512 | tf_op jit(solution)/shard_map/psum | solution.py:145
  1223.2 29.3 %psum.190 = f32[64]{0:T(128)} all-reduce(f32[64]{0:T(128)S(1)} %reduce_sum.238), channel_id=1, replica_groups=mesh['mode'=8,'mer'=16] {'mer'}, use_global_device_ids=true, to_apply=%region_45.46 | all-reduce | flops 64 | bytes 512 | tf_op jit(solution)/shard_map/psum | solution.py:136
  1291.6 30.0 %psum.191 = f32[64]{0:T(128)} all-reduce(f32[64]{0:T(128)} %reduce_sum.239), channel_id=1, replica_groups=mesh['mode'=8,'mer'=16] {'mer'}, use_global_device_ids=true, to_apply=%region_47.48 | all-reduce | flops 64 | bytes 512 | tf_op jit(solution)/shard_map/psum | solution.py:145
  1330.2 74.3 %all_to_all.92 = f32[2,9,9,16,128]{4,0,2,1,3:T(2,128)S(1)} all-to-all(f32[2,9,9,16,128]{4,0,2,1,3:T(2,128)S(1)} %copy.843), channel_id=1, replica_groups=mesh['mode'=8,'mer'=16] {'mode'}, dimensions={3} | all-to-all | bytes 2654208 | tf_op jit(solution)/shard_map/all_to_all | solution.py:158
  1441.3 14.4 reshape.1555
  1472.0 18.7 %reshape.1556 = f32[1024,1,9,2,9]{4,3,2,1,0:T(2,128)} reshape(f32[8,20736]{1,0:T(8,128)S(1)} %reduce.2) | data formatting | bytes 1327104
  (539 shorter events, 786.8 us)
Async XLA Ops:
  2.8 115.7 %collective-permute-start = (f32[1,9,1024]{2,0,1:T(1,128)}, f32[1,9,1024]{2,0,1:T(1,128)}, u32[]{:S(2)}, u32[]{:S(2)}) collective-permute-start(f32[1,9,1024]{2,0,1:T(1,128)} %get-tuple-element.163), channel_id=1, source_target_pairs={{0,1},{1,2},{2,3},{3,4},{4,5},{5,6},{6,7},{7,8},{8,9},{9,10},{10,1... | collective-permute-start | bytes 110600 | tf_op jit(solution)/shard_map/ppermute | solution.py:27
  7.4 111.0 %collective-permute-start.1 = (f32[1,9,1024]{2,0,1:T(1,128)}, f32[1,9,1024]{2,0,1:T(1,128)}, u32[]{:S(2)}, u32[]{:S(2)}) collective-permute-start(f32[1,9,1024]{2,0,1:T(1,128)} %get-tuple-element.164), channel_id=1, source_target_pairs={{1,0},{2,1},{3,2},{4,3},{5,4},{6,5},{7,6},{8,7},{9,8},{10,9},{11,1... | collective-permute-start | bytes 110600 | tf_op jit(solution)/shard_map/ppermute | solution.py:29
  10.4 61.1 %all-to-all-start = ((f32[1,9,9,16,128]{4,0,2,1,3:T(1,128)}), f32[1,9,9,16,128]{4,0,2,1,3:T(1,128)}, u32[]{:S(2)}, u32[]{:S(2)}) async-start(f32[1,9,9,16,128]{4,0,2,1,3:T(1,128)} %copy.745), calls=%async_computation | async-start | bytes 1327104 | tf_op jit(solution)/shard_map/all_to_all | solution.py:158
  113.5 18.8 %all-to-all-start.1 = ((f32[8,1,20736]{2,1,0:T(1,128)}), f32[8,1,20736]{2,1,0:T(1,128)}, u32[]{:S(2)}, u32[]{:S(2)}) async-start(f32[8,1,20736]{2,1,0:T(1,128)} %reshape.1551), calls=%async_computation.1 | async-start | bytes 1327104 | tf_op jit(solution)/shard_map/all_to_all | solution.py:185
  180.1 17.3 %collective-permute-start.8 = (f32[1,9,1024]{2,0,1:T(1,128)}, f32[1,9,1024]{2,0,1:T(1,128)}, u32[]{:S(2)}, u32[]{:S(2)}) collective-permute-start(f32[1,9,1024]{2,0,1:T(1,128)} %get-tuple-element.157), channel_id=1, source_target_pairs={{0,1},{1,2},{2,3},{3,4},{4,5},{5,6},{6,7},{7,8},{8,9},{9,10},{10,1... | collective-permute-start | bytes 110600 | tf_op jit(solution)/shard_map/ppermute | solution.py:27
  184.9 12.4 collective-permute-start.9
  329.5 17.0 %collective-permute-start.2 = (f32[1,9,1024]{2,0,1:T(1,128)S(1)}, f32[1,9,1024]{2,0,1:T(1,128)S(1)}, u32[]{:S(2)}, u32[]{:S(2)}) collective-permute-start(f32[1,9,1024]{2,0,1:T(1,128)S(1)} %get-tuple-element.151), channel_id=1, source_target_pairs={{0,1},{1,2},{2,3},{3,4},{4,5},{5,6},{6,7},{7,8},{8,9},{9,10},{10,1... | collective-permute-start | bytes 110600 | tf_op jit(solution)/shard_map/ppermute | solution.py:27
  332.9 13.7 collective-permute-start.3
  338.0 14.3 collective-permute-start.10
  342.6 9.7 collective-permute-start.11
  494.7 16.6 %collective-permute-start.4 = (f32[1,9,1024]{2,0,1:T(1,128)S(1)}, f32[1,9,1024]{2,0,1:T(1,128)S(1)}, u32[]{:S(2)}, u32[]{:S(2)}) collective-permute-start(f32[1,9,1024]{2,0,1:T(1,128)S(1)} %get-tuple-element.139), channel_id=1, source_target_pairs={{0,1},{1,2},{2,3},{3,4},{4,5},{5,6},{6,7},{7,8},{8,9},{9,10},{10,1... | collective-permute-start | bytes 110600 | tf_op jit(solution)/shard_map/ppermute | solution.py:27
  498.0 13.2 collective-permute-start.5
  503.2 13.9 collective-permute-start.12
  507.7 9.3 collective-permute-start.13
  658.4 16.6 %collective-permute-start.6 = (f32[1,9,1024]{2,0,1:T(1,128)S(1)}, f32[1,9,1024]{2,0,1:T(1,128)S(1)}, u32[]{:S(2)}, u32[]{:S(2)}) collective-permute-start(f32[1,9,1024]{2,0,1:T(1,128)S(1)} %get-tuple-element.127), channel_id=1, source_target_pairs={{0,1},{1,2},{2,3},{3,4},{4,5},{5,6},{6,7},{7,8},{8,9},{9,10},{10,1... | collective-permute-start | bytes 110600 | tf_op jit(solution)/shard_map/ppermute | solution.py:27
  661.8 13.2 collective-permute-start.7
  664.7 16.1 %collective-permute-start.14 = (f32[1,9,1024]{2,0,1:T(1,128)}, f32[1,9,1024]{2,0,1:T(1,128)}, u32[]{:S(2)}, u32[]{:S(2)}) collective-permute-start(f32[1,9,1024]{2,0,1:T(1,128)} %get-tuple-element.121), channel_id=1, source_target_pairs={{0,1},{1,2},{2,3},{3,4},{4,5},{5,6},{6,7},{7,8},{8,9},{9,10},{10,1... | collective-permute-start | bytes 110600 | tf_op jit(solution)/shard_map/ppermute | solution.py:27
  669.3 11.5 collective-permute-start.15
  947.1 9.8 collective-permute-start.16
  949.0 7.9 collective-permute-start.17
  1045.4 6.9 collective-permute-start.18
  1157.1 6.6 collective-permute-start.20
  1268.2 6.6 collective-permute-start.22
  1271.2 5.0 collective-permute-start.23
  (47 other events, 376.6 us)
where the time goes:
time: 1530 us; the launch traced here: 1510 us
  blocking collectives  609 us (40%)
  local copies, waits for them, and re-layouts  457 us (30%)
  other arithmetic  222 us (15%)
  matrix products  143 us (9%)
  starting transfers between devices  70.7 us (5%)
    psum x8, blocking collectives, squared_norm(): return lax.psum(per_mode_dot(residual, residual), 'mer')  244 us
    psum x6, blocking collectives, conjugate_solve(): curvature_sum = lax.psum(per_mode_dot(direction, applied), 'mer')  185 us
    all_to_all x2, blocking collectives, to_planes(): lax.all_to_all(blocks, 'mode', split_axis=3, concat_axis=4, tiled=True)  152 us
    unnamed x108, local copies, waits for them, and re-layouts  108 us
    reshape x24, local copies, waits for them, and re-layouts, per_mode_dot(): (first * second).reshape(NODE * NODE * elem_dev * 2, local_modes)  61.3 us
    dot_general x12, matrix products, operate(): jnp.einsum('ab,bjl->ajl', stiffness, field, precision=HIGHEST)  51.2 us
    reduce_sum x24, other arithmetic, per_mode_dot(): jnp.sum((first * second).reshape(NODE * NODE * elem_dev * 2, local_modes)...  46.7 us
    ppermute x12, starting transfers between devices, padded_2(): lax.ppermute(tail, axis, [(i, (i + 1) % count) for i in range(ends)])  44.3 us
  transfers between devices with their start and end apart: 26, of which 3 were waited for; matrix products, arithmetic and copies ran while one was open for 11% of the time, Pallas kernels for 0%

commit v1 on v0

v1 whole, which is shorter than its diff:
```python
import functools
import math

import jax
import jax.numpy as jnp
import ml_dtypes
import numpy as np
from jax import lax
from jax.experimental import pallas as pl
from jax.experimental.pallas import tpu as pltpu
from jax.sharding import PartitionSpec as P

NODE = 9
NODES = NODE * NODE
RADIAL = 8
ITERS = 4
MODES = 512
PLANES = 1024
ELEMENTS = 256
N_MODE = 8
N_MER = 16
ELEM_DEV = 16
GROUPS = 11
PADDED = GROUPS * 8
LANES = 128
AZIMUTH_WEIGHT = 4.0
HIGHEST = lax.Precision.HIGHEST
F32 = jnp.float32
BF16 = jnp.bfloat16


def tables():
    index = np.outer(np.arange(MODES), np.arange(MODES)) % PLANES
    angles = index.astype(np.float64) * (2.0 * math.pi / PLANES)
    out = []
    for values in (np.cos(angles), np.sin(angles)):
        values = values.astype(np.float32)
        high = values.astype(ml_dtypes.bfloat16)
        low = (values - high.astype(np.float32)).astype(ml_dtypes.bfloat16)
        out += [high, low]
    return np.stack(out)


def mix(first, second):
    shape = first.shape
    low = lax.broadcasted_iota(jnp.int32, shape, len(shape) - 2) % 8 < 4
    axis = len(shape) - 2
    return (
        jnp.where(low, first, pltpu.roll(second, 4, axis)),
        jnp.where(low, pltpu.roll(first, 4, axis), second),
    )


def exchange(tiles):
    block = lax.broadcasted_iota(jnp.int32, (8, LANES), 1) // 16
    tiles = list(tiles)
    for bit in (1, 2, 4):
        clear = (block & bit) == 0
        for at in range(8):
            if at & bit:
                continue
            one, two = tiles[at], tiles[at | bit]
            tiles[at] = jnp.where(clear, one, pltpu.roll(two, 16 * bit, 1))
            tiles[at | bit] = jnp.where(clear, pltpu.roll(one, LANES - 16 * bit, 1), two)
    return tiles


def native_to_tiles_kernel(x_ref, out_ref, rows):
    rows[pl.ds(NODES * ELEM_DEV, PADDED * ELEM_DEV - NODES * ELEM_DEV), :] = jnp.zeros(
        ((PADDED - NODES) * ELEM_DEV, LANES), F32
    )
    for i in range(NODE):
        for e in range(ELEM_DEV):
            rows[pl.ds(i * NODE * ELEM_DEV + e, NODE, stride=ELEM_DEV), :] = x_ref[
                i, :, e * LANES : (e + 1) * LANES
            ]
    for group in range(GROUPS):
        turned = rows[group * LANES : (group + 1) * LANES, :].T
        both = turned.reshape(2, 8, 8, LANES)
        even, odd = mix(both[0], both[1])
        out_ref[group] = jnp.stack([even, odd], axis=1).reshape(N_MER, 8, LANES)


def native_to_tiles(x):
    return pl.pallas_call(
        native_to_tiles_kernel,
        out_shape=jax.ShapeDtypeStruct((GROUPS, N_MER, 8, LANES), F32),
        scratch_shapes=[pltpu.VMEM((PADDED * ELEM_DEV, LANES), F32)],
        compiler_params=pltpu.CompilerParams(vmem_limit_bytes=32 << 20),
        name="native_to_tiles",
    )(x)


def tiles_to_native_kernel(t_ref, out_ref, rows):
    for group in range(GROUPS):
        tiles = t_ref[group].reshape(8, 2, 8, LANES)
        real, imag = mix(tiles[:, 0], tiles[:, 1])
        both = jnp.concatenate([real.reshape(64, LANES), imag.reshape(64, LANES)], axis=0)
        rows[group * LANES : (group + 1) * LANES, :] = both.T
    for i in range(NODE):
        for e in range(ELEM_DEV):
            out_ref[i, :, e * LANES : (e + 1) * LANES] = rows[
                pl.ds(i * NODE * ELEM_DEV + e, NODE, stride=ELEM_DEV), :
            ]


def tiles_to_native(tiles):
    return pl.pallas_call(
        tiles_to_native_kernel,
        out_shape=jax.ShapeDtypeStruct((NODE, NODE, ELEM_DEV * LANES), F32),
        scratch_shapes=[pltpu.VMEM((PADDED * ELEM_DEV, LANES), F32)],
        compiler_params=pltpu.CompilerParams(vmem_limit_bytes=32 << 20),
        name="tiles_to_native",
    )(tiles)


def solve_kernel(weigh_in, weigh_out, b_ref, mass_ref, inv_ref, k_ref, out_ref, x, r, p, q, diag, kb):
    halves = (slice(0, LANES), slice(LANES, 2 * LANES))
    mode_group = lax.axis_index("mode")
    place = lax.axis_index("mer")
    sub = lax.broadcasted_iota(jnp.int32, (8, LANES), 0) % 4
    fraction = (mode_group * 64 + place * 4 + sub).astype(F32) / MODES
    azimuth = AZIMUTH_WEIGHT * fraction * fraction
    lane = lax.broadcasted_iota(jnp.int32, (8, LANES), 1)
    not_last = lane % RADIAL != RADIAL - 1
    not_row = lane < LANES - RADIAL

    for a in range(NODE):
        for b in range(NODE):
            kb[a * NODE + b] = jnp.full((8, LANES), k_ref[a, b], F32)

    def load(group, norm):
        for h in range(2):
            tiles = exchange([b_ref[group, 8 * h + at] for at in range(8)])
            for at in range(8):
                node = jnp.minimum(group * 8 + at, NODES - 1)
                mass = mass_ref[node, :, halves[h]]
                inv = inv_ref[node, :, halves[h]]
                diag[group * 8 + at, :, halves[h]] = mass * (1.0 + azimuth * inv)
                value = tiles[at]
                if weigh_in:
                    value = mass * value
                value = jnp.where(group * 8 + at < NODES, value, 0.0)
                r[group * 8 + at, :, halves[h]] = value
                norm = norm + value * value
        return norm

    def total(acc):
        summed = jnp.broadcast_to(jnp.sum(acc, axis=1, keepdims=True), (8, LANES))
        return summed + pltpu.roll(summed, 4, 0)

    zero = jnp.zeros((8, LANES), F32)
    norm = total(lax.fori_loop(0, GROUPS, load, zero))

    alpha = None
    beta = None
    for sweep in range(ITERS):

        def columns(j, _, sweep=sweep, alpha=alpha, beta=beta):
            for h in range(2):
                column = []
                for i in range(NODE):
                    at = i * NODE + j
                    value = r[at, :, halves[h]]
                    if sweep > 0:
                        old = p[at, :, halves[h]]
                        if sweep > 1:
                            x[at, :, halves[h]] = x[at, :, halves[h]] + alpha * old
                        else:
                            x[at, :, halves[h]] = alpha * old
                        value = value + beta * old
                    p[at, :, halves[h]] = value
                    column.append(value)
                jump = jnp.where(
                    not_last, column[8] - pltpu.roll(column[0], LANES - 1, 1), 0.0
                )
                back = pltpu.roll(jump, 1, 1)
                for a in range(NODE):
                    at = a * NODE + j
                    acc = diag[at, :, halves[h]] * column[a]
                    for b in range(NODE):
                        acc = acc + kb[a * NODE + b] * column[b]
                    if a == 0:
                        acc = acc - back
                    if a == NODE - 1:
                        acc = acc + jump
                    q[at, :, halves[h]] = acc
            return 0

        def rows(i, curve):
            row = [[p[i * NODE + b, :, halves[h]] for b in range(NODE)] for h in range(2)]
            ahead = [pltpu.roll(row[h][0], LANES - RADIAL, 1) for h in range(2)]
            jumps = [
                row[0][8] - jnp.where(not_row, ahead[0], ahead[1]),
                jnp.where(not_row, row[1][8] - ahead[1], 0.0),
            ]
            behind = [pltpu.roll(jump, RADIAL, 1) for jump in jumps]
            wrap = lane < RADIAL
            backs = [
                jnp.where(wrap, 0.0, behind[0]),
                jnp.where(wrap, behind[0], behind[1]),
            ]
            for h in range(2):
                for a in range(NODE):
                    at = i * NODE + a
                    acc = q[at, :, halves[h]]
                    for b in range(NODE):
                        acc = acc + kb[a * NODE + b] * row[h][b]
                    if a == 0:
                        acc = acc - backs[h]
                    if a == NODE - 1:
                        acc = acc + jumps[h]
                    q[at, :, halves[h]] = acc
                    curve = curve + row[h][a] * acc
            return curve

        lax.fori_loop(0, NODE, columns, 0)
        alpha = norm / total(lax.fori_loop(0, NODE, rows, zero))
        if sweep == ITERS - 1:
            break

        def step(i, acc, alpha=alpha):
            for b in range(NODE):
                at = i * NODE + b
                for h in range(2):
                    value = r[at, :, halves[h]] - alpha * q[at, :, halves[h]]
                    r[at, :, halves[h]] = value
                    acc = acc + value * value
            return acc

        after = total(lax.fori_loop(0, NODE, step, zero))
        beta = after / norm
        norm = after

    def store(group, _):
        for h in range(2):
            tiles = []
            for at in range(8):
                node = jnp.minimum(group * 8 + at, NODES - 1)
                value = x[node, :, halves[h]] + alpha * p[node, :, halves[h]]
                if weigh_out:
                    value = value * mass_ref[node, :, halves[h]]
                tiles.append(value)
            tiles = exchange(tiles)
            for at in range(8):
                out_ref[group, 8 * h + at] = tiles[at]
        return 0

    lax.fori_loop(0, GROUPS, store, 0)


def solve(tiles, mass, inv, stiffness, weigh_in, weigh_out):
    field = pltpu.VMEM((PADDED, 8, 2 * LANES), F32)
    vmem = pl.BlockSpec(memory_space=pltpu.VMEM)
    return pl.pallas_call(
        functools.partial(solve_kernel, weigh_in, weigh_out),
        out_shape=jax.ShapeDtypeStruct((GROUPS, N_MER, 8, LANES), F32),
        in_specs=[vmem, vmem, vmem, pl.BlockSpec(memory_space=pltpu.SMEM)],
        out_specs=vmem,
        scratch_shapes=[field] * 5 + [pltpu.VMEM((NODES, 8, LANES), F32)],
        compiler_params=pltpu.CompilerParams(vmem_limit_bytes=32 << 20),
        name="solve",
    )(tiles, mass, inv, stiffness)


def split(value):
    high = value.astype(BF16)
    return high, (value - high.astype(F32)).astype(BF16)


def apply(t_ref, which, rows, field):
    high, low = field
    table_high = t_ref[2 * which, rows, :]
    table_low = t_ref[2 * which + 1, rows, :]
    return (
        jnp.dot(table_high, high, preferred_element_type=F32)
        + jnp.dot(table_high, low, preferred_element_type=F32)
        + jnp.dot(table_low, high, preferred_element_type=F32)
    )


def parts_of(u_ref):
    real, imag = [], []
    for slot in range(2):
        tiles = u_ref[:, slot].reshape(MODES // 8, 2, 8, LANES)
        one, two = mix(tiles[:, 0], tiles[:, 1])
        real.append(one.reshape(MODES, LANES))
        imag.append(two.reshape(MODES, LANES))
    return jnp.concatenate(real, axis=1), jnp.concatenate(imag, axis=1)


def parts_to(out_ref, real, imag):
    for slot in range(2):
        lanes = slice(slot * LANES, (slot + 1) * LANES)
        one, two = mix(
            real[:, lanes].reshape(MODES // 8, 8, LANES), imag[:, lanes].reshape(MODES // 8, 8, LANES)
        )
        out_ref[:, slot] = jnp.stack([one, two], axis=1).reshape(MODES // 4, 8, LANES)


def mode_rows(width):
    mode = lax.broadcasted_iota(jnp.int32, (MODES, width), 0)
    fraction = mode.astype(F32) / MODES
    weight = jnp.where(mode == 0, 1.0 / PLANES, 2.0 / PLANES).astype(F32)
    sign = jnp.where(mode % 2 == 0, 1.0, -1.0).astype(F32)
    return fraction, weight, sign


WIDTH = 2 * LANES
ROWS = 128


def to_planes(t_ref, cos_field, sin_field, outs):
    for at in range(MODES // ROWS):
        rows = slice(at * ROWS, (at + 1) * ROWS)
        outs(rows, apply(t_ref, 0, rows, cos_field), apply(t_ref, 1, rows, sin_field))


def first_kernel(u_ref, t_ref, out_ref, planes_ref, plus, minus):
    real, imag = parts_of(u_ref)
    fraction, weight, sign = mode_rows(WIDTH)
    cos_field = split(jnp.concatenate([real, fraction * imag], axis=1))
    sin_field = split(jnp.concatenate([imag, fraction * real], axis=1))
    middle = jnp.sum(sign * real, axis=0, keepdims=True)
    middle_turned = -jnp.sum(sign * fraction * imag, axis=0, keepdims=True)

    def store(rows, cos, sin):
        planes_ref[0, rows, :] = cos[:, :WIDTH] - sin[:, :WIDTH]
        planes_ref[1, rows, :] = cos[:, :WIDTH] + sin[:, :WIDTH]
        planes_ref[2, rows, :] = -cos[:, WIDTH:] - sin[:, WIDTH:]
        planes_ref[3, rows, :] = sin[:, WIDTH:] - cos[:, WIDTH:]

    to_planes(t_ref, cos_field, sin_field, store)
    planes_ref[1, 0:1, :] = middle
    planes_ref[3, 0:1, :] = middle_turned
    low = planes_ref[0] * planes_ref[2]
    high = planes_ref[1] * planes_ref[3]
    first = lax.broadcasted_iota(jnp.int32, (MODES, WIDTH), 0) == 0
    plus[...] = jnp.where(first, low, low + high)
    minus[...] = low - high
    cos_side, sin_side = split(plus[...]), split(minus[...])
    every = slice(0, MODES)
    a = apply(t_ref, 0, every, cos_side) + sign * high[0:1]
    b = -apply(t_ref, 1, every, sin_side)
    parts_to(out_ref, real - weight * a, imag - weight * b)


def finish(t_ref, s_real, s_imag, planes, adjoint, fraction, sign, out_ref):
    first = lax.broadcasted_iota(jnp.int32, (MODES, WIDTH), 0) == 0
    pluses, minuses, middles = [], [], []
    for low, high in ((planes[2], planes[3]), (planes[0], planes[1])):
        low = low * adjoint[0]
        high = high * adjoint[1]
        pluses.append(jnp.where(first, low, low + high))
        minuses.append(low - high)
        middles.append(high[0:1])
    every = slice(0, MODES)
    cos = apply(t_ref, 0, every, split(jnp.concatenate(pluses, axis=1)))
    sin = apply(t_ref, 1, every, split(jnp.concatenate(minuses, axis=1)))
    a1 = cos[:, :WIDTH] + sign * middles[0]
    a2 = cos[:, WIDTH:] + sign * middles[1]
    b1 = -sin[:, :WIDTH]
    b2 = -sin[:, WIDTH:]
    parts_to(out_ref, s_real - a1 - fraction * b2, s_imag - b1 + fraction * a2)


def second_kernel(u_ref, s_ref, t_ref, out_ref, planes):
    real, imag = parts_of(u_ref)
    s_real, s_imag = parts_of(s_ref)
    fraction, weight, sign = mode_rows(WIDTH)
    cos_field = split(jnp.concatenate([real, fraction * imag, weight * s_real], axis=1))
    sin_field = split(jnp.concatenate([imag, fraction * real, weight * s_imag], axis=1))

    def store(rows, cos, sin):
        planes[0, rows, :] = cos[:, :WIDTH] - sin[:, :WIDTH]
        planes[1, rows, :] = cos[:, :WIDTH] + sin[:, :WIDTH]
        planes[2, rows, :] = -cos[:, WIDTH : 2 * WIDTH] - sin[:, WIDTH : 2 * WIDTH]
        planes[3, rows, :] = sin[:, WIDTH : 2 * WIDTH] - cos[:, WIDTH : 2 * WIDTH]
        planes[4, rows, :] = cos[:, 2 * WIDTH :] - sin[:, 2 * WIDTH :]
        planes[5, rows, :] = cos[:, 2 * WIDTH :] + sin[:, 2 * WIDTH :]

    to_planes(t_ref, cos_field, sin_field, store)
    planes[1, 0:1, :] = jnp.sum(sign * real, axis=0, keepdims=True)
    planes[3, 0:1, :] = -jnp.sum(sign * fraction * imag, axis=0, keepdims=True)
    planes[5, 0:1, :] = jnp.sum(sign * weight * s_real, axis=0, keepdims=True)
    finish(
        t_ref,
        s_real,
        s_imag,
        [planes[at] for at in range(4)],
        (planes[4], planes[5]),
        fraction,
        sign,
        out_ref,
    )


def third_kernel(s_ref, u_planes, t_ref, out_ref, planes):
    s_real, s_imag = parts_of(s_ref)
    fraction, weight, sign = mode_rows(WIDTH)

    def store(rows, cos, sin):
        planes[0, rows, :] = cos - sin
        planes[1, rows, :] = cos + sin

    to_planes(t_ref, split(weight * s_real), split(weight * s_imag), store)
    planes[1, 0:1, :] = jnp.sum(sign * weight * s_real, axis=0, keepdims=True)
    finish(
        t_ref,
        s_real,
        s_imag,
        [u_planes[at] for at in range(4)],
        (planes[0], planes[1]),
        fraction,
        sign,
        out_ref,
    )


TILES_SHAPE = jax.ShapeDtypeStruct((MODES // 4, 2, 8, LANES), F32)
PLANES_SHAPE = jax.ShapeDtypeStruct((4, MODES, WIDTH), F32)
PARAMS = pltpu.CompilerParams(vmem_limit_bytes=50 << 20)


def first_stage(u, table):
    field = pltpu.VMEM((MODES, WIDTH), F32)
    return pl.pallas_call(
        first_kernel,
        out_shape=(TILES_SHAPE, PLANES_SHAPE),
        scratch_shapes=[field, field],
        compiler_params=PARAMS,
        name="first_stage",
    )(u, table)


def second_stage(u, s, table):
    return pl.pallas_call(
        second_kernel,
        out_shape=TILES_SHAPE,
        scratch_shapes=[pltpu.VMEM((6, MODES, WIDTH), F32)],
        compiler_params=PARAMS,
        name="second_stage",
    )(u, s, table)


def third_stage(s, u_planes, table):
    return pl.pallas_call(
        third_kernel,
        out_shape=TILES_SHAPE,
        scratch_shapes=[pltpu.VMEM((2, MODES, WIDTH), F32)],
        compiler_params=PARAMS,
        name="third_stage",
    )(s, u_planes, table)


def by_slot(tiles, axis):
    pad = [(0, 0)] * tiles.ndim
    pad[axis] = (0, 16 - GROUPS)
    tiles = jnp.pad(tiles, pad)
    return tiles.reshape(tiles.shape[:axis] + (2, 8) + tiles.shape[axis + 1 :])


def native_to_planes(tiles):
    sent = by_slot(tiles, 0).transpose(1, 0, 2, 3, 4)
    got = lax.all_to_all(sent, "mode", 0, 0)
    return got.transpose(0, 2, 1, 3, 4).reshape(MODES // 4, 2, 8, LANES)


def planes_to_native(tiles):
    sent = tiles.reshape(N_MODE, N_MER, 2, 8, LANES).transpose(0, 2, 1, 3, 4)
    got = lax.all_to_all(sent, "mode", 0, 0)
    return got.transpose(1, 0, 2, 3, 4).reshape(16, N_MER, 8, LANES)[:GROUPS]


def native_to_modes(tiles):
    return lax.all_to_all(tiles.transpose(1, 0, 2, 3), "mer", 0, 0).transpose(1, 0, 2, 3)


def modes_to_planes(tiles):
    sent = by_slot(tiles, 0).transpose(1, 2, 0, 3, 4).reshape(N_MODE * N_MER, 2, 8, LANES)
    return lax.all_to_all(sent, ("mode", "mer"), 0, 0)


def planes_to_modes(tiles):
    got = lax.all_to_all(tiles, ("mode", "mer"), 0, 0)
    got = got.reshape(N_MODE, N_MER, 2, 8, LANES).transpose(2, 0, 1, 3, 4)
    return got.reshape(16, N_MER, 8, LANES)[:GROUPS]


def shards(cotangent, checkpoint, mass, inv_radius_sq, derivative):
    table = jnp.asarray(tables())
    stiffness = jnp.dot(derivative.T, derivative, precision=HIGHEST, preferred_element_type=F32)
    mass = lax.all_gather(mass, "mer", axis=2, tiled=True).reshape(NODES, 1, ELEMENTS)
    inv = lax.all_gather(inv_radius_sq, "mer", axis=2, tiled=True).reshape(NODES, 1, ELEMENTS)
    state = native_to_planes(native_to_tiles(checkpoint))
    rhs, planes = first_stage(state, table)
    rhs = planes_to_modes(rhs)
    weighted = solve(native_to_modes(native_to_tiles(cotangent)), mass, inv, stiffness, False, True)
    weighted = modes_to_planes(weighted)
    later = solve(rhs, mass, inv, stiffness, True, False)
    adjoint = second_stage(modes_to_planes(later), weighted, table)
    weighted = solve(planes_to_modes(adjoint), mass, inv, stiffness, False, True)
    return tiles_to_native(planes_to_native(third_stage(modes_to_planes(weighted), planes, table)))


def solution(mesh):
    return jax.shard_map(
        shards,
        mesh=mesh,
        in_specs=(
            P(None, None, ("mer", "mode")),
            P(None, None, ("mer", "mode")),
            P(None, None, "mer"),
            P(None, None, "mer"),
            P(),
        ),
        out_specs=P(None, None, ("mer", "mode")),
        check_vma=False,
    )
```

time: 1530 us -> 286 us (0.19); the launches traced: 1510 us -> 285 us
  blocking collectives: 609 us -> 144 us
  local copies, waits for them, and re-layouts: 457 us -> 8.41 us
  other arithmetic: 222 us -> 0 us
  matrix products: 143 us -> 0.2 us
  Pallas kernels: 0 us -> 74.2 us
  starting transfers between devices: 70.7 us -> 38.1 us
  waiting for transfers between devices: 3.44 us -> 20.5 us
    psum x14 -> x0, blocking collectives: 429 us -> none  [the longest x8 244 us: squared_norm(): return lax.psum(per_mode_dot(residual, residual), 'mer')]
    dot_general x32 -> x0, matrix products: 143 us -> none  [the longest x12 51.2 us: operate(): jnp.einsum('ab,bjl->ajl', stiffness, field, precision=HIGHEST)]
    reshape x50 -> x11, local copies, waits for them, and re-layouts: 114 us -> 5.25 us  [the longest x4 2.31 us: by_slot(): return tiles.reshape(tiles.shape[:axis] + (2, 8) + tiles.shape[axis + 1:])]
    unnamed x108 -> x16, local copies, waits for them, and re-layouts: 108 us -> 1.62 us
    all_to_all x4, blocking collectives: 180 us -> 93.2 us  [the longest x2 51.4 us: modes_to_planes(): return lax.all_to_all(sent, ('mode', 'mer'), 0, 0)]
    pallas_call x0 -> x9, Pallas kernels: none -> 74.2 us  [the longest x3 54.4 us: solve(): pl.pallas_call(functools.partial(solve_kernel, weigh_in, weigh_out), out_...]
    mul x41 -> x0, other arithmetic: 64.1 us -> none  [the longest x12 24.6 us: per_mode_dot(): first * second]
    ppermute x24 -> x0, starting transfers between devices: 60.5 us -> none  [the longest x12 44.3 us: padded_2(): lax.ppermute(tail, axis, [(i, (i + 1) % count) for i in range(ends)])]
  transfers between devices with their start and end apart: 26 -> 4, of which waited for: 3 -> 2; matrix products, arithmetic and copies ran while one was open for 11% -> 2% of each run, Pallas kernels for 0% -> 15%
where the time goes in v1:
time: 286 us; the launch traced here: 285 us
  blocking collectives  144 us (50%)
  Pallas kernels  74.2 us (26%)
  starting transfers between devices  38.1 us (13%)
  waiting for transfers between devices  20.5 us (7%)
  local copies, waits for them, and re-layouts  8.41 us (3%)
    pallas_call x3, Pallas kernels, solve(): pl.pallas_call(functools.partial(solve_kernel, weigh_in, weigh_out), out_...  54.4 us
    all_to_all x2, blocking collectives, modes_to_planes(): return lax.all_to_all(sent, ('mode', 'mer'), 0, 0)  51.4 us
    all_gather x1, blocking collectives, shards(): lax.all_gather(inv_radius_sq, 'mer', axis=2, tiled=True)  30.9 us
    all_to_all x1, blocking collectives, planes_to_modes(): got = lax.all_to_all(tiles, ('mode', 'mer'), 0, 0)  23 us
    all_gather x1, blocking collectives, shards(): lax.all_gather(mass, 'mer', axis=2, tiled=True).reshape(NODES, 1, ELEMENTS)  19.5 us
    all_to_all x1, blocking collectives, planes_to_native(): got = lax.all_to_all(sent, 'mode', 0, 0)  18.8 us
    all_to_all x1, starting transfers between devices, modes_to_planes(): return lax.all_to_all(sent, ('mode', 'mer'), 0, 0)  17.7 us
    all_to_all x1, waiting for transfers between devices, native_to_planes(): got = lax.all_to_all(sent, 'mode', 0, 0)  13.8 us
  transfers between devices with their start and end apart: 4, of which 2 were waited for; matrix products, arithmetic and copies ran while one was open for 2% of the time, Pallas kernels for 15%

profile of v1, /device:TPU:1, one launch (start us, length us, event | category | flops | bytes accessed | tf_op | source)
XLA Modules:
  0.0 285.3 jit_solution(13800886853133589553)
XLA Ops:
  0.0 1.3 copy-done.1
  1.8 1.1 copy.34
  2.9 5.8 %all-to-all-start = ((f32[8,2,16,8,128]{4,3,1,2,0:T(8,128)}), f32[8,2,16,8,128]{4,3,1,2,0:T(8,128)S(1)}, u32[]{:S(2)}, u32[]{:S(2)}) async-start(f32[8,2,16,8,128]{4,3,1,2,0:T(8,128)} %bitcast.41), calls=%async_computation | async-start | bytes 2097152 | tf_op jit(solution)/shard_map/all_to_all | solution.py:465
  9.1 0.9 copy.21
  10.0 13.8 %all-to-all-done = f32[8,2,16,8,128]{4,3,1,2,0:T(8,128)S(1)} async-done(((f32[8,2,16,8,128]{4,3,1,2,0:T(8,128)}), f32[8,2,16,8,128]{4,3,1,2,0:T(8,128)S(1)}, u32[]{:S(2)}, u32[]{:S(2)}) %all-to-all-start) | async-done | bytes 1048608 | tf_op jit(solution)/shard_map/all_to_all | solution.py:465
  23.8 7.8 %all-to-all-start.3 = ((f32[16,11,8,128]{3,2,1,0:T(8,128)}), f32[16,11,8,128]{3,2,1,0:T(8,128)S(1)}, u32[]{:S(2)}, u32[]{:S(2)}) async-start(f32[16,11,8,128]{3,2,1,0:T(8,128)} %copy.21), calls=%async_computation.3 | async-start | bytes 1441792 | tf_op jit(solution)/shard_map/all_to_all | solution.py:476
  31.6 5.5 %first_stage.1 = (f32[128,2,8,128]{3,2,1,0:T(8,128)}, f32[4,512,256]{2,1,0:T(8,128)}) custom-call(f32[128,2,8,128]{3,2,1,0:T(8,128)S(1)} %bitcast.43, bf16[4,512,512]{2,1,0:T(8,128)(2,1)} %constant.5.clone.t_ref), custom_call_target="tpu_custom_call" | custom-call | tf_op jit(solution)/shard_map/first_stage/pallas_call | solution.py:427
  37.1 6.7 %all-to-all-done.3 = f32[16,11,8,128]{3,2,1,0:T(8,128)S(1)} async-done(((f32[16,11,8,128]{3,2,1,0:T(8,128)}), f32[16,11,8,128]{3,2,1,0:T(8,128)S(1)}, u32[]{:S(2)}, u32[]{:S(2)}) %all-to-all-start.3) | async-done | bytes 720928 | tf_op jit(solution)/shard_map/all_to_all | solution.py:476
  43.8 6.8 %all-to-all-start.1 = ((f32[128,2,8,128]{3,2,1,0:T(8,128)}), f32[128,2,8,128]{3,2,1,0:T(8,128)}, u32[]{:S(2)}, u32[]{:S(2)}) async-start(f32[128,2,8,128]{3,2,1,0:T(8,128)} %get-tuple-element.7), calls=%async_computation.1 | async-start | bytes 2097152 | tf_op jit(solution)/shard_map/all_to_all | solution.py:485
  51.0 30.9 %all_gather.7 = f32[9,9,256]{1,0,2:T(8,128)S(1)} all-gather(f32[9,9,16]{1,0,2:T(8,128)S(1)} %copy.18), channel_id=1, replica_groups=mesh['mode'=8,'mer'=16] {'mer'}, dimensions={2}, use_global_device_ids=true | all-gather | bytes 88128 | tf_op jit(solution)/shard_map/all_gather | solution.py:494
  82.6 19.5 %all_gather.6 = f32[9,9,256]{1,0,2:T(8,128)S(1)} all-gather(f32[9,9,16]{1,0,2:T(8,128)S(1)} %copy.16), channel_id=1, replica_groups=mesh['mode'=8,'mer'=16] {'mer'}, dimensions={2}, use_global_device_ids=true | all-gather | bytes 88128 | tf_op jit(solution)/shard_map/all_gather | solution.py:493
  103.1 18.1 %solve.4 = f32[11,16,8,128]{3,2,1,0:T(8,128)S(1)} custom-call(f32[11,16,8,128]{3,2,1,0:T(8,128)S(1)} %bitcast.45, f32[81,1,256]{2,1,0:T(1,128)S(1)} %copy.28.mass_ref, f32[81,1,256]{2,1,0:T(1,128)S(1)} %copy.29.inv_ref, f32[9,9]{1,0:T(8,128)S(1)} %fusion.k_ref), custom_call_target="tpu_custom_call" | custom-call | tf_op jit(solution)/shard_map/solve/pallas_call | solution.py:255
  121.3 1.1 copy.23
  122.4 17.7 %all-to-all-start.4 = ((f32[128,2,8,128]{3,2,1,0:T(8,128)}), f32[128,2,8,128]{3,2,1,0:T(8,128)S(1)}, u32[]{:S(2)}, u32[]{:S(2)}) async-start(f32[128,2,8,128]{3,2,1,0:T(8,128)} %bitcast.14), calls=%async_computation.4 | async-start | bytes 2097152 | tf_op jit(solution)/shard_map/all_to_all | solution.py:481
  140.2 1.3 copy.15
  141.6 18.1 %solve.3 = f32[11,16,8,128]{3,2,1,0:T(8,128)S(1)} custom-call(f32[11,16,8,128]{3,2,1,0:T(8,128)S(1)} %slice.12.b_ref, f32[81,1,256]{2,1,0:T(1,128)S(1)} %copy.28.mass_ref, f32[81,1,256]{2,1,0:T(1,128)S(1)} %copy.29.inv_ref, f32[9,9]{1,0:T(8,128)S(1)} %fusion.k_ref), custom_call_target="tpu_custom_call" | custom-call | tf_op jit(solution)/shard_map/solve/pallas_call | solution.py:255
  159.9 28.4 %all_to_all.40.u_ref = f32[128,2,8,128]{3,2,1,0:T(8,128)S(1)} all-to-all(f32[128,2,8,128]{3,2,1,0:T(8,128)S(1)} %bitcast.47), channel_id=1, replica_groups=mesh['mode'=8,'mer'=16] {'mode','mer'}, dimensions={0} | all-to-all | bytes 2097152 | tf_op jit(solution)/shard_map/all_to_all | solution.py:481
  188.3 6.8 %second_stage.1 = f32[128,2,8,128]{3,2,1,0:T(8,128)S(1)} custom-call(f32[128,2,8,128]{3,2,1,0:T(8,128)S(1)} %all_to_all.40.u_ref, f32[128,2,8,128]{3,2,1,0:T(8,128)S(1)} %all-to-all-done.4.s_ref, bf16[4,512,512]{2,1,0:T(8,128)(2,1)} %constant.5.clone.t_ref), custom_call_target="tpu_custom_call" | custom-call | tf_op jit(solution)/shard_map/second_stage/pallas_call | solution.py:437
  195.1 23.0 %all_to_all.41 = f32[128,2,8,128]{3,2,1,0:T(8,128)S(1)} all-to-all(f32[128,2,8,128]{3,2,1,0:T(8,128)S(1)} %second_stage.1), channel_id=1, replica_groups=mesh['mode'=8,'mer'=16] {'mode','mer'}, dimensions={0} | all-to-all | bytes 2097152 | tf_op jit(solution)/shard_map/all_to_all | solution.py:485
  218.3 18.1 %solve.5 = f32[11,16,8,128]{3,2,1,0:T(8,128)S(1)} custom-call(f32[11,16,8,128]{3,2,1,0:T(8,128)S(1)} %slice.13.b_ref, f32[81,1,256]{2,1,0:T(1,128)S(1)} %copy.28.mass_ref, f32[81,1,256]{2,1,0:T(1,128)S(1)} %copy.29.inv_ref, f32[9,9]{1,0:T(8,128)S(1)} %fusion.k_ref), custom_call_target="tpu_custom_call" | custom-call | tf_op jit(solution)/shard_map/solve/pallas_call | solution.py:255
  236.6 23.0 %all_to_all.42.s_ref = f32[128,2,8,128]{3,2,1,0:T(8,128)S(1)} all-to-all(f32[128,2,8,128]{3,2,1,0:T(8,128)S(1)} %bitcast.53), channel_id=1, replica_groups=mesh['mode'=8,'mer'=16] {'mode','mer'}, dimensions={0} | all-to-all | bytes 2097152 | tf_op jit(solution)/shard_map/all_to_all | solution.py:481
  259.6 5.3 %third_stage.1 = f32[128,2,8,128]{3,2,1,0:T(8,128)S(1)} custom-call(f32[128,2,8,128]{3,2,1,0:T(8,128)S(1)} %all_to_all.42.s_ref, f32[4,512,256]{2,1,0:T(8,128)} %get-tuple-element.8.u_planes, bf16[4,512,512]{2,1,0:T(8,128)(2,1)} %constant.5.clone.t_ref), custom_call_target="tpu_custom_call" | custom-call | tf_op jit(solution)/shard_map/third_stage/pallas_call | solution.py:447
  265.0 18.8 %all_to_all.43 = f32[8,2,16,8,128]{4,3,2,1,0:T(8,128)S(1)} all-to-all(f32[8,2,16,8,128]{4,3,2,1,0:T(8,128)S(1)} %bitcast.54), channel_id=1, replica_groups=mesh['mode'=8,'mer'=16] {'mode'}, dimensions={0} | all-to-all | bytes 2097152 | tf_op jit(solution)/shard_map/all_to_all | solution.py:471
  283.9 1.4 tiles_to_native.1
  (37 shorter events, 3.8 us)
Async XLA Ops:
  0.0 102.8 %copy-start = (f32[9,9]{1,0:T(8,128)S(1)}, f32[9,9]{1,0:T(8,128)}, u32[]{:S(2)}) copy-start(f32[9,9]{1,0:T(8,128)} %param.10) | copy-start | bytes 976
  0.0 1.3 copy-start.1
  1.8 6.9 %copy-start.2 = (f32[9,9,2048]{2,1,0:T(8,128)S(1)}, f32[9,9,2048]{2,1,0:T(8,128)}, u32[]{:S(2)}) copy-start(f32[9,9,2048]{2,1,0:T(8,128)} %x_ref.3) | copy-start | bytes 1990660
  2.9 20.9 %all-to-all-start = ((f32[8,2,16,8,128]{4,3,1,2,0:T(8,128)}), f32[8,2,16,8,128]{4,3,1,2,0:T(8,128)S(1)}, u32[]{:S(2)}, u32[]{:S(2)}) async-start(f32[8,2,16,8,128]{4,3,1,2,0:T(8,128)} %bitcast.41), calls=%async_computation | async-start | bytes 2097152 | tf_op jit(solution)/shard_map/all_to_all | solution.py:465
  23.8 20.0 %all-to-all-start.3 = ((f32[16,11,8,128]{3,2,1,0:T(8,128)}), f32[16,11,8,128]{3,2,1,0:T(8,128)S(1)}, u32[]{:S(2)}, u32[]{:S(2)}) async-start(f32[16,11,8,128]{3,2,1,0:T(8,128)} %copy.21), calls=%async_computation.3 | async-start | bytes 1441792 | tf_op jit(solution)/shard_map/all_to_all | solution.py:476
  31.5 19.1 %copy-start.5 = (f32[9,9,16]{2,1,0:T(8,128)S(1)}, f32[9,9,16]{2,1,0:T(8,128)}, u32[]{:S(2)}) copy-start(f32[9,9,16]{2,1,0:T(8,128)} %param.8) | copy-start | bytes 15556
  31.6 19.3 %copy-start.6 = (f32[9,9,16]{2,1,0:T(8,128)S(1)}, f32[9,9,16]{2,1,0:T(8,128)}, u32[]{:S(2)}) copy-start(f32[9,9,16]{2,1,0:T(8,128)} %param.9) | copy-start | bytes 15556
  43.8 7.0 %copy-start.3 = (f32[16,11,8,128]{3,2,1,0:T(8,128)}, f32[16,11,8,128]{3,2,1,0:T(8,128)S(1)}, u32[]{:S(2)}) copy-start(f32[16,11,8,128]{3,2,1,0:T(8,128)S(1)} %all-to-all-done.3) | copy-start | bytes 2162692
  43.8 78.6 %all-to-all-start.1 = ((f32[128,2,8,128]{3,2,1,0:T(8,128)}), f32[128,2,8,128]{3,2,1,0:T(8,128)}, u32[]{:S(2)}, u32[]{:S(2)}) async-start(f32[128,2,8,128]{3,2,1,0:T(8,128)} %get-tuple-element.7), calls=%async_computation.1 | async-start | bytes 2097152 | tf_op jit(solution)/shard_map/all_to_all | solution.py:485
  82.6 20.4 %copy-start.4 = (f32[16,11,8,128]{3,2,1,0:T(8,128)S(1)}, f32[16,11,8,128]{3,2,1,0:T(8,128)}, u32[]{:S(2)}) copy-start(f32[16,11,8,128]{3,2,1,0:T(8,128)} %copy-done.3) | copy-start | bytes 2162692
  122.4 37.5 %all-to-all-start.4 = ((f32[128,2,8,128]{3,2,1,0:T(8,128)}), f32[128,2,8,128]{3,2,1,0:T(8,128)S(1)}, u32[]{:S(2)}, u32[]{:S(2)}) async-start(f32[128,2,8,128]{3,2,1,0:T(8,128)} %bitcast.14), calls=%async_computation.4 | async-start | bytes 2097152 | tf_op jit(solution)/shard_map/all_to_all | solution.py:481

commit v2 on v1

v2 whole, which is shorter than its diff:
```python
import functools
import math

import jax
import jax.numpy as jnp
import ml_dtypes
import numpy as np
from jax import lax
from jax.experimental import pallas as pl
from jax.experimental.pallas import tpu as pltpu
from jax.sharding import PartitionSpec as P

NODE = 9
NODES = NODE * NODE
RADIAL = 8
ITERS = 4
MODES = 512
PLANES = 1024
ELEMENTS = 256
N_MODE = 8
N_MER = 16
ELEM_DEV = 16
GROUPS = 11
PADDED = GROUPS * 8
LANES = 128
AZIMUTH_WEIGHT = 4.0
HIGHEST = lax.Precision.HIGHEST
F32 = jnp.float32
BF16 = jnp.bfloat16


def tables():
    index = np.outer(np.arange(MODES), np.arange(MODES)) % PLANES
    angles = index.astype(np.float64) * (2.0 * math.pi / PLANES)
    out = []
    for values in (np.cos(angles), np.sin(angles)):
        values = values.astype(np.float32)
        high = values.astype(ml_dtypes.bfloat16)
        low = (values - high.astype(np.float32)).astype(ml_dtypes.bfloat16)
        out += [high, low]
    return np.stack(out)


def mix(first, second):
    shape = first.shape
    low = lax.broadcasted_iota(jnp.int32, shape, len(shape) - 2) % 8 < 4
    axis = len(shape) - 2
    return (
        jnp.where(low, first, pltpu.roll(second, 4, axis)),
        jnp.where(low, pltpu.roll(first, 4, axis), second),
    )


def exchange(tiles):
    tiles = list(tiles)
    axis = tiles[0].ndim - 1
    block = lax.broadcasted_iota(jnp.int32, tiles[0].shape, axis) // 16
    for bit in (1, 2, 4):
        clear = (block & bit) == 0
        for at in range(8):
            if at & bit:
                continue
            one, two = tiles[at], tiles[at | bit]
            tiles[at] = jnp.where(clear, one, pltpu.roll(two, 16 * bit, axis))
            tiles[at | bit] = jnp.where(clear, pltpu.roll(one, LANES - 16 * bit, axis), two)
    return tiles


def native_to_tiles(x_ref, out_ref, rows):
    rows[pl.ds(NODES * ELEM_DEV, PADDED * ELEM_DEV - NODES * ELEM_DEV), :] = jnp.zeros(
        ((PADDED - NODES) * ELEM_DEV, LANES), F32
    )
    for i in range(NODE):
        for e in range(ELEM_DEV):
            rows[pl.ds(i * NODE * ELEM_DEV + e, NODE, stride=ELEM_DEV), :] = x_ref[
                i, :, e * LANES : (e + 1) * LANES
            ]
    for group in range(GROUPS):
        turned = rows[group * LANES : (group + 1) * LANES, :].T
        both = turned.reshape(2, 8, 8, LANES)
        even, odd = mix(both[0], both[1])
        out_ref[group // 8, group % 8] = jnp.stack([even, odd], axis=1).reshape(N_MER, 8, LANES)


def tiles_to_native_kernel(t_ref, out_ref, rows):
    for group in range(GROUPS):
        tiles = t_ref[group].reshape(8, 2, 8, LANES)
        real, imag = mix(tiles[:, 0], tiles[:, 1])
        both = jnp.concatenate([real.reshape(64, LANES), imag.reshape(64, LANES)], axis=0)
        rows[group * LANES : (group + 1) * LANES, :] = both.T
    for i in range(NODE):
        for e in range(ELEM_DEV):
            out_ref[i, :, e * LANES : (e + 1) * LANES] = rows[
                pl.ds(i * NODE * ELEM_DEV + e, NODE, stride=ELEM_DEV), :
            ]


def tiles_to_native(tiles):
    return pl.pallas_call(
        tiles_to_native_kernel,
        out_shape=jax.ShapeDtypeStruct((NODE, NODE, ELEM_DEV * LANES), F32),
        scratch_shapes=[pltpu.VMEM((PADDED * ELEM_DEV, LANES), F32)],
        compiler_params=pltpu.CompilerParams(vmem_limit_bytes=32 << 20),
        name="tiles_to_native",
    )(tiles)


def stiffness_tables(d_ref, k_ref):
    def dot(a, b):
        return jnp.dot(a, b, precision=HIGHEST, preferred_element_type=F32)

    derivative = d_ref[...]
    stiffness = lax.dot_general(
        derivative, derivative, (((0,), (0,)), ((), ())), precision=HIGHEST, preferred_element_type=F32
    )

    def pick(shape, node_axis, outer):
        node = lax.broadcasted_iota(jnp.int32, shape, node_axis)
        other = lax.broadcasted_iota(jnp.int32, shape, 1 - node_axis)
        place = node // NODE if outer else node % NODE
        return jnp.where((place == other) & (node < NODES), 1.0, 0.0).astype(F32)

    outer, inner = pick((PADDED, NODE), 0, True), pick((PADDED, NODE), 0, False)
    outer_t, inner_t = pick((NODE, PADDED), 1, True), pick((NODE, PADDED), 1, False)
    whole = dot(dot(outer, stiffness), outer_t) * dot(inner, inner_t)
    whole = whole + dot(dot(inner, stiffness), inner_t) * dot(outer, outer_t)
    high = whole.astype(BF16).astype(F32)
    low = whole - high
    top = jnp.concatenate([high, high], axis=1)
    bottom = jnp.concatenate([low, jnp.zeros_like(low)], axis=1)
    k_ref[...] = jnp.concatenate([top, bottom], axis=0).astype(BF16)


def metric_rows(mass_ref, inverse_ref, rows, out_ref):
    lane = lax.broadcasted_iota(jnp.int32, (ELEM_DEV, LANES), 1) % ELEM_DEV
    element = lax.broadcasted_iota(jnp.int32, (ELEM_DEV, LANES), 0)
    repeat = jnp.where(lane == element, 1.0, 0.0).astype(F32)
    shape = (PADDED, LANES)
    node = lax.broadcasted_iota(jnp.int32, shape, 0)
    block = lax.broadcasted_iota(jnp.int32, shape, 1) // ELEM_DEV
    keep = (node % 8 == block) & (node < NODES)
    for kind, ref in ((0, mass_ref), (1, inverse_ref)):
        for i in range(NODE):
            rows[i * NODE : (i + 1) * NODE, :ELEM_DEV] = ref[i]
        values = jnp.dot(
            rows[:PADDED, :ELEM_DEV], repeat, precision=HIGHEST, preferred_element_type=F32
        )
        values = jnp.where(keep, values, 0.0).reshape(GROUPS, 8, LANES)
        out_ref[kind, :GROUPS] = jnp.sum(values, axis=1)
        out_ref[kind, GROUPS:] = jnp.zeros((16 - GROUPS, LANES), F32)


def metric_tables(m_ref, mode_group, place, mass, diag, faces, turn):
    inverse = diag.at[0]
    for kind, out in ((0, mass), (1, inverse)):
        for h in range(2):
            rows = exchange([m_ref[8 * h + at, kind] for at in range(8)])
            for at in range(8):
                for group in range(GROUPS):
                    turn[h, group, at : at + 1] = rows[at][group : group + 1]
            for group in range(GROUPS):
                out[group * 8 : (group + 1) * 8, h * LANES : (h + 1) * LANES] = turn[h, group, 0:8]
    shape = (PADDED, ELEMENTS)
    node = lax.broadcasted_iota(jnp.int32, shape, 0)
    element = lax.broadcasted_iota(jnp.int32, shape, 1)
    inside = node < NODES
    upper = (node % NODE == NODE - 1) & (element < ELEMENTS - RADIAL) & inside
    lower = (node % NODE == 0) & (element >= RADIAL) & inside
    outer = (node // NODE == NODE - 1) & (element % RADIAL != RADIAL - 1) & inside
    inner = (node // NODE == 0) & (element % RADIAL != 0)
    marks = [jnp.where(mark, 1.0, 0.0).astype(F32) for mark in (upper, lower, outer, inner)]
    for at in range(4):
        faces[at] = marks[at]
    count = marks[0] + marks[1] + marks[2] + marks[3]
    values = inverse[...]
    for n in range(4):
        fraction = (mode_group * 64 + place * 4 + n).astype(F32) / MODES
        diag[n] = mass[...] * (1.0 + AZIMUTH_WEIGHT * fraction * fraction * values) + count


CHUNKS = ((0, 0, 3), (0, 3, 6), (0, 6, 8), (1, 0, 3))


def load_tiles(b_ref, turn, weight, out):
    for slot, start, stop in CHUNKS:
        for h in range(2):
            tiles = exchange([b_ref[slot, start:stop, 8 * h + at] for at in range(8)])
            for at in range(8):
                turn[h, 8 * slot + start : 8 * slot + stop, at * 8 : (at + 1) * 8] = tiles[at]
    for s in range(8):
        for h in range(2):
            lanes = slice(h * LANES, (h + 1) * LANES)
            for group in range(GROUPS):
                rows = slice(group * 8, (group + 1) * 8)
                value = turn[h, group, pl.ds(s, 8, stride=8), :]
                if weight is not None:
                    value = value * weight[rows, lanes]
                out[s, rows, lanes] = value


def store_tiles(value_of, turn, out_ref):
    for s in range(8):
        value = value_of(s)
        for h in range(2):
            for group in range(GROUPS):
                turn[h, group, pl.ds(s, 8, stride=8), :] = value[
                    group * 8 : (group + 1) * 8, h * LANES : (h + 1) * LANES
                ]
    for slot, start, stop in CHUNKS:
        for h in range(2):
            groups = slice(8 * slot + start, 8 * slot + stop)
            tiles = exchange([turn[h, groups, at * 8 : (at + 1) * 8] for at in range(8)])
            for at in range(8):
                out_ref[slot, start:stop, 8 * h + at] = tiles[at]


def total(parts):
    half = parts[:, :LANES] + parts[:, LANES:]
    return jnp.broadcast_to(jnp.sum(half, axis=(0, 1), keepdims=True), (1, ELEMENTS))


def fold(value):
    return jnp.sum(value.reshape(GROUPS, 8, ELEMENTS), axis=0)


def solve(b_ref, out_ref, weigh_in, weigh_out, scratch):
    mass, diag, faces, k_ref, x, r, p, q, turn = scratch
    load_tiles(b_ref, turn, mass if weigh_in else None, r)
    norms = []
    for n in range(4):
        norms.append(total(fold(r[n] * r[n]) + fold(r[n + 4] * r[n + 4])))
    x[...] = jnp.zeros_like(x)
    p[...] = jnp.zeros_like(p)
    empty = jnp.zeros((8, ELEMENTS), F32)
    edge = jnp.zeros((16, ELEMENTS), F32)

    def sweep_body(sweep, carry):
        norms, alphas, betas = carry
        curves = []
        for n in range(4):
            curve = None
            for s in (n, n + 4):
                old = p[s]
                x[s] = x[s] + alphas[n] * old
                now = r[s] + betas[n] * old
                p[s] = now
                high = now.astype(BF16).astype(F32)
                halves = jnp.concatenate([high, now - high], axis=0).astype(BF16)
                image = jnp.dot(k_ref[...], halves, preferred_element_type=F32)
                ahead = pltpu.roll(now[: PADDED - 8], ELEMENTS - RADIAL, 1)
                behind = pltpu.roll(now[8:], RADIAL, 1)
                image = (
                    image[:PADDED]
                    + image[PADDED:]
                    + diag[n] * now
                    - faces[0] * jnp.concatenate([empty, ahead], axis=0)
                    - faces[1] * jnp.concatenate([behind, empty], axis=0)
                )
                outward = pltpu.roll(now[:16], ELEMENTS - 1, 1)
                inward = pltpu.roll(now[72:], 1, 1)
                image = jnp.concatenate(
                    [
                        image[:16] - faces[3, :16] * inward,
                        image[16:72],
                        image[72:] - faces[2, 72:] * outward,
                    ],
                    axis=0,
                )
                q[s] = image
                part = fold(now * image)
                curve = part if curve is None else curve + part
            curves.append(total(curve))
        alphas = [norms[n] / curves[n] for n in range(4)]

        def update():
            after = []
            for n in range(4):
                part = None
                for s in (n, n + 4):
                    value = r[s] - alphas[n] * q[s]
                    r[s] = value
                    add = fold(value * value)
                    part = add if part is None else part + add
                after.append(total(part))
            return after

        after = lax.cond(sweep < ITERS - 1, update, lambda: norms)
        betas = [after[n] / norms[n] for n in range(4)]
        return after, alphas, betas

    none = [jnp.zeros((1, ELEMENTS), F32)] * 4
    norms, alphas, betas = lax.fori_loop(0, ITERS, sweep_body, (norms, none, none))

    def value_of(s):
        value = x[s] + alphas[s % 4] * p[s]
        return value * mass[...] if weigh_out else value

    store_tiles(value_of, turn, out_ref)


FIELD = pltpu.VMEM((8, PADDED, ELEMENTS), F32)
SOLVE_SCRATCH = [
    pltpu.VMEM((PADDED, ELEMENTS), F32),
    pltpu.VMEM((4, PADDED, ELEMENTS), F32),
    pltpu.VMEM((4, PADDED, ELEMENTS), F32),
    pltpu.VMEM((2 * PADDED, 2 * PADDED), BF16),
    FIELD,
    FIELD,
    FIELD,
    FIELD,
    pltpu.VMEM((2, GROUPS, 64, LANES), F32),
]


def split(value):
    high = value.astype(BF16)
    return high, (value - high.astype(F32)).astype(BF16)


def apply(t_ref, which, rows, field):
    high, low = field
    table_high = t_ref[2 * which, rows, :]
    table_low = t_ref[2 * which + 1, rows, :]
    return (
        jnp.dot(table_high, high, preferred_element_type=F32)
        + jnp.dot(table_high, low, preferred_element_type=F32)
        + jnp.dot(table_low, high, preferred_element_type=F32)
    )


def parts_of(u_ref):
    real, imag = [], []
    for slot in range(2):
        tiles = u_ref[slot].reshape(MODES // 8, 2, 8, LANES)
        one, two = mix(tiles[:, 0], tiles[:, 1])
        real.append(one.reshape(MODES, LANES))
        imag.append(two.reshape(MODES, LANES))
    return jnp.concatenate(real, axis=1), jnp.concatenate(imag, axis=1)


def parts_to(out_ref, real, imag):
    for slot in range(2):
        lanes = slice(slot * LANES, (slot + 1) * LANES)
        one, two = mix(
            real[:, lanes].reshape(MODES // 8, 8, LANES), imag[:, lanes].reshape(MODES // 8, 8, LANES)
        )
        out_ref[slot] = jnp.stack([one, two], axis=1).reshape(MODES // 4, 8, LANES)


def mode_rows(width):
    mode = lax.broadcasted_iota(jnp.int32, (MODES, width), 0)
    fraction = mode.astype(F32) / MODES
    weight = jnp.where(mode == 0, 1.0 / PLANES, 2.0 / PLANES).astype(F32)
    sign = jnp.where(mode % 2 == 0, 1.0, -1.0).astype(F32)
    return fraction, weight, sign


WIDTH = 2 * LANES
ROWS = 128


def to_planes(t_ref, cos_field, sin_field, outs):
    for at in range(MODES // ROWS):
        rows = slice(at * ROWS, (at + 1) * ROWS)
        outs(rows, apply(t_ref, 0, rows, cos_field), apply(t_ref, 1, rows, sin_field))


def first_stage(u_ref, t_ref, out_ref, planes_ref):
    real, imag = parts_of(u_ref)
    fraction, weight, sign = mode_rows(WIDTH)
    cos_field = split(jnp.concatenate([real, fraction * imag], axis=1))
    sin_field = split(jnp.concatenate([imag, fraction * real], axis=1))
    middle = jnp.sum(sign * real, axis=0, keepdims=True)
    middle_turned = -jnp.sum(sign * fraction * imag, axis=0, keepdims=True)

    def store(rows, cos, sin):
        planes_ref[0, rows, :] = cos[:, :WIDTH] - sin[:, :WIDTH]
        planes_ref[1, rows, :] = cos[:, :WIDTH] + sin[:, :WIDTH]
        planes_ref[2, rows, :] = -cos[:, WIDTH:] - sin[:, WIDTH:]
        planes_ref[3, rows, :] = sin[:, WIDTH:] - cos[:, WIDTH:]

    to_planes(t_ref, cos_field, sin_field, store)
    planes_ref[1, 0:1, :] = middle
    planes_ref[3, 0:1, :] = middle_turned
    low = planes_ref[0] * planes_ref[2]
    high = planes_ref[1] * planes_ref[3]
    first = lax.broadcasted_iota(jnp.int32, (MODES, WIDTH), 0) == 0
    cos_side, sin_side = split(jnp.where(first, low, low + high)), split(low - high)
    every = slice(0, MODES)
    a = apply(t_ref, 0, every, cos_side) + sign * high[0:1]
    b = -apply(t_ref, 1, every, sin_side)
    parts_to(out_ref, real - weight * a, imag - weight * b)


def finish(t_ref, s_ref, planes, adjoint, at, out_ref):
    s_real, s_imag = parts_of(s_ref)
    fraction, _, sign = mode_rows(WIDTH)
    first = lax.broadcasted_iota(jnp.int32, (MODES, WIDTH), 0) == 0
    pluses, minuses, middles = [], [], []
    for which in (2, 0):
        low = planes[which] * adjoint[at]
        high = planes[which + 1] * adjoint[at + 1]
        pluses.append(jnp.where(first, low, low + high))
        minuses.append(low - high)
        middles.append(high[0:1])
    every = slice(0, MODES)
    cos = apply(t_ref, 0, every, split(jnp.concatenate(pluses, axis=1)))
    sin = apply(t_ref, 1, every, split(jnp.concatenate(minuses, axis=1)))
    a1 = cos[:, :WIDTH] + sign * middles[0]
    a2 = cos[:, WIDTH:] + sign * middles[1]
    b1 = -sin[:, :WIDTH]
    b2 = -sin[:, WIDTH:]
    parts_to(out_ref, s_real - a1 - fraction * b2, s_imag - b1 + fraction * a2)


def second_stage(u_ref, s_ref, t_ref, out_ref, planes):
    real, imag = parts_of(u_ref)
    fraction, weight, sign = mode_rows(WIDTH)

    def store(rows, cos, sin):
        planes[0, rows, :] = cos[:, :WIDTH] - sin[:, :WIDTH]
        planes[1, rows, :] = cos[:, :WIDTH] + sin[:, :WIDTH]
        planes[2, rows, :] = -cos[:, WIDTH:] - sin[:, WIDTH:]
        planes[3, rows, :] = sin[:, WIDTH:] - cos[:, WIDTH:]

    cos_field = split(jnp.concatenate([real, fraction * imag], axis=1))
    sin_field = split(jnp.concatenate([imag, fraction * real], axis=1))
    to_planes(t_ref, cos_field, sin_field, store)
    planes[1, 0:1, :] = jnp.sum(sign * real, axis=0, keepdims=True)
    planes[3, 0:1, :] = -jnp.sum(sign * fraction * imag, axis=0, keepdims=True)
    finish(t_ref, s_ref, planes, planes, 4, out_ref)


def adjoint_planes(s_ref, t_ref, planes):
    s_real, s_imag = parts_of(s_ref)
    _, weight, sign = mode_rows(WIDTH)

    def store(rows, cos, sin):
        planes[4, rows, :] = cos - sin
        planes[5, rows, :] = cos + sin

    to_planes(t_ref, split(weight * s_real), split(weight * s_imag), store)
    planes[5, 0:1, :] = jnp.sum(sign * weight * s_real, axis=0, keepdims=True)


COUNT = N_MODE * N_MER
SPARE = GROUPS - 8


def send(source, target, mode, mer, sems, at):
    pltpu.make_async_remote_copy(
        src_ref=source,
        dst_ref=target,
        send_sem=sems[0].at[at],
        recv_sem=sems[1].at[at],
        device_id={"mode": mode, "mer": mer},
        device_id_type=pl.DeviceIdType.MESH,
    ).start()


def wait(blank, tiles, sem):
    whole = blank.at[pl.ds(0, tiles)]
    pltpu.make_async_copy(whole, whole, sem).wait()


def wait_either(double, blank, tiles_double, tiles_single, sem):
    @pl.when(double)
    def _():
        wait(blank, tiles_double, sem)

    @pl.when(jnp.logical_not(double))
    def _():
        wait(blank, tiles_single, sem)


def place_at(mer, k):
    y = lax.rem(lax.rem(mer, 4) + lax.rem(k, 4), 4)
    z = lax.rem(mer // 4 + k // 4, 4)
    return z * 4 + y


def each_group(mode, act):
    for other in range(N_MODE):

        @pl.when(mode != other)
        def _(other=other):
            act(other)


def each_place(mer, act):
    def body(k, _):
        act(place_at(mer, k))
        return 0

    lax.fori_loop(1, N_MER, body, 0)


def each_other(mode, mer, act):
    def body(place):
        for other in range(N_MODE):
            act(other, place)

    each_place(mer, body)
    each_group(mode, lambda other: act(other, mer))


def program_kernel(
    state_ref,
    cotangent_ref,
    mass_ref,
    inverse_ref,
    d_ref,
    t_ref,
    out_ref,
    rows,
    native_out,
    native_in,
    mode_out,
    mode_in,
    plane_out,
    plane_in,
    metric_out,
    metric_in,
    u_planes,
    planes,
    blank,
    send_sems,
    recv_sems,
    *solve_scratch,
):
    mode = lax.axis_index("mode")
    mer = lax.axis_index("mer")
    me = mode * N_MER + mer
    double = mode < SPARE
    sems = (send_sems, recv_sems)
    sent = []

    barrier = pltpu.get_barrier_semaphore()

    def greet(other, place):
        pl.semaphore_signal(
            barrier,
            inc=1,
            device_id={"mode": other, "mer": place},
            device_id_type=pl.DeviceIdType.MESH,
        )

    each_other(mode, mer, greet)
    native_to_tiles(state_ref, native_out.at[0], rows)
    pl.semaphore_wait(barrier, COUNT - 1)

    def send_to_planes(source, target, at):
        target[:, me] = source[:, mode, mer]

        def act(other, place):
            if other < SPARE:
                send(source.at[:, other, place], target.at[:, me], other, place, sems, at)
            else:
                send(source.at[0, other, place], target.at[0, me], other, place, sems, at)

        each_other(mode, mer, act)
        sent.append((at, 16 * GROUPS - 2, 16 * GROUPS - 1))

    def wait_planes(at):
        wait_either(double, blank, 2 * (COUNT - 1), COUNT - 1, recv_sems.at[at])

    def send_to_modes(source, target, at):
        target[:, mode, mer] = source[:, me]

        @pl.when(double)
        def _():
            def act(other, place):
                index = other * N_MER + place
                send(source.at[:, index], target.at[:, mode, mer], other, place, sems, at)

            each_other(mode, mer, act)

        @pl.when(jnp.logical_not(double))
        def _():
            def act(other, place):
                index = other * N_MER + place
                send(source.at[0, index], target.at[0, mode, mer], other, place, sems, at)

            each_other(mode, mer, act)

        sent.append((at, 2 * (COUNT - 1), COUNT - 1))

    def wait_modes(at):
        wait_either(double, blank, 16 * GROUPS - 2, 16 * GROUPS - 1, recv_sems.at[at])

    mine = pl.ds(pl.multiple_of(mode * N_MER, N_MER), N_MER)
    plane_in[0, :, mine] = native_out[0, :, mode]

    def send_state(other):
        if other < SPARE:
            send(native_out.at[0, :, other], plane_in.at[0, :, mine], other, mer, sems, 0)
        else:
            send(native_out.at[0, 0, other], plane_in.at[0, 0, mine], other, mer, sems, 0)

    each_group(mode, send_state)
    sent.append((0, N_MER * (GROUPS - 2), N_MER * (GROUPS - 1)))

    native_to_tiles(cotangent_ref, native_out.at[1], rows)
    mode_in[0, :, :, mer] = native_out[1, :, :, mer]
    metric_rows(mass_ref, inverse_ref, rows, metric_out)
    metric_in[mer] = metric_out[...]

    def send_cotangent(other):
        send(native_out.at[1, 0, :, other], mode_in.at[0, 0, :, mer], mode, other, sems, 1)
        send(native_out.at[1, 1, 0:SPARE, other], mode_in.at[0, 1, 0:SPARE, mer], mode, other, sems, 1)
        send(metric_out, metric_in.at[mer], mode, other, sems, 2)

    each_place(mer, send_cotangent)
    sent.append((1, (N_MER - 1) * GROUPS, (N_MER - 1) * GROUPS))
    sent.append((2, (N_MER - 1) * 4, (N_MER - 1) * 4))

    mass, diag, faces, k_ref = solve_scratch[:4]
    turn = solve_scratch[8]
    stiffness_tables(d_ref, k_ref)

    wait_either(double, blank, 2 * (N_MODE - 1) * N_MER, (N_MODE - 1) * N_MER, recv_sems.at[0])
    first_stage(plane_in.at[0], t_ref, plane_out.at[0], u_planes)
    send_to_modes(plane_out.at[0], mode_in.at[1], 3)

    wait(blank, (N_MER - 1) * 4, recv_sems.at[2])
    metric_tables(metric_in, mode, mer, mass, diag, faces, turn)
    wait(blank, (N_MER - 1) * GROUPS, recv_sems.at[1])
    solve(mode_in.at[0], mode_out.at[0], False, True, solve_scratch)
    send_to_planes(mode_out.at[0], plane_in.at[1], 4)

    wait_modes(3)
    solve(mode_in.at[1], mode_out.at[1], True, False, solve_scratch)
    send_to_planes(mode_out.at[1], plane_in.at[2], 5)

    wait_planes(4)
    adjoint_planes(plane_in.at[1], t_ref, planes)
    wait_planes(5)
    second_stage(plane_in.at[2], plane_in.at[1], t_ref, plane_out.at[1], planes)
    send_to_modes(plane_out.at[1], mode_in.at[2], 6)

    wait_modes(6)
    solve(mode_in.at[2], mode_out.at[2], False, True, solve_scratch)
    send_to_planes(mode_out.at[2], plane_in.at[3], 7)

    wait_planes(7)
    adjoint_planes(plane_in.at[3], t_ref, planes)
    finish(t_ref, plane_in.at[3], u_planes, planes, 4, plane_out.at[2])

    native_in[:, mode] = plane_out[2, :, mine]

    def send_gradient(other):
        theirs = slice(other * N_MER, (other + 1) * N_MER)

        @pl.when(double)
        def _():
            send(plane_out.at[2, :, theirs], native_in.at[:, mode], other, mer, sems, 8)

        @pl.when(jnp.logical_not(double))
        def _():
            send(plane_out.at[2, 0, theirs], native_in.at[0, mode], other, mer, sems, 8)

    each_group(mode, send_gradient)
    sent.append((8, 2 * (N_MODE - 1) * N_MER, (N_MODE - 1) * N_MER))
    wait_either(double, blank, N_MER * (GROUPS - 2), N_MER * (GROUPS - 1), recv_sems.at[8])
    for group in range(GROUPS):
        out_ref[group] = native_in[group // 8, group % 8]
    for at, tiles_double, tiles_single in sent:
        wait_either(double, blank, tiles_double, tiles_single, send_sems.at[at])


def program(state, cotangent, mass, inverse, derivative, table):
    by_mode = (2, N_MODE, N_MER, 8, LANES)
    by_plane = (2, COUNT, 8, LANES)

    def scratch(count, shape):
        return pltpu.VMEM((count,) + shape, F32)

    return pl.pallas_call(
        program_kernel,
        out_shape=jax.ShapeDtypeStruct((GROUPS, N_MER, 8, LANES), F32),
        in_specs=[pl.BlockSpec(memory_space=pltpu.VMEM)] * 6,
        out_specs=pl.BlockSpec(memory_space=pltpu.VMEM),
        scratch_shapes=[
            pltpu.VMEM((PADDED * ELEM_DEV, LANES), F32),
            scratch(2, by_mode),
            pltpu.VMEM(by_mode, F32),
            scratch(3, by_mode),
            scratch(3, by_mode),
            scratch(3, by_plane),
            scratch(4, by_plane),
            pltpu.VMEM((2, 16, LANES), F32),
            scratch(N_MER, (2, 16, LANES)),
            pltpu.VMEM((4, MODES, WIDTH), F32),
            pltpu.VMEM((6, MODES, WIDTH), F32),
            pltpu.VMEM((2 * COUNT, 8, LANES), F32),
            pltpu.SemaphoreType.DMA((9,)),
            pltpu.SemaphoreType.DMA((9,)),
            *SOLVE_SCRATCH,
        ],
        compiler_params=pltpu.CompilerParams(
            collective_id=0, has_side_effects=True, vmem_limit_bytes=60 << 20
        ),
        name="program",
    )(state, cotangent, mass, inverse, derivative, table)


def shards(cotangent, checkpoint, mass, inv_radius_sq, derivative):
    table = jnp.asarray(tables())
    return tiles_to_native(program(checkpoint, cotangent, mass, inv_radius_sq, derivative, table))


def solution(mesh):
    return jax.shard_map(
        shards,
        mesh=mesh,
        in_specs=(
            P(None, None, ("mer", "mode")),
            P(None, None, ("mer", "mode")),
            P(None, None, "mer"),
            P(None, None, "mer"),
            P(),
        ),
        out_specs=P(None, None, ("mer", "mode")),
        check_vma=False,
    )
```

time: 286 us -> 121 us (0.42)
  blocking collectives: 144 us -> 0 us
  Pallas kernels: 74.2 us -> 120 us
  starting transfers between devices: 38.1 us -> 0 us
  waiting for transfers between devices: 20.5 us -> 0 us
  local copies, waits for them, and re-layouts: 8.41 us -> 1.1 us
    all_to_all x4 -> x0, blocking collectives: 93.2 us -> none  [the longest x2 51.4 us: modes_to_planes(): return lax.all_to_all(sent, ('mode', 'mer'), 0, 0)]
    all_gather x2 -> x0, blocking collectives: 50.4 us -> none  [the longest x1 30.9 us: shards(): lax.all_gather(inv_radius_sq, 'mer', axis=2, tiled=True)]
    pallas_call x8 -> x1, Pallas kernels: 72.8 us -> 118 us  [program(): pl.pallas_call(program_kernel, out_shape=jax.ShapeDtypeStruct((GROUPS, N_...]
    all_to_all x4 -> x0, starting transfers between devices: 38.1 us -> none  [the longest x1 17.7 us: modes_to_planes(): return lax.all_to_all(sent, ('mode', 'mer'), 0, 0)]
    all_to_all x4 -> x0, waiting for transfers between devices: 20.5 us -> none  [the longest x1 13.8 us: native_to_planes(): got = lax.all_to_all(sent, 'mode', 0, 0)]
    reshape x11 -> x0, local copies, waits for them, and re-layouts: 5.25 us -> none  [the longest x4 2.31 us: by_slot(): return tiles.reshape(tiles.shape[:axis] + (2, 8) + tiles.shape[axis + 1:])]
  transfers between devices with their start and end apart: 4 -> 0, of which waited for: 2 -> 0; matrix products, arithmetic and copies ran while one was open for 2% -> 0% of each run, Pallas kernels for 15% -> 0%
where the time goes in v2:
time: 121 us
  Pallas kernels  120 us (99%)
    pallas_call x1, Pallas kernels, program(): pl.pallas_call(program_kernel, out_shape=jax.ShapeDtypeStruct((GROUPS, N_...  118 us

profile of v2, /device:TPU:1, one launch (start us, length us, event | category | flops | bytes accessed | tf_op | source)
XLA Modules:
  0.0 120.6 jit_solution(3237175420134851191)
XLA Ops:
  0.0 118.1 %program.1.t_ref = f32[11,16,8,128]{3,2,1,0:T(8,128)} custom-call(f32[9,9,2048]{2,1,0:T(8,128)} %state_ref.1, f32[9,9,2048]{2,1,0:T(8,128)} %cotangent_ref.1, f32[9,9,16]{2,1,0:T(8,128)} %mass_ref.1, f32[9,9,16]{2,1,0:T(8,128)} %inverse_ref.1, f32[9,9]{1,0:T(8,128)} %d_ref.1, bf16[4,512,512]{2,1,0:T(8,128)(2,1)} %constant.2.clone.t_ref), custom_call_target="tpu_custom_call" | custom-call | tf_op jit(solution)/shard_map/program/pallas_call | solution.py:678
  118.1 0.0 copy-start
  118.1 1.1 copy-done
  119.3 1.4 %tiles_to_native.1 = f32[9,9,2048]{2,1,0:T(8,128)} custom-call(f32[11,16,8,128]{3,2,1,0:T(8,128)S(1)} %copy-done), custom_call_target="tpu_custom_call" | custom-call | tf_op jit(solution)/shard_map/tiles_to_native/pallas_call | solution.py:99
Async XLA Ops:
  118.1 1.1 copy-start

commit v3 on v2

--- a/solution.py
+++ b/solution.py
@@ -30,7 +30,8 @@
 
 
 def tables():
-    index = np.outer(np.arange(MODES), np.arange(MODES)) % PLANES
+    order = np.arange(MODES).reshape(4, 2, 64).transpose(1, 0, 2).reshape(-1)
+    index = np.outer(order, order) % PLANES
     angles = index.astype(np.float64) * (2.0 * math.pi / PLANES)
     out = []
     for values in (np.cos(angles), np.sin(angles)):
@@ -82,9 +83,9 @@
         out_ref[group // 8, group % 8] = jnp.stack([even, odd], axis=1).reshape(N_MER, 8, LANES)
 
 
-def tiles_to_native_kernel(t_ref, out_ref, rows):
+def tiles_to_native(t_ref, out_ref, rows):
     for group in range(GROUPS):
-        tiles = t_ref[group].reshape(8, 2, 8, LANES)
+        tiles = t_ref[group // 8, group % 8].reshape(8, 2, 8, LANES)
         real, imag = mix(tiles[:, 0], tiles[:, 1])
         both = jnp.concatenate([real.reshape(64, LANES), imag.reshape(64, LANES)], axis=0)
         rows[group * LANES : (group + 1) * LANES, :] = both.T
@@ -93,16 +94,6 @@
             out_ref[i, :, e * LANES : (e + 1) * LANES] = rows[
                 pl.ds(i * NODE * ELEM_DEV + e, NODE, stride=ELEM_DEV), :
             ]
-
-
-def tiles_to_native(tiles):
-    return pl.pallas_call(
-        tiles_to_native_kernel,
-        out_shape=jax.ShapeDtypeStruct((NODE, NODE, ELEM_DEV * LANES), F32),
-        scratch_shapes=[pltpu.VMEM((PADDED * ELEM_DEV, LANES), F32)],
-        compiler_params=pltpu.CompilerParams(vmem_limit_bytes=32 << 20),
-        name="tiles_to_native",
-    )(tiles)
 
 
 def stiffness_tables(d_ref, k_ref):
@@ -198,20 +189,25 @@
                 out[s, rows, lanes] = value
 
 
-def store_tiles(value_of, turn, out_ref):
-    for s in range(8):
-        value = value_of(s)
-        for h in range(2):
-            for group in range(GROUPS):
-                turn[h, group, pl.ds(s, 8, stride=8), :] = value[
-                    group * 8 : (group + 1) * 8, h * LANES : (h + 1) * LANES
-                ]
-    for slot, start, stop in CHUNKS:
-        for h in range(2):
-            groups = slice(8 * slot + start, 8 * slot + stop)
-            tiles = exchange([turn[h, groups, at * 8 : (at + 1) * 8] for at in range(8)])
-            for at in range(8):
-                out_ref[slot, start:stop, 8 * h + at] = tiles[at]
+OWNED = (((0, 0), (0, 2), (0, 4), (0, 6), (1, 0), (1, 1), (1, 2)), ((0, 1), (0, 3), (0, 5), (0, 7)))
+
+
+def store_tiles(value_of, turn, out_ref, emit):
+    for core in range(2):
+        for s in range(8):
+            for slot, at_group in OWNED[core]:
+                group = 8 * slot + at_group
+                for h in range(2):
+                    turn[h, group, pl.ds(s, 8, stride=8), :] = value_of(
+                        s, slice(group * 8, (group + 1) * 8), slice(h * LANES, (h + 1) * LANES)
+                    )
+        for slot, at_group in OWNED[core]:
+            for h in range(2):
+                group = 8 * slot + at_group
+                tiles = exchange([turn[h, group, at * 8 : (at + 1) * 8] for at in range(8)])
+                for at in range(8):
+                    out_ref[slot, at_group, 8 * h + at] = tiles[at]
+        emit(core)
 
 
 def total(parts):
@@ -223,7 +219,7 @@
     return jnp.sum(value.reshape(GROUPS, 8, ELEMENTS), axis=0)
 
 
-def solve(b_ref, out_ref, weigh_in, weigh_out, scratch):
+def solve(b_ref, out_ref, weigh_in, weigh_out, scratch, emit):
     mass, diag, faces, k_ref, x, r, p, q, turn = scratch
     load_tiles(b_ref, turn, mass if weigh_in else None, r)
     norms = []
@@ -291,11 +287,11 @@
     none = [jnp.zeros((1, ELEMENTS), F32)] * 4
     norms, alphas, betas = lax.fori_loop(0, ITERS, sweep_body, (norms, none, none))
 
-    def value_of(s):
-        value = x[s] + alphas[s % 4] * p[s]
-        return value * mass[...] if weigh_out else value
-
-    store_tiles(value_of, turn, out_ref)
+    def value_of(s, rows, lanes):
+        value = x[s, rows, lanes] + alphas[s % 4][:, lanes] * p[s, rows, lanes]
+        return value * mass[rows, lanes] if weigh_out else value
+
+    store_tiles(value_of, turn, out_ref, emit)
 
 
 FIELD = pltpu.VMEM((8, PADDED, ELEMENTS), F32)
@@ -338,17 +334,21 @@
     return jnp.concatenate(real, axis=1), jnp.concatenate(imag, axis=1)
 
 
-def parts_to(out_ref, real, imag):
+def parts_to(out_ref, half, real, imag):
+    count = MODES // 2 // 8
     for slot in range(2):
         lanes = slice(slot * LANES, (slot + 1) * LANES)
         one, two = mix(
-            real[:, lanes].reshape(MODES // 8, 8, LANES), imag[:, lanes].reshape(MODES // 8, 8, LANES)
+            real[:, lanes].reshape(count, 8, LANES), imag[:, lanes].reshape(count, 8, LANES)
         )
-        out_ref[slot] = jnp.stack([one, two], axis=1).reshape(MODES // 4, 8, LANES)
+        out_ref[slot, 2 * count * half : 2 * count * (half + 1)] = jnp.stack(
+            [one, two], axis=1
+        ).reshape(2 * count, 8, LANES)
 
 
 def mode_rows(width):
-    mode = lax.broadcasted_iota(jnp.int32, (MODES, width), 0)
+    row = lax.broadcasted_iota(jnp.int32, (MODES, width), 0)
+    mode = (row // 64 % 4 * 2 + row // 256) * 64 + row % 64
     fraction = mode.astype(F32) / MODES
     weight = jnp.where(mode == 0, 1.0 / PLANES, 2.0 / PLANES).astype(F32)
     sign = jnp.where(mode % 2 == 0, 1.0, -1.0).astype(F32)
@@ -365,7 +365,7 @@
         outs(rows, apply(t_ref, 0, rows, cos_field), apply(t_ref, 1, rows, sin_field))
 
 
-def first_stage(u_ref, t_ref, out_ref, planes_ref):
+def first_stage(u_ref, t_ref, out_ref, planes_ref, emit):
     real, imag = parts_of(u_ref)
     fraction, weight, sign = mode_rows(WIDTH)
     cos_field = split(jnp.concatenate([real, fraction * imag], axis=1))
@@ -386,13 +386,17 @@
     high = planes_ref[1] * planes_ref[3]
     first = lax.broadcasted_iota(jnp.int32, (MODES, WIDTH), 0) == 0
     cos_side, sin_side = split(jnp.where(first, low, low + high)), split(low - high)
-    every = slice(0, MODES)
-    a = apply(t_ref, 0, every, cos_side) + sign * high[0:1]
-    b = -apply(t_ref, 1, every, sin_side)
-    parts_to(out_ref, real - weight * a, imag - weight * b)
-
-
-def finish(t_ref, s_ref, planes, adjoint, at, out_ref):
+    for half in range(2):
+        rows = slice(half * 256, (half + 1) * 256)
+        a = apply(t_ref, 0, rows, cos_side) + sign[rows] * high[0:1]
+        b = -apply(t_ref, 1, rows, sin_side)
+        parts_to(
+            out_ref, half, real[rows] - weight[rows] * a, imag[rows] - weight[rows] * b
+        )
+        emit(half)
+
+
+def finish(t_ref, s_ref, planes, adjoint, at, out_ref, emit):
     s_real, s_imag = parts_of(s_ref)
     fraction, _, sign = mode_rows(WIDTH)
     first = lax.broadcasted_iota(jnp.int32, (MODES, WIDTH), 0) == 0
@@ -403,17 +407,26 @@
         pluses.append(jnp.where(first, low, low + high))
         minuses.append(low - high)
         middles.append(high[0:1])
-    every = slice(0, MODES)
-    cos = apply(t_ref, 0, every, split(jnp.concatenate(pluses, axis=1)))
-    sin = apply(t_ref, 1, every, split(jnp.concatenate(minuses, axis=1)))
-    a1 = cos[:, :WIDTH] + sign * middles[0]
-    a2 = cos[:, WIDTH:] + sign * middles[1]
-    b1 = -sin[:, :WIDTH]
-    b2 = -sin[:, WIDTH:]
-    parts_to(out_ref, s_real - a1 - fraction * b2, s_imag - b1 + fraction * a2)
-
-
-def second_stage(u_ref, s_ref, t_ref, out_ref, planes):
+    cos_side = split(jnp.concatenate(pluses, axis=1))
+    sin_side = split(jnp.concatenate(minuses, axis=1))
+    for half in range(2):
+        rows = slice(half * 256, (half + 1) * 256)
+        cos = apply(t_ref, 0, rows, cos_side)
+        sin = apply(t_ref, 1, rows, sin_side)
+        a1 = cos[:, :WIDTH] + sign[rows] * middles[0]
+        a2 = cos[:, WIDTH:] + sign[rows] * middles[1]
+        b1 = -sin[:, :WIDTH]
+        b2 = -sin[:, WIDTH:]
+        parts_to(
+            out_ref,
+            half,
+            s_real[rows] - a1 - fraction[rows] * b2,
+            s_imag[rows] - b1 + fraction[rows] * a2,
+        )
+        emit(half)
+
+
+def second_stage(u_ref, s_ref, t_ref, out_ref, planes, emit):
     real, imag = parts_of(u_ref)
     fraction, weight, sign = mode_rows(WIDTH)
 
@@ -428,7 +441,7 @@
     to_planes(t_ref, cos_field, sin_field, store)
     planes[1, 0:1, :] = jnp.sum(sign * real, axis=0, keepdims=True)
     planes[3, 0:1, :] = -jnp.sum(sign * fraction * imag, axis=0, keepdims=True)
-    finish(t_ref, s_ref, planes, planes, 4, out_ref)
+    finish(t_ref, s_ref, planes, planes, 4, out_ref, emit)
 
 
 def adjoint_planes(s_ref, t_ref, planes):
@@ -479,12 +492,19 @@
     return z * 4 + y
 
 
-def each_group(mode, act):
-    for other in range(N_MODE):
-
-        @pl.when(mode != other)
-        def _(other=other):
-            act(other)
+def extra(x, mer):
+    turn = lax.rem(lax.rem(mer, 4) + mer // 4, 4)
+    return lax.rem(x + 4 - turn, 4)
+
+
+def each_group(mode, cores, act):
+    for core in cores:
+        for x in range(4):
+            other = 2 * x + core
+
+            @pl.when(mode != other)
+            def _(other=other):
+                act(other)
 
 
 def each_place(mer, act):
@@ -495,23 +515,31 @@
     lax.fori_loop(1, N_MER, body, 0)
 
 
-def each_other(mode, mer, act):
+def each_other(mode, mer, cores, act):
     def body(place):
-        for other in range(N_MODE):
-            act(other, place)
+        for core in cores:
+            for x in range(4):
+                act(2 * x + core, place)
 
     each_place(mer, body)
-    each_group(mode, lambda other: act(other, mer))
+    each_group(mode, cores, lambda other: act(other, mer))
+
+
+def order_of(mode):
+    return lax.rem(mode, 2) * 4 + mode // 2 if not isinstance(mode, int) else mode % 2 * 4 + mode // 2
 
 
 def program_kernel(
     state_ref,
-    cotangent_ref,
+    cotangent_hbm,
     mass_ref,
     inverse_ref,
     d_ref,
+    t_hbm,
+    out_ref,
+    cotangent_in,
     t_ref,
-    out_ref,
+    copy_sems,
     rows,
     native_out,
     native_in,
@@ -530,11 +558,16 @@
 ):
     mode = lax.axis_index("mode")
     mer = lax.axis_index("mer")
-    me = mode * N_MER + mer
-    double = mode < SPARE
+    me = order_of(mode) * N_MER + mer
+    mine_extra = extra(mode // 2, mer)
+    double = (lax.rem(mode, 2) == 0) & (mine_extra < SPARE)
     sems = (send_sems, recv_sems)
     sent = []
 
+    cotangent_copy = pltpu.make_async_copy(cotangent_hbm, cotangent_in, copy_sems.at[0])
+    table_copy = pltpu.make_async_copy(t_hbm, t_ref, copy_sems.at[1])
+    cotangent_copy.start()
+    table_copy.start()
     barrier = pltpu.get_barrier_semaphore()
 
     def greet(other, place):
@@ -545,62 +578,82 @@
             device_id_type=pl.DeviceIdType.MESH,
         )
 
-    each_other(mode, mer, greet)
+    each_other(mode, mer, (0, 1), greet)
     native_to_tiles(state_ref, native_out.at[0], rows)
     pl.semaphore_wait(barrier, COUNT - 1)
 
     def send_to_planes(source, target, at):
-        target[:, me] = source[:, mode, mer]
-
         def act(other, place):
-            if other < SPARE:
-                send(source.at[:, other, place], target.at[:, me], other, place, sems, at)
-            else:
-                send(source.at[0, other, place], target.at[0, me], other, place, sems, at)
-
-        each_other(mode, mer, act)
+            send(source.at[0, other, place], target.at[0, me], other, place, sems, at)
+            if other % 2 == 0:
+                index = extra(other // 2, place)
+
+                @pl.when(index < SPARE)
+                def _():
+                    send(source.at[1, index, place], target.at[1, me], other, place, sems, at)
+
+        def emit(core):
+            each_other(mode, mer, (core,), act)
+            if core == 1:
+                target[0, me] = source[0, mode, mer]
+                target[1, me] = source[1, mine_extra, mer]
+
         sent.append((at, 16 * GROUPS - 2, 16 * GROUPS - 1))
+        return emit
 
     def wait_planes(at):
         wait_either(double, blank, 2 * (COUNT - 1), COUNT - 1, recv_sems.at[at])
 
     def send_to_modes(source, target, at):
-        target[:, mode, mer] = source[:, me]
-
-        @pl.when(double)
-        def _():
-            def act(other, place):
-                index = other * N_MER + place
-                send(source.at[:, index], target.at[:, mode, mer], other, place, sems, at)
-
-            each_other(mode, mer, act)
-
-        @pl.when(jnp.logical_not(double))
-        def _():
-            def act(other, place):
-                index = other * N_MER + place
-                send(source.at[0, index], target.at[0, mode, mer], other, place, sems, at)
-
-            each_other(mode, mer, act)
+        def act(other, place):
+            index = order_of(other) * N_MER + place
+            send(source.at[0, index], target.at[0, mode, mer], other, place, sems, at)
+
+        def act_double(other, place):
+            index = order_of(other) * N_MER + place
+            send(source.at[0, index], target.at[0, mode, mer], other, place, sems, at)
+            send(source.at[1, index], target.at[1, mine_extra, mer], other, place, sems, at)
+
+        def emit(core):
+            @pl.when(double)
+            def _():
+                each_other(mode, mer, (core,), act_double)
+
+            @pl.when(jnp.logical_not(double))
+            def _():
+                each_other(mode, mer, (core,), act)
+
+            if core == 1:
+                target[0, mode, mer] = source[0, me]
+
+                @pl.when(double)
+                def _():
+                    target[1, mine_extra, mer] = source[1, me]
 
         sent.append((at, 2 * (COUNT - 1), COUNT - 1))
+        return emit
 
     def wait_modes(at):
         wait_either(double, blank, 16 * GROUPS - 2, 16 * GROUPS - 1, recv_sems.at[at])
 
-    mine = pl.ds(pl.multiple_of(mode * N_MER, N_MER), N_MER)
-    plane_in[0, :, mine] = native_out[0, :, mode]
+    mine = pl.ds(pl.multiple_of(order_of(mode) * N_MER, N_MER), N_MER)
+    plane_in[0, 0, mine] = native_out[0, 0, mode]
+    plane_in[0, 1, mine] = native_out[0, 1, mine_extra]
 
     def send_state(other):
-        if other < SPARE:
-            send(native_out.at[0, :, other], plane_in.at[0, :, mine], other, mer, sems, 0)
-        else:
-            send(native_out.at[0, 0, other], plane_in.at[0, 0, mine], other, mer, sems, 0)
-
-    each_group(mode, send_state)
+        send(native_out.at[0, 0, other], plane_in.at[0, 0, mine], other, mer, sems, 0)
+        if other % 2 == 0:
+            index = extra(other // 2, mer)
+
+            @pl.when(index < SPARE)
+            def _():
+                send(native_out.at[0, 1, index], plane_in.at[0, 1, mine], other, mer, sems, 0)
+
+    each_group(mode, (0, 1), send_state)
     sent.append((0, N_MER * (GROUPS - 2), N_MER * (GROUPS - 1)))
 
-    native_to_tiles(cotangent_ref, native_out.at[1], rows)
+    cotangent_copy.wait()
+    native_to_tiles(cotangent_in, native_out.at[1], rows)
     mode_in[0, :, :, mer] = native_out[1, :, :, mer]
     metric_rows(mass_ref, inverse_ref, rows, metric_out)
     metric_in[mer] = metric_out[...]
@@ -619,51 +672,55 @@
     stiffness_tables(d_ref, k_ref)
 
     wait_either(double, blank, 2 * (N_MODE - 1) * N_MER, (N_MODE - 1) * N_MER, recv_sems.at[0])
-    first_stage(plane_in.at[0], t_ref, plane_out.at[0], u_planes)
-    send_to_modes(plane_out.at[0], mode_in.at[1], 3)
+    table_copy.wait()
+    emit = send_to_modes(plane_out.at[0], mode_in.at[1], 3)
+    first_stage(plane_in.at[0], t_ref, plane_out.at[0], u_planes, emit)
 
     wait(blank, (N_MER - 1) * 4, recv_sems.at[2])
     metric_tables(metric_in, mode, mer, mass, diag, faces, turn)
     wait(blank, (N_MER - 1) * GROUPS, recv_sems.at[1])
-    solve(mode_in.at[0], mode_out.at[0], False, True, solve_scratch)
-    send_to_planes(mode_out.at[0], plane_in.at[1], 4)
+    emit = send_to_planes(mode_out.at[0], plane_in.at[1], 4)
+    solve(mode_in.at[0], mode_out.at[0], False, True, solve_scratch, emit)
 
     wait_modes(3)
-    solve(mode_in.at[1], mode_out.at[1], True, False, solve_scratch)
-    send_to_planes(mode_out.at[1], plane_in.at[2], 5)
+    emit = send_to_planes(mode_out.at[1], plane_in.at[2], 5)
+    solve(mode_in.at[1], mode_out.at[1], True, False, solve_scratch, emit)
 
     wait_planes(4)
     adjoint_planes(plane_in.at[1], t_ref, planes)
     wait_planes(5)
-    second_stage(plane_in.at[2], plane_in.at[1], t_ref, plane_out.at[1], planes)
-    send_to_modes(plane_out.at[1], mode_in.at[2], 6)
+    emit = send_to_modes(plane_out.at[1], mode_in.at[2], 6)
+    second_stage(plane_in.at[2], plane_in.at[1], t_ref, plane_out.at[1], planes, emit)
 
     wait_modes(6)
-    solve(mode_in.at[2], mode_out.at[2], False, True, solve_scratch)
-    send_to_planes(mode_out.at[2], plane_in.at[3], 7)
+    emit = send_to_planes(mode_out.at[2], plane_in.at[3], 7)
+    solve(mode_in.at[2], mode_out.at[2], False, True, solve_scratch, emit)
 
     wait_planes(7)
     adjoint_planes(plane_in.at[3], t_ref, planes)
-    finish(t_ref, plane_in.at[3], u_planes, planes, 4, plane_out.at[2])
-
-    native_in[:, mode] = plane_out[2, :, mine]
+
 
     def send_gradient(other):
-        theirs = slice(other * N_MER, (other + 1) * N_MER)
+        theirs = slice(order_of(other) * N_MER, (order_of(other) + 1) * N_MER)
+        send(plane_out.at[2, 0, theirs], native_in.at[0, mode], other, mer, sems, 8)
 
         @pl.when(double)
         def _():
-            send(plane_out.at[2, :, theirs], native_in.at[:, mode], other, mer, sems, 8)
-
-        @pl.when(jnp.logical_not(double))
-        def _():
-            send(plane_out.at[2, 0, theirs], native_in.at[0, mode], other, mer, sems, 8)
-
-    each_group(mode, send_gradient)
+            send(plane_out.at[2, 1, theirs], native_in.at[1, mine_extra], other, mer, sems, 8)
+
+    def emit_gradient(core):
+        each_group(mode, (core,), send_gradient)
+
+    finish(t_ref, plane_in.at[3], u_planes, planes, 4, plane_out.at[2], emit_gradient)
+    native_in[0, mode] = plane_out[2, 0, mine]
+
+    @pl.when(double)
+    def _():
+        native_in[1, mine_extra] = plane_out[2, 1, mine]
+
     sent.append((8, 2 * (N_MODE - 1) * N_MER, (N_MODE - 1) * N_MER))
     wait_either(double, blank, N_MER * (GROUPS - 2), N_MER * (GROUPS - 1), recv_sems.at[8])
-    for group in range(GROUPS):
-        out_ref[group] = native_in[group // 8, group % 8]
+    tiles_to_native(native_in, out_ref, rows)
     for at, tiles_double, tiles_single in sent:
         wait_either(double, blank, tiles_double, tiles_single, send_sems.at[at])
 
@@ -671,16 +728,21 @@
 def program(state, cotangent, mass, inverse, derivative, table):
     by_mode = (2, N_MODE, N_MER, 8, LANES)
     by_plane = (2, COUNT, 8, LANES)
+    vmem = pl.BlockSpec(memory_space=pltpu.VMEM)
+    hbm = pl.BlockSpec(memory_space=pl.ANY)
 
     def scratch(count, shape):
         return pltpu.VMEM((count,) + shape, F32)
 
     return pl.pallas_call(
         program_kernel,
-        out_shape=jax.ShapeDtypeStruct((GROUPS, N_MER, 8, LANES), F32),
-        in_specs=[pl.BlockSpec(memory_space=pltpu.VMEM)] * 6,
-        out_specs=pl.BlockSpec(memory_space=pltpu.VMEM),
+        out_shape=jax.ShapeDtypeStruct((NODE, NODE, ELEM_DEV * LANES), F32),
+        in_specs=[vmem, hbm, vmem, vmem, vmem, hbm],
+        out_specs=vmem,
         scratch_shapes=[
+            pltpu.VMEM((NODE, NODE, ELEM_DEV * LANES), F32),
+            pltpu.VMEM((4, MODES, MODES), BF16),
+            pltpu.SemaphoreType.DMA((2,)),
             pltpu.VMEM((PADDED * ELEM_DEV, LANES), F32),
             scratch(2, by_mode),
             pltpu.VMEM(by_mode, F32),
@@ -706,7 +768,7 @@
 
 def shards(cotangent, checkpoint, mass, inv_radius_sq, derivative):
     table = jnp.asarray(tables())
-    return tiles_to_native(program(checkpoint, cotangent, mass, inv_radius_sq, derivative, table))
+    return program(checkpoint, cotangent, mass, inv_radius_sq, derivative, table)
 
 
 def solution(mesh):

time: 121 us -> 104 us (0.86)
  Pallas kernels: 120 us -> 101 us
  local copies, waits for them, and re-layouts: 1.1 us -> 2.39 us
    pallas_call x2 -> x1, Pallas kernels: 120 us -> 101 us  [program(): pl.pallas_call(program_kernel, out_shape=jax.ShapeDtypeStruct((NODE, NODE...]
    unnamed x2 -> x1, local copies, waits for them, and re-layouts: 1.1 us -> 2.39 us
where the time goes in v3:
time: 104 us
  Pallas kernels  101 us (97%)
  local copies, waits for them, and re-layouts  2.39 us (2%)
    pallas_call x1, Pallas kernels, program(): pl.pallas_call(program_kernel, out_shape=jax.ShapeDtypeStruct((NODE, NODE...  101 us
    unnamed x1, local copies, waits for them, and re-layouts  2.39 us

profile of v3, /device:TPU:1, one launch (start us, length us, event | category | flops | bytes accessed | tf_op | source)
XLA Modules:
  0.0 103.8 jit_solution(10017652878887350498)
XLA Ops:
  0.0 101.4 %program.1 = f32[9,9,2048]{2,1,0:T(8,128)} custom-call(f32[9,9,2048]{2,1,0:T(8,128)} %state_ref.1, f32[9,9,2048]{2,1,0:T(8,128)} %cotangent_hbm.1, f32[9,9,16]{2,1,0:T(8,128)} %mass_ref.1, f32[9,9,16]{2,1,0:T(8,128)} %inverse_ref.1, f32[9,9]{1,0:T(8,128)} %d_ref.1, bf16[4,512,512]{2,1,0:T(8,128)(2,1)} %constant.2.clone.t_hbm), custom_call_target="tpu_custom_call" | custom-call | tf_op jit(solution)/shard_map/program/pallas_call | solution.py:737
  101.4 2.4 %copy.8 = f32[9,9,2048]{2,1,0:T(8,128)} copy(f32[9,9,2048]{2,1,0:T(8,128)} %program.1) | data formatting | bytes 1327104

commit v4 on v3

--- a/solution.py
+++ b/solution.py
@@ -15,6 +15,7 @@
 RADIAL = 8
 ITERS = 4
 MODES = 512
+HALF = 256
 PLANES = 1024
 ELEMENTS = 256
 N_MODE = 8
@@ -30,16 +31,18 @@
 
 
 def tables():
-    order = np.arange(MODES).reshape(4, 2, 64).transpose(1, 0, 2).reshape(-1)
-    index = np.outer(order, order) % PLANES
-    angles = index.astype(np.float64) * (2.0 * math.pi / PLANES)
+    order = np.arange(HALF).reshape(4, 2, HALF // N_MODE).transpose(1, 0, 2).reshape(-1)
     out = []
-    for values in (np.cos(angles), np.sin(angles)):
-        values = values.astype(np.float32)
-        high = values.astype(ml_dtypes.bfloat16)
-        low = (values - high.astype(np.float32)).astype(ml_dtypes.bfloat16)
-        out += [high, low]
-    return np.stack(out)
+    for wave in (np.cos, np.sin):
+        for odd in range(2):
+            index = np.outer(np.arange(HALF), 2 * order + odd) % PLANES
+            values = wave(index.astype(np.float64) * (2.0 * math.pi / PLANES)).astype(np.float32)
+            high = values.astype(ml_dtypes.bfloat16)
+            low = (values - high.astype(np.float32)).astype(ml_dtypes.bfloat16)
+            out.append((high, low))
+    both = [np.concatenate(pair) for pair in out]
+    turned = [np.concatenate([high.T, low.T]) for high, low in out]
+    return np.stack(both + turned)
 
 
 def mix(first, second):
@@ -67,7 +70,7 @@
     return tiles
 
 
-def native_to_tiles(x_ref, out_ref, rows):
+def native_to_tiles(x_ref, out_ref, rows, turn):
     rows[pl.ds(NODES * ELEM_DEV, PADDED * ELEM_DEV - NODES * ELEM_DEV), :] = jnp.zeros(
         ((PADDED - NODES) * ELEM_DEV, LANES), F32
     )
@@ -78,16 +81,23 @@
             ]
     for group in range(GROUPS):
         turned = rows[group * LANES : (group + 1) * LANES, :].T
-        both = turned.reshape(2, 8, 8, LANES)
-        even, odd = mix(both[0], both[1])
-        out_ref[group // 8, group % 8] = jnp.stack([even, odd], axis=1).reshape(N_MER, 8, LANES)
-
-
-def tiles_to_native(t_ref, out_ref, rows):
+        turn[0, group] = turned[:64]
+        turn[1, group] = turned[64:]
+        for odd in range(2):
+            real = turn[0, group, pl.ds(odd, 32, stride=2), :].reshape(4, 8, LANES)
+            imag = turn[1, group, pl.ds(odd, 32, stride=2), :].reshape(4, 8, LANES)
+            one, two = mix(real, imag)
+            out_ref[group // 8, group % 8, odd] = jnp.stack([one, two], axis=1).reshape(8, 8, LANES)
+
+
+def tiles_to_native(t_ref, out_ref, rows, turn):
     for group in range(GROUPS):
-        tiles = t_ref[group // 8, group % 8].reshape(8, 2, 8, LANES)
-        real, imag = mix(tiles[:, 0], tiles[:, 1])
-        both = jnp.concatenate([real.reshape(64, LANES), imag.reshape(64, LANES)], axis=0)
+        for odd in range(2):
+            tiles = t_ref[group // 8, group % 8, odd].reshape(4, 2, 8, LANES)
+            real, imag = mix(tiles[:, 0], tiles[:, 1])
+            turn[0, group, pl.ds(odd, 32, stride=2), :] = real.reshape(32, LANES)
+            turn[1, group, pl.ds(odd, 32, stride=2), :] = imag.reshape(32, LANES)
+        both = jnp.concatenate([turn[0, group], turn[1, group]], axis=0)
         rows[group * LANES : (group + 1) * LANES, :] = both.T
     for i in range(NODE):
         for e in range(ELEM_DEV):
@@ -165,7 +175,8 @@
     count = marks[0] + marks[1] + marks[2] + marks[3]
     values = inverse[...]
     for n in range(4):
-        fraction = (mode_group * 64 + place * 4 + n).astype(F32) / MODES
+        number = mode_group * 64 + lax.rem(place, 8) * 8 + 2 * n + place // 8
+        fraction = number.astype(F32) / MODES
         diag[n] = mass[...] * (1.0 + AZIMUTH_WEIGHT * fraction * fraction * values) + count
 
 
@@ -189,25 +200,25 @@
                 out[s, rows, lanes] = value
 
 
-OWNED = (((0, 0), (0, 2), (0, 4), (0, 6), (1, 0), (1, 1), (1, 2)), ((0, 1), (0, 3), (0, 5), (0, 7)))
+OWNED = (((1, 0), (1, 1), (1, 2)), ((0, 0), (0, 2), (0, 4), (0, 6)), ((0, 1), (0, 3), (0, 5), (0, 7)))
 
 
 def store_tiles(value_of, turn, out_ref, emit):
-    for core in range(2):
+    for phase in range(3):
         for s in range(8):
-            for slot, at_group in OWNED[core]:
+            for slot, at_group in OWNED[phase]:
                 group = 8 * slot + at_group
                 for h in range(2):
                     turn[h, group, pl.ds(s, 8, stride=8), :] = value_of(
                         s, slice(group * 8, (group + 1) * 8), slice(h * LANES, (h + 1) * LANES)
                     )
-        for slot, at_group in OWNED[core]:
+        for slot, at_group in OWNED[phase]:
             for h in range(2):
                 group = 8 * slot + at_group
                 tiles = exchange([turn[h, group, at * 8 : (at + 1) * 8] for at in range(8)])
                 for at in range(8):
                     out_ref[slot, at_group, 8 * h + at] = tiles[at]
-        emit(core)
+        emit(phase)
 
 
 def total(parts):
@@ -313,147 +324,131 @@
     return high, (value - high.astype(F32)).astype(BF16)
 
 
-def apply(t_ref, which, rows, field):
-    high, low = field
-    table_high = t_ref[2 * which, rows, :]
-    table_low = t_ref[2 * which + 1, rows, :]
-    return (
-        jnp.dot(table_high, high, preferred_element_type=F32)
-        + jnp.dot(table_high, low, preferred_element_type=F32)
-        + jnp.dot(table_low, high, preferred_element_type=F32)
-    )
+def apply(t_ref, which, field):
+    high, low = split(field)
+    width = field.shape[1]
+    if width == LANES:
+        both = jnp.concatenate([high, low], axis=1)
+        out = jnp.dot(t_ref[which], both, preferred_element_type=F32)
+        return out[:HALF, :LANES] + out[:HALF, LANES:] + out[HALF:, :LANES]
+    out = jnp.dot(t_ref[which], high, preferred_element_type=F32)
+    out = out[:HALF] + out[HALF:]
+    return out + jnp.dot(t_ref[which, :HALF], low, preferred_element_type=F32)
 
 
 def parts_of(u_ref):
-    real, imag = [], []
-    for slot in range(2):
-        tiles = u_ref[slot].reshape(MODES // 8, 2, 8, LANES)
+    out = []
+    for odd in range(2):
+        tiles = u_ref[odd].reshape(32, 2, 8, LANES)
         one, two = mix(tiles[:, 0], tiles[:, 1])
-        real.append(one.reshape(MODES, LANES))
-        imag.append(two.reshape(MODES, LANES))
-    return jnp.concatenate(real, axis=1), jnp.concatenate(imag, axis=1)
-
-
-def parts_to(out_ref, half, real, imag):
-    count = MODES // 2 // 8
-    for slot in range(2):
-        lanes = slice(slot * LANES, (slot + 1) * LANES)
-        one, two = mix(
-            real[:, lanes].reshape(count, 8, LANES), imag[:, lanes].reshape(count, 8, LANES)
-        )
-        out_ref[slot, 2 * count * half : 2 * count * (half + 1)] = jnp.stack(
-            [one, two], axis=1
-        ).reshape(2 * count, 8, LANES)
-
-
-def mode_rows(width):
-    row = lax.broadcasted_iota(jnp.int32, (MODES, width), 0)
-    mode = (row // 64 % 4 * 2 + row // 256) * 64 + row % 64
+        out.append((one.reshape(HALF, LANES), two.reshape(HALF, LANES)))
+    return out
+
+
+def parts_to(out_ref, parts):
+    for odd in range(2):
+        real, imag = parts[odd]
+        one, two = mix(real.reshape(32, 8, LANES), imag.reshape(32, 8, LANES))
+        out_ref[odd] = jnp.stack([one, two], axis=1).reshape(64, 8, LANES)
+
+
+def mode_rows(odd):
+    row = lax.broadcasted_iota(jnp.int32, (HALF, LANES), 0)
+    mode = 2 * ((row // 32 % 4 * 2 + row // 128) * 32 + row % 32) + odd
     fraction = mode.astype(F32) / MODES
     weight = jnp.where(mode == 0, 1.0 / PLANES, 2.0 / PLANES).astype(F32)
-    sign = jnp.where(mode % 2 == 0, 1.0, -1.0).astype(F32)
+    sign = jnp.where(row % 2 == 0, 1.0, -1.0).astype(F32)
     return fraction, weight, sign
 
 
-WIDTH = 2 * LANES
-ROWS = 128
-
-
-def to_planes(t_ref, cos_field, sin_field, outs):
-    for at in range(MODES // ROWS):
-        rows = slice(at * ROWS, (at + 1) * ROWS)
-        outs(rows, apply(t_ref, 0, rows, cos_field), apply(t_ref, 1, rows, sin_field))
-
-
-def first_stage(u_ref, t_ref, out_ref, planes_ref, emit):
-    real, imag = parts_of(u_ref)
-    fraction, weight, sign = mode_rows(WIDTH)
-    cos_field = split(jnp.concatenate([real, fraction * imag], axis=1))
-    sin_field = split(jnp.concatenate([imag, fraction * real], axis=1))
-    middle = jnp.sum(sign * real, axis=0, keepdims=True)
-    middle_turned = -jnp.sum(sign * fraction * imag, axis=0, keepdims=True)
-
-    def store(rows, cos, sin):
-        planes_ref[0, rows, :] = cos[:, :WIDTH] - sin[:, :WIDTH]
-        planes_ref[1, rows, :] = cos[:, :WIDTH] + sin[:, :WIDTH]
-        planes_ref[2, rows, :] = -cos[:, WIDTH:] - sin[:, WIDTH:]
-        planes_ref[3, rows, :] = sin[:, WIDTH:] - cos[:, WIDTH:]
-
-    to_planes(t_ref, cos_field, sin_field, store)
-    planes_ref[1, 0:1, :] = middle
-    planes_ref[3, 0:1, :] = middle_turned
-    low = planes_ref[0] * planes_ref[2]
-    high = planes_ref[1] * planes_ref[3]
-    first = lax.broadcasted_iota(jnp.int32, (MODES, WIDTH), 0) == 0
-    cos_side, sin_side = split(jnp.where(first, low, low + high)), split(low - high)
-    for half in range(2):
-        rows = slice(half * 256, (half + 1) * 256)
-        a = apply(t_ref, 0, rows, cos_side) + sign[rows] * high[0:1]
-        b = -apply(t_ref, 1, rows, sin_side)
-        parts_to(
-            out_ref, half, real[rows] - weight[rows] * a, imag[rows] - weight[rows] * b
+def first_row(shape):
+    return lax.broadcasted_iota(jnp.int32, shape, 0) == 0
+
+
+def to_planes(t_ref, cos_fields, sin_fields, out_ref):
+    sign = mode_rows(0)[2][:, :1]
+    cos_even, cos_odd = apply(t_ref, 0, cos_fields[0]), apply(t_ref, 1, cos_fields[1])
+    sin_even, sin_odd = apply(t_ref, 2, sin_fields[0]), apply(t_ref, 3, sin_fields[1])
+    quarter_cos = jnp.sum(sign * cos_fields[0], axis=0, keepdims=True)
+    quarter_sin = jnp.sum(sign * sin_fields[1], axis=0, keepdims=True)
+    cos, sin = cos_even + cos_odd, sin_even + sin_odd
+    out_ref[0] = cos - sin
+    out_ref[1] = cos + sin
+    cos, sin = cos_even - cos_odd, sin_even - sin_odd
+    out_ref[2] = cos + sin
+    out_ref[3] = cos - sin
+    out_ref[1, 0:1] = quarter_cos - quarter_sin
+    out_ref[3, 0:1] = quarter_cos + quarter_sin
+
+
+def from_planes(t_ref, values):
+    shape = values[0].shape
+    sign = mode_rows(0)[2][:, :1]
+    first = first_row(shape)
+    quarter, three = values[1][0:1], values[3][0:1]
+    one = values[0]
+    two = jnp.where(first, 0.0, values[1])
+    four = jnp.where(first, 0.0, values[3])
+    plus, minus = one + two, one - two
+    plus_far, minus_far = values[2] + four, values[2] - four
+    a_even = apply(t_ref, 4, plus + plus_far) + sign * (quarter + three)
+    a_odd = apply(t_ref, 5, plus - plus_far)
+    b_even = -apply(t_ref, 6, minus - minus_far)
+    b_odd = -apply(t_ref, 7, minus + minus_far) - sign * (quarter - three)
+    return (a_even, b_even), (a_odd, b_odd)
+
+
+def state_planes(parts, t_ref, out_ref):
+    cos_fields, sin_fields = [], []
+    for odd in range(2):
+        real, imag = parts[odd]
+        fraction = mode_rows(odd)[0]
+        cos_fields.append(jnp.concatenate([real, -fraction * imag], axis=1))
+        sin_fields.append(jnp.concatenate([imag, fraction * real], axis=1))
+    to_planes(t_ref, cos_fields, sin_fields, out_ref)
+
+
+def first_stage(u_ref, t_ref, planes, out_ref):
+    parts = parts_of(u_ref)
+    state_planes(parts, t_ref, planes)
+    values = [planes[at, :, :LANES] * planes[at, :, LANES:] for at in range(4)]
+    found = from_planes(t_ref, values)
+    out = []
+    for odd in range(2):
+        weight = mode_rows(odd)[1]
+        out.append(tuple(parts[odd][c] - weight * found[odd][c] for c in range(2)))
+    parts_to(out_ref, out)
+
+
+def adjoint_planes(s_ref, t_ref, out_ref):
+    parts = parts_of(s_ref)
+    weights = [mode_rows(odd)[1] for odd in range(2)]
+    to_planes(
+        t_ref,
+        [weights[odd] * parts[odd][0] for odd in range(2)],
+        [weights[odd] * parts[odd][1] for odd in range(2)],
+        out_ref,
+    )
+
+
+def finish(t_ref, s_ref, planes, adjoint, out_ref):
+    values = []
+    for at in range(4):
+        factor = adjoint[at]
+        values.append(planes[at] * jnp.concatenate([factor, factor], axis=1))
+    found = from_planes(t_ref, values)
+    parts = parts_of(s_ref)
+    out = []
+    for odd in range(2):
+        fraction = mode_rows(odd)[0]
+        a, b = found[odd]
+        out.append(
+            (
+                parts[odd][0] - a[:, LANES:] - fraction * b[:, :LANES],
+                parts[odd][1] - b[:, LANES:] + fraction * a[:, :LANES],
+            )
         )
-        emit(half)
-
-
-def finish(t_ref, s_ref, planes, adjoint, at, out_ref, emit):
-    s_real, s_imag = parts_of(s_ref)
-    fraction, _, sign = mode_rows(WIDTH)
-    first = lax.broadcasted_iota(jnp.int32, (MODES, WIDTH), 0) == 0
-    pluses, minuses, middles = [], [], []
-    for which in (2, 0):
-        low = planes[which] * adjoint[at]
-        high = planes[which + 1] * adjoint[at + 1]
-        pluses.append(jnp.where(first, low, low + high))
-        minuses.append(low - high)
-        middles.append(high[0:1])
-    cos_side = split(jnp.concatenate(pluses, axis=1))
-    sin_side = split(jnp.concatenate(minuses, axis=1))
-    for half in range(2):
-        rows = slice(half * 256, (half + 1) * 256)
-        cos = apply(t_ref, 0, rows, cos_side)
-        sin = apply(t_ref, 1, rows, sin_side)
-        a1 = cos[:, :WIDTH] + sign[rows] * middles[0]
-        a2 = cos[:, WIDTH:] + sign[rows] * middles[1]
-        b1 = -sin[:, :WIDTH]
-        b2 = -sin[:, WIDTH:]
-        parts_to(
-            out_ref,
-            half,
-            s_real[rows] - a1 - fraction[rows] * b2,
-            s_imag[rows] - b1 + fraction[rows] * a2,
-        )
-        emit(half)
-
-
-def second_stage(u_ref, s_ref, t_ref, out_ref, planes, emit):
-    real, imag = parts_of(u_ref)
-    fraction, weight, sign = mode_rows(WIDTH)
-
-    def store(rows, cos, sin):
-        planes[0, rows, :] = cos[:, :WIDTH] - sin[:, :WIDTH]
-        planes[1, rows, :] = cos[:, :WIDTH] + sin[:, :WIDTH]
-        planes[2, rows, :] = -cos[:, WIDTH:] - sin[:, WIDTH:]
-        planes[3, rows, :] = sin[:, WIDTH:] - cos[:, WIDTH:]
-
-    cos_field = split(jnp.concatenate([real, fraction * imag], axis=1))
-    sin_field = split(jnp.concatenate([imag, fraction * real], axis=1))
-    to_planes(t_ref, cos_field, sin_field, store)
-    planes[1, 0:1, :] = jnp.sum(sign * real, axis=0, keepdims=True)
-    planes[3, 0:1, :] = -jnp.sum(sign * fraction * imag, axis=0, keepdims=True)
-    finish(t_ref, s_ref, planes, planes, 4, out_ref, emit)
-
-
-def adjoint_planes(s_ref, t_ref, planes):
-    s_real, s_imag = parts_of(s_ref)
-    _, weight, sign = mode_rows(WIDTH)
-
-    def store(rows, cos, sin):
-        planes[4, rows, :] = cos - sin
-        planes[5, rows, :] = cos + sin
-
-    to_planes(t_ref, split(weight * s_real), split(weight * s_imag), store)
-    planes[5, 0:1, :] = jnp.sum(sign * weight * s_real, axis=0, keepdims=True)
+    parts_to(out_ref, out)
 
 
 COUNT = N_MODE * N_MER
@@ -551,6 +546,7 @@
     metric_in,
     u_planes,
     planes,
+    s_planes,
     blank,
     send_sems,
     recv_sems,
@@ -558,10 +554,14 @@
 ):
     mode = lax.axis_index("mode")
     mer = lax.axis_index("mer")
-    me = order_of(mode) * N_MER + mer
+    odd, eighth = mer // 8, lax.rem(mer, 8)
+    row = order_of(mode) * 8 + eighth
     mine_extra = extra(mode // 2, mer)
     double = (lax.rem(mode, 2) == 0) & (mine_extra < SPARE)
+    slots = jnp.where(double, 2, 1)
     sems = (send_sems, recv_sems)
+    mass, diag, faces, k_ref = solve_scratch[:4]
+    turn = solve_scratch[8]
     sent = []
 
     cotangent_copy = pltpu.make_async_copy(cotangent_hbm, cotangent_in, copy_sems.at[0])
@@ -579,56 +579,53 @@
         )
 
     each_other(mode, mer, (0, 1), greet)
-    native_to_tiles(state_ref, native_out.at[0], rows)
+    native_to_tiles(state_ref, native_out.at[0], rows, turn)
     pl.semaphore_wait(barrier, COUNT - 1)
+
+    def each_slot(act):
+        def body(k, _):
+            act(slots - 1 - k)
+            return 0
+
+        lax.fori_loop(0, slots, body, 0)
 
     def send_to_planes(source, target, at):
         def act(other, place):
-            send(source.at[0, other, place], target.at[0, me], other, place, sems, at)
-            if other % 2 == 0:
-                index = extra(other // 2, place)
-
-                @pl.when(index < SPARE)
-                def _():
-                    send(source.at[1, index, place], target.at[1, me], other, place, sems, at)
-
-        def emit(core):
-            each_other(mode, mer, (core,), act)
-            if core == 1:
-                target[0, me] = source[0, mode, mer]
-                target[1, me] = source[1, mine_extra, mer]
-
-        sent.append((at, 16 * GROUPS - 2, 16 * GROUPS - 1))
+            send(source.at[0, other, place], target.at[0, odd, row], other, place, sems, at)
+
+        def act_extra(other, place):
+            index = extra(other // 2, place)
+
+            @pl.when(index < SPARE)
+            def _():
+                send(source.at[1, index, place], target.at[1, odd, row], other, place, sems, at + 1)
+
+        def emit(phase):
+            if phase == 0:
+                target[1, odd, row] = source[1, mine_extra, mer]
+                each_other(mode, mer, (0,), act_extra)
+            else:
+                each_other(mode, mer, (phase - 1,), act)
+            if phase == 2:
+                target[0, odd, row] = source[0, mode, mer]
+
+        sent.append((at, COUNT - 1, COUNT - 1))
+        sent.append((at + 1, 16 * SPARE - 1, 16 * SPARE))
         return emit
 
-    def wait_planes(at):
-        wait_either(double, blank, 2 * (COUNT - 1), COUNT - 1, recv_sems.at[at])
+    def wait_planes(at, slot):
+        wait(blank, COUNT - 1, recv_sems.at[at + slot])
 
     def send_to_modes(source, target, at):
-        def act(other, place):
-            index = order_of(other) * N_MER + place
-            send(source.at[0, index], target.at[0, mode, mer], other, place, sems, at)
-
-        def act_double(other, place):
-            index = order_of(other) * N_MER + place
-            send(source.at[0, index], target.at[0, mode, mer], other, place, sems, at)
-            send(source.at[1, index], target.at[1, mine_extra, mer], other, place, sems, at)
-
-        def emit(core):
-            @pl.when(double)
-            def _():
-                each_other(mode, mer, (core,), act_double)
-
-            @pl.when(jnp.logical_not(double))
-            def _():
-                each_other(mode, mer, (core,), act)
-
-            if core == 1:
-                target[0, mode, mer] = source[0, me]
-
-                @pl.when(double)
-                def _():
-                    target[1, mine_extra, mer] = source[1, me]
+        def emit(slot):
+            group = jnp.where(slot == 1, mine_extra, mode)
+            target[slot, group, mer] = source[slot, odd, row]
+
+            def act(other, place):
+                piece = source.at[slot, place // 8, order_of(other) * 8 + lax.rem(place, 8)]
+                send(piece, target.at[slot, group, mer], other, place, sems, at)
+
+            each_other(mode, mer, (0, 1), act)
 
         sent.append((at, 2 * (COUNT - 1), COUNT - 1))
         return emit
@@ -636,98 +633,117 @@
     def wait_modes(at):
         wait_either(double, blank, 16 * GROUPS - 2, 16 * GROUPS - 1, recv_sems.at[at])
 
-    mine = pl.ds(pl.multiple_of(order_of(mode) * N_MER, N_MER), N_MER)
-    plane_in[0, 0, mine] = native_out[0, 0, mode]
-    plane_in[0, 1, mine] = native_out[0, 1, mine_extra]
+    mine = pl.ds(pl.multiple_of(order_of(mode) * 8, 8), 8)
+    plane_in[0, 0, :, mine] = native_out[0, 0, mode]
+    plane_in[0, 1, :, mine] = native_out[0, 1, mine_extra]
+
+    def send_extra_state(other):
+        index = extra(other // 2, mer)
+
+        @pl.when(index < SPARE)
+        def _():
+            send(native_out.at[0, 1, index], plane_in.at[0, 1, :, mine], other, mer, sems, 1)
 
     def send_state(other):
-        send(native_out.at[0, 0, other], plane_in.at[0, 0, mine], other, mer, sems, 0)
-        if other % 2 == 0:
-            index = extra(other // 2, mer)
-
-            @pl.when(index < SPARE)
-            def _():
-                send(native_out.at[0, 1, index], plane_in.at[0, 1, mine], other, mer, sems, 0)
-
+        send(native_out.at[0, 0, other], plane_in.at[0, 0, :, mine], other, mer, sems, 0)
+
+    each_group(mode, (0,), send_extra_state)
     each_group(mode, (0, 1), send_state)
-    sent.append((0, N_MER * (GROUPS - 2), N_MER * (GROUPS - 1)))
+    sent.append((0, N_MER * (N_MODE - 1), N_MER * (N_MODE - 1)))
+    sent.append((1, N_MER * (SPARE - 1), N_MER * SPARE))
 
     cotangent_copy.wait()
-    native_to_tiles(cotangent_in, native_out.at[1], rows)
-    mode_in[0, :, :, mer] = native_out[1, :, :, mer]
+    native_to_tiles(cotangent_in, native_out.at[1], rows, turn)
+    mode_in[0, 0, :, mer] = native_out[1, 0, :, odd, eighth]
+    mode_in[0, 1, 0:SPARE, mer] = native_out[1, 1, 0:SPARE, odd, eighth]
     metric_rows(mass_ref, inverse_ref, rows, metric_out)
     metric_in[mer] = metric_out[...]
 
-    def send_cotangent(other):
-        send(native_out.at[1, 0, :, other], mode_in.at[0, 0, :, mer], mode, other, sems, 1)
-        send(native_out.at[1, 1, 0:SPARE, other], mode_in.at[0, 1, 0:SPARE, mer], mode, other, sems, 1)
-        send(metric_out, metric_in.at[mer], mode, other, sems, 2)
+    def send_cotangent(place):
+        which, at = place // 8, lax.rem(place, 8)
+        send(native_out.at[1, 0, :, which, at], mode_in.at[0, 0, :, mer], mode, place, sems, 2)
+        send(
+            native_out.at[1, 1, 0:SPARE, which, at],
+            mode_in.at[0, 1, 0:SPARE, mer],
+            mode,
+            place,
+            sems,
+            2,
+        )
+        send(metric_out, metric_in.at[mer], mode, place, sems, 3)
 
     each_place(mer, send_cotangent)
-    sent.append((1, (N_MER - 1) * GROUPS, (N_MER - 1) * GROUPS))
-    sent.append((2, (N_MER - 1) * 4, (N_MER - 1) * 4))
-
-    mass, diag, faces, k_ref = solve_scratch[:4]
-    turn = solve_scratch[8]
+    sent.append((2, (N_MER - 1) * GROUPS, (N_MER - 1) * GROUPS))
+    sent.append((3, (N_MER - 1) * 4, (N_MER - 1) * 4))
+
     stiffness_tables(d_ref, k_ref)
-
-    wait_either(double, blank, 2 * (N_MODE - 1) * N_MER, (N_MODE - 1) * N_MER, recv_sems.at[0])
     table_copy.wait()
-    emit = send_to_modes(plane_out.at[0], mode_in.at[1], 3)
-    first_stage(plane_in.at[0], t_ref, plane_out.at[0], u_planes, emit)
-
-    wait(blank, (N_MER - 1) * 4, recv_sems.at[2])
+
+    emit_rhs = send_to_modes(plane_out.at[0], mode_in.at[1], 4)
+
+    def first(slot):
+        wait(blank, (N_MODE - 1) * N_MER, recv_sems.at[slot])
+        first_stage(plane_in.at[0, slot], t_ref, u_planes.at[slot], plane_out.at[0, slot])
+        emit_rhs(slot)
+
+    each_slot(first)
+
+    wait(blank, (N_MER - 1) * 4, recv_sems.at[3])
     metric_tables(metric_in, mode, mer, mass, diag, faces, turn)
-    wait(blank, (N_MER - 1) * GROUPS, recv_sems.at[1])
-    emit = send_to_planes(mode_out.at[0], plane_in.at[1], 4)
+    wait(blank, (N_MER - 1) * GROUPS, recv_sems.at[2])
+    emit = send_to_planes(mode_out.at[0], plane_in.at[1], 5)
     solve(mode_in.at[0], mode_out.at[0], False, True, solve_scratch, emit)
 
-    wait_modes(3)
-    emit = send_to_planes(mode_out.at[1], plane_in.at[2], 5)
+    wait_modes(4)
+    emit = send_to_planes(mode_out.at[1], plane_in.at[2], 7)
     solve(mode_in.at[1], mode_out.at[1], True, False, solve_scratch, emit)
 
-    wait_planes(4)
-    adjoint_planes(plane_in.at[1], t_ref, planes)
-    wait_planes(5)
-    emit = send_to_modes(plane_out.at[1], mode_in.at[2], 6)
-    second_stage(plane_in.at[2], plane_in.at[1], t_ref, plane_out.at[1], planes, emit)
-
-    wait_modes(6)
-    emit = send_to_planes(mode_out.at[2], plane_in.at[3], 7)
+    def multiplier(slot):
+        wait_planes(5, slot)
+        adjoint_planes(plane_in.at[1, slot], t_ref, s_planes.at[slot])
+
+    each_slot(multiplier)
+    emit_adjoint = send_to_modes(plane_out.at[1], mode_in.at[2], 9)
+
+    def second(slot):
+        wait_planes(7, slot)
+        state_planes(parts_of(plane_in.at[2, slot]), t_ref, planes)
+        finish(t_ref, plane_in.at[1, slot], planes, s_planes.at[slot], plane_out.at[1, slot])
+        emit_adjoint(slot)
+
+    each_slot(second)
+
+    wait_modes(9)
+    emit = send_to_planes(mode_out.at[2], plane_in.at[3], 10)
     solve(mode_in.at[2], mode_out.at[2], False, True, solve_scratch, emit)
 
-    wait_planes(7)
-    adjoint_planes(plane_in.at[3], t_ref, planes)
-
-
-    def send_gradient(other):
-        theirs = slice(order_of(other) * N_MER, (order_of(other) + 1) * N_MER)
-        send(plane_out.at[2, 0, theirs], native_in.at[0, mode], other, mer, sems, 8)
-
-        @pl.when(double)
-        def _():
-            send(plane_out.at[2, 1, theirs], native_in.at[1, mine_extra], other, mer, sems, 8)
-
-    def emit_gradient(core):
-        each_group(mode, (core,), send_gradient)
-
-    finish(t_ref, plane_in.at[3], u_planes, planes, 4, plane_out.at[2], emit_gradient)
-    native_in[0, mode] = plane_out[2, 0, mine]
-
-    @pl.when(double)
-    def _():
-        native_in[1, mine_extra] = plane_out[2, 1, mine]
-
-    sent.append((8, 2 * (N_MODE - 1) * N_MER, (N_MODE - 1) * N_MER))
-    wait_either(double, blank, N_MER * (GROUPS - 2), N_MER * (GROUPS - 1), recv_sems.at[8])
-    tiles_to_native(native_in, out_ref, rows)
+    def third(slot):
+        wait_planes(10, slot)
+        adjoint_planes(plane_in.at[3, slot], t_ref, s_planes.at[slot])
+        finish(
+            t_ref, plane_in.at[3, slot], u_planes.at[slot], s_planes.at[slot], plane_out.at[2, slot]
+        )
+        group = jnp.where(slot == 1, mine_extra, mode)
+        native_in[slot, group] = plane_out[2, slot, :, mine]
+
+        def send_gradient(other):
+            theirs = slice(order_of(other) * 8, (order_of(other) + 1) * 8)
+            send(plane_out.at[2, slot, :, theirs], native_in.at[slot, group], other, mer, sems, 12)
+
+        each_group(mode, (0, 1), send_gradient)
+
+    each_slot(third)
+    sent.append((12, 2 * (N_MODE - 1) * N_MER, (N_MODE - 1) * N_MER))
+    wait_either(double, blank, N_MER * (GROUPS - 2), N_MER * (GROUPS - 1), recv_sems.at[12])
+    tiles_to_native(native_in, out_ref, rows, turn)
     for at, tiles_double, tiles_single in sent:
         wait_either(double, blank, tiles_double, tiles_single, send_sems.at[at])
 
 
 def program(state, cotangent, mass, inverse, derivative, table):
     by_mode = (2, N_MODE, N_MER, 8, LANES)
-    by_plane = (2, COUNT, 8, LANES)
+    by_native = (2, N_MODE, 2, 8, 8, LANES)
+    by_plane = (2, 2, COUNT // 2, 8, LANES)
     vmem = pl.BlockSpec(memory_space=pltpu.VMEM)
     hbm = pl.BlockSpec(memory_space=pl.ANY)
 
@@ -741,22 +757,23 @@
         out_specs=vmem,
         scratch_shapes=[
             pltpu.VMEM((NODE, NODE, ELEM_DEV * LANES), F32),
-            pltpu.VMEM((4, MODES, MODES), BF16),
+            pltpu.VMEM((8, 2 * HALF, HALF), BF16),
             pltpu.SemaphoreType.DMA((2,)),
             pltpu.VMEM((PADDED * ELEM_DEV, LANES), F32),
-            scratch(2, by_mode),
-            pltpu.VMEM(by_mode, F32),
+            scratch(2, by_native),
+            pltpu.VMEM(by_native, F32),
             scratch(3, by_mode),
             scratch(3, by_mode),
             scratch(3, by_plane),
             scratch(4, by_plane),
             pltpu.VMEM((2, 16, LANES), F32),
             scratch(N_MER, (2, 16, LANES)),
-            pltpu.VMEM((4, MODES, WIDTH), F32),
-            pltpu.VMEM((6, MODES, WIDTH), F32),
+            scratch(2, (4, HALF, 2 * LANES)),
+            scratch(4, (HALF, 2 * LANES)),
+            scratch(2, (4, HALF, LANES)),
             pltpu.VMEM((2 * COUNT, 8, LANES), F32),
-            pltpu.SemaphoreType.DMA((9,)),
-            pltpu.SemaphoreType.DMA((9,)),
+            pltpu.SemaphoreType.DMA((13,)),
+            pltpu.SemaphoreType.DMA((13,)),
             *SOLVE_SCRATCH,
         ],
         compiler_params=pltpu.CompilerParams(

time: 104 us -> 104 us (level); the launches traced: 104 us -> 103 us
    pallas_call x1, Pallas kernels: 101 us -> 100 us  [program(): pl.pallas_call(program_kernel, out_shape=jax.ShapeDtypeStruct((NODE, NODE...]
where the time goes in v4:
time: 104 us; the launch traced here: 103 us
  Pallas kernels  100 us (96%)
  local copies, waits for them, and re-layouts  2.39 us (2%)
    pallas_call x1, Pallas kernels, program(): pl.pallas_call(program_kernel, out_shape=jax.ShapeDtypeStruct((NODE, NODE...  100 us
    unnamed x1, local copies, waits for them, and re-layouts  2.39 us

profile of v4, /device:TPU:1, one launch (start us, length us, event | category | flops | bytes accessed | tf_op | source)
XLA Modules:
  0.0 102.6 jit_solution(14942461645322419673)
XLA Ops:
  0.0 100.2 %program.1 = f32[9,9,2048]{2,1,0:T(8,128)} custom-call(f32[9,9,2048]{2,1,0:T(8,128)} %state_ref.1, f32[9,9,2048]{2,1,0:T(8,128)} %cotangent_hbm.1, f32[9,9,16]{2,1,0:T(8,128)} %mass_ref.1, f32[9,9,16]{2,1,0:T(8,128)} %inverse_ref.1, f32[9,9]{1,0:T(8,128)} %d_ref.1, bf16[8,512,256]{2,1,0:T(8,128)(2,1)} %constant.2.clone.t_hbm), custom_call_target="tpu_custom_call" | custom-call | tf_op jit(solution)/shard_map/program/pallas_call | solution.py:753
  100.2 2.4 %copy.8 = f32[9,9,2048]{2,1,0:T(8,128)} copy(f32[9,9,2048]{2,1,0:T(8,128)} %program.1) | data formatting | bytes 1327104

commit v5 on v4

--- a/solution.py
+++ b/solution.py
@@ -231,75 +231,75 @@
 
 
 def solve(b_ref, out_ref, weigh_in, weigh_out, scratch, emit):
-    mass, diag, faces, k_ref, x, r, p, q, turn = scratch
+    mass, diag, faces, k_ref, r, p, q, alphas, turn = scratch
     load_tiles(b_ref, turn, mass if weigh_in else None, r)
-    norms = []
+    norms = tuple(total(fold(r[n] * r[n]) + fold(r[n + 4] * r[n + 4])) for n in range(4))
+    p[ITERS - 1] = jnp.zeros_like(p[ITERS - 1])
+    empty = jnp.zeros((8, ELEMENTS), F32)
+
+    def operate(sweep, before, n, beta, norm):
+        curve = None
+        for s in (n, n + 4):
+            now = r[s] + beta * p[before, s]
+            p[sweep, s] = now
+            high = now.astype(BF16).astype(F32)
+            halves = jnp.concatenate([high, now - high], axis=0).astype(BF16)
+            image = jnp.dot(k_ref[...], halves, preferred_element_type=F32)
+            ahead = pltpu.roll(now[: PADDED - 8], ELEMENTS - RADIAL, 1)
+            behind = pltpu.roll(now[8:], RADIAL, 1)
+            image = (
+                image[:PADDED]
+                + image[PADDED:]
+                + diag[n] * now
+                - faces[0] * jnp.concatenate([empty, ahead], axis=0)
+                - faces[1] * jnp.concatenate([behind, empty], axis=0)
+            )
+            outward = pltpu.roll(now[:16], ELEMENTS - 1, 1)
+            inward = pltpu.roll(now[72:], 1, 1)
+            image = jnp.concatenate(
+                [
+                    image[:16] - faces[3, :16] * inward,
+                    image[16:72],
+                    image[72:] - faces[2, 72:] * outward,
+                ],
+                axis=0,
+            )
+            q[s] = image
+            part = fold(now * image)
+            curve = part if curve is None else curve + part
+        alpha = norm / total(curve)
+        alphas[sweep * 4 + n] = alpha
+        return alpha
+
+    def reduce(n, alpha):
+        part = None
+        for s in (n, n + 4):
+            value = r[s] - alpha * q[s]
+            r[s] = value
+            add = fold(value * value)
+            part = add if part is None else part + add
+        return total(part)
+
+    def sweep_body(sweep, carry):
+        norms, betas = carry
+        before = lax.rem(sweep + ITERS - 1, ITERS)
+        step, after = [None] * 4, [None] * 4
+        for n in range(5):
+            if n < 4:
+                step[n] = operate(sweep, before, n, betas[n], norms[n])
+            if n > 0:
+                after[n - 1] = reduce(n - 1, step[n - 1])
+        return tuple(after), tuple(after[n] / norms[n] for n in range(4))
+
+    none = (jnp.zeros((1, ELEMENTS), F32),) * 4
+    norms, betas = lax.fori_loop(0, ITERS - 1, sweep_body, (norms, none))
     for n in range(4):
-        norms.append(total(fold(r[n] * r[n]) + fold(r[n + 4] * r[n + 4])))
-    x[...] = jnp.zeros_like(x)
-    p[...] = jnp.zeros_like(p)
-    empty = jnp.zeros((8, ELEMENTS), F32)
-    edge = jnp.zeros((16, ELEMENTS), F32)
-
-    def sweep_body(sweep, carry):
-        norms, alphas, betas = carry
-        curves = []
-        for n in range(4):
-            curve = None
-            for s in (n, n + 4):
-                old = p[s]
-                x[s] = x[s] + alphas[n] * old
-                now = r[s] + betas[n] * old
-                p[s] = now
-                high = now.astype(BF16).astype(F32)
-                halves = jnp.concatenate([high, now - high], axis=0).astype(BF16)
-                image = jnp.dot(k_ref[...], halves, preferred_element_type=F32)
-                ahead = pltpu.roll(now[: PADDED - 8], ELEMENTS - RADIAL, 1)
-                behind = pltpu.roll(now[8:], RADIAL, 1)
-                image = (
-                    image[:PADDED]
-                    + image[PADDED:]
-                    + diag[n] * now
-                    - faces[0] * jnp.concatenate([empty, ahead], axis=0)
-                    - faces[1] * jnp.concatenate([behind, empty], axis=0)
-                )
-                outward = pltpu.roll(now[:16], ELEMENTS - 1, 1)
-                inward = pltpu.roll(now[72:], 1, 1)
-                image = jnp.concatenate(
-                    [
-                        image[:16] - faces[3, :16] * inward,
-                        image[16:72],
-                        image[72:] - faces[2, 72:] * outward,
-                    ],
-                    axis=0,
-                )
-                q[s] = image
-                part = fold(now * image)
-                curve = part if curve is None else curve + part
-            curves.append(total(curve))
-        alphas = [norms[n] / curves[n] for n in range(4)]
-
-        def update():
-            after = []
-            for n in range(4):
-                part = None
-                for s in (n, n + 4):
-                    value = r[s] - alphas[n] * q[s]
-                    r[s] = value
-                    add = fold(value * value)
-                    part = add if part is None else part + add
-                after.append(total(part))
-            return after
-
-        after = lax.cond(sweep < ITERS - 1, update, lambda: norms)
-        betas = [after[n] / norms[n] for n in range(4)]
-        return after, alphas, betas
-
-    none = [jnp.zeros((1, ELEMENTS), F32)] * 4
-    norms, alphas, betas = lax.fori_loop(0, ITERS, sweep_body, (norms, none, none))
+        operate(ITERS - 1, ITERS - 2, n, betas[n], norms[n])
 
     def value_of(s, rows, lanes):
-        value = x[s, rows, lanes] + alphas[s % 4][:, lanes] * p[s, rows, lanes]
+        value = alphas[s % 4, :, lanes] * p[0, s, rows, lanes]
+        for sweep in range(1, ITERS):
+            value = value + alphas[sweep * 4 + s % 4, :, lanes] * p[sweep, s, rows, lanes]
         return value * mass[rows, lanes] if weigh_out else value
 
     store_tiles(value_of, turn, out_ref, emit)
@@ -312,9 +312,9 @@
     pltpu.VMEM((4, PADDED, ELEMENTS), F32),
     pltpu.VMEM((2 * PADDED, 2 * PADDED), BF16),
     FIELD,
+    pltpu.VMEM((ITERS, 8, PADDED, ELEMENTS), F32),
     FIELD,
-    FIELD,
-    FIELD,
+    pltpu.VMEM((ITERS * 4, 1, ELEMENTS), F32),
     pltpu.VMEM((2, GROUPS, 64, LANES), F32),
 ]
 
@@ -482,8 +482,9 @@
 
 
 def place_at(mer, k):
-    y = lax.rem(lax.rem(mer, 4) + lax.rem(k, 4), 4)
-    z = lax.rem(mer // 4 + k // 4, 4)
+    step = lax.rem(7 * k, N_MER)
+    y = lax.rem(lax.rem(mer, 4) + lax.rem(step, 4), 4)
+    z = lax.rem(mer // 4 + step // 4, 4)
     return z * 4 + y
 
 
@@ -492,14 +493,21 @@
     return lax.rem(x + 4 - turn, 4)
 
 
+def groups_on(mode, core):
+    x = mode // 2
+    return [2 * lax.rem(x + step, 4) + core for step in (1, 3, 2, 0)]
+
+
 def each_group(mode, cores, act):
     for core in cores:
-        for x in range(4):
-            other = 2 * x + core
-
-            @pl.when(mode != other)
-            def _(other=other):
-                act(other)
+        one, two, three, own = groups_on(mode, core)
+        act(one, core)
+        act(two, core)
+        act(three, core)
+
+        @pl.when(lax.rem(mode, 2) != core)
+        def _(own=own, core=core):
+            act(own, core)
 
 
 def each_place(mer, act):
@@ -511,17 +519,18 @@
 
 
 def each_other(mode, mer, cores, act):
+    groups = [(other, core) for core in cores for other in groups_on(mode, core)]
+
     def body(place):
-        for core in cores:
-            for x in range(4):
-                act(2 * x + core, place)
+        for other, core in groups:
+            act(other, core, place)
 
     each_place(mer, body)
-    each_group(mode, cores, lambda other: act(other, mer))
+    each_group(mode, cores, lambda other, core: act(other, core, mer))
 
 
 def order_of(mode):
-    return lax.rem(mode, 2) * 4 + mode // 2 if not isinstance(mode, int) else mode % 2 * 4 + mode // 2
+    return lax.rem(mode, 2) * 4 + mode // 2
 
 
 def program_kernel(
@@ -570,7 +579,7 @@
     table_copy.start()
     barrier = pltpu.get_barrier_semaphore()
 
-    def greet(other, place):
+    def greet(other, core, place):
         pl.semaphore_signal(
             barrier,
             inc=1,
@@ -590,10 +599,10 @@
         lax.fori_loop(0, slots, body, 0)
 
     def send_to_planes(source, target, at):
-        def act(other, place):
+        def act(other, core, place):
             send(source.at[0, other, place], target.at[0, odd, row], other, place, sems, at)
 
-        def act_extra(other, place):
+        def act_extra(other, core, place):
             index = extra(other // 2, place)
 
             @pl.when(index < SPARE)
@@ -621,7 +630,7 @@
             group = jnp.where(slot == 1, mine_extra, mode)
             target[slot, group, mer] = source[slot, odd, row]
 
-            def act(other, place):
+            def act(other, core, place):
                 piece = source.at[slot, place // 8, order_of(other) * 8 + lax.rem(place, 8)]
                 send(piece, target.at[slot, group, mer], other, place, sems, at)
 
@@ -637,14 +646,14 @@
     plane_in[0, 0, :, mine] = native_out[0, 0, mode]
     plane_in[0, 1, :, mine] = native_out[0, 1, mine_extra]
 
-    def send_extra_state(other):
+    def send_extra_state(other, core):
         index = extra(other // 2, mer)
 
         @pl.when(index < SPARE)
         def _():
             send(native_out.at[0, 1, index], plane_in.at[0, 1, :, mine], other, mer, sems, 1)
 
-    def send_state(other):
+    def send_state(other, core):
         send(native_out.at[0, 0, other], plane_in.at[0, 0, :, mine], other, mer, sems, 0)
 
     each_group(mode, (0,), send_extra_state)
@@ -726,8 +735,8 @@
         group = jnp.where(slot == 1, mine_extra, mode)
         native_in[slot, group] = plane_out[2, slot, :, mine]
 
-        def send_gradient(other):
-            theirs = slice(order_of(other) * 8, (order_of(other) + 1) * 8)
+        def send_gradient(other, core):
+            theirs = pl.ds(pl.multiple_of(order_of(other) * 8, 8), 8)
             send(plane_out.at[2, slot, :, theirs], native_in.at[slot, group], other, mer, sems, 12)
 
         each_group(mode, (0, 1), send_gradient)

time: 104 us -> 102 us (0.981); the launches traced: 103 us -> 102 us
  no operation moved by 1% of the time
where the time goes in v5:
time: 102 us
  Pallas kernels  99.4 us (97%)
  local copies, waits for them, and re-layouts  2.39 us (2%)
    pallas_call x1, Pallas kernels, program(): pl.pallas_call(program_kernel, out_shape=jax.ShapeDtypeStruct((NODE, NODE...  99.4 us
    unnamed x1, local copies, waits for them, and re-layouts  2.39 us

profile of v5, /device:TPU:1, one launch (start us, length us, event | category | flops | bytes accessed | tf_op | source)
XLA Modules:
  0.0 101.8 jit_solution(17548218497453302094)
XLA Ops:
  0.0 99.4 %program.1 = f32[9,9,2048]{2,1,0:T(8,128)} custom-call(f32[9,9,2048]{2,1,0:T(8,128)} %state_ref.1, f32[9,9,2048]{2,1,0:T(8,128)} %cotangent_hbm.1, f32[9,9,16]{2,1,0:T(8,128)} %mass_ref.1, f32[9,9,16]{2,1,0:T(8,128)} %inverse_ref.1, f32[9,9]{1,0:T(8,128)} %d_ref.1, bf16[8,512,256]{2,1,0:T(8,128)(2,1)} %constant.2.clone.t_hbm), custom_call_target="tpu_custom_call" | custom-call | tf_op jit(solution)/shard_map/program/pallas_call | solution.py:762
  99.4 2.4 %copy.8 = f32[9,9,2048]{2,1,0:T(8,128)} copy(f32[9,9,2048]{2,1,0:T(8,128)} %program.1) | data formatting | bytes 1327104

commit v6 on v5

--- a/solution.py
+++ b/solution.py
@@ -90,20 +90,56 @@
             out_ref[group // 8, group % 8, odd] = jnp.stack([one, two], axis=1).reshape(8, 8, LANES)
 
 
-def tiles_to_native(t_ref, out_ref, rows, turn):
+def tiles_to_native_kernel(t_hbm, out_hbm, tiles_in, rows, turn, native, in_sems, out_sems):
+    loads = [
+        pltpu.make_async_copy(t_hbm.at[group], tiles_in.at[group], in_sems.at[group])
+        for group in range(GROUPS)
+    ]
+    stores = [
+        pltpu.make_async_copy(native.at[i], out_hbm.at[i], out_sems.at[i]) for i in range(NODE)
+    ]
+    for load in loads:
+        load.start()
+    done = 0
     for group in range(GROUPS):
+        loads[group].wait()
         for odd in range(2):
-            tiles = t_ref[group // 8, group % 8, odd].reshape(4, 2, 8, LANES)
+            tiles = tiles_in[group, odd].reshape(4, 2, 8, LANES)
             real, imag = mix(tiles[:, 0], tiles[:, 1])
             turn[0, group, pl.ds(odd, 32, stride=2), :] = real.reshape(32, LANES)
             turn[1, group, pl.ds(odd, 32, stride=2), :] = imag.reshape(32, LANES)
         both = jnp.concatenate([turn[0, group], turn[1, group]], axis=0)
         rows[group * LANES : (group + 1) * LANES, :] = both.T
-    for i in range(NODE):
-        for e in range(ELEM_DEV):
-            out_ref[i, :, e * LANES : (e + 1) * LANES] = rows[
-                pl.ds(i * NODE * ELEM_DEV + e, NODE, stride=ELEM_DEV), :
-            ]
+        while done < NODE and (done + 1) * NODE <= (group + 1) * 8:
+            for e in range(ELEM_DEV):
+                native[done, :, e * LANES : (e + 1) * LANES] = rows[
+                    pl.ds(done * NODE * ELEM_DEV + e, NODE, stride=ELEM_DEV), :
+                ]
+            stores[done].start()
+            done += 1
+    for store in stores:
+        store.wait()
+
+
+def tiles_to_native(tiles):
+    hbm = pl.BlockSpec(memory_space=pltpu.HBM)
+    shape = (NODE, NODE, ELEM_DEV * LANES)
+    return pl.pallas_call(
+        tiles_to_native_kernel,
+        out_shape=jax.ShapeDtypeStruct(shape, F32),
+        in_specs=[hbm],
+        out_specs=hbm,
+        scratch_shapes=[
+            pltpu.VMEM((GROUPS, 2, 8, 8, LANES), F32),
+            pltpu.VMEM((PADDED * ELEM_DEV, LANES), F32),
+            pltpu.VMEM((2, GROUPS, 64, LANES), F32),
+            pltpu.VMEM(shape, F32),
+            pltpu.SemaphoreType.DMA((GROUPS,)),
+            pltpu.SemaphoreType.DMA((NODE,)),
+        ],
+        compiler_params=pltpu.CompilerParams(vmem_limit_bytes=62 << 20),
+        name="tiles_to_native",
+    )(tiles)
 
 
 def stiffness_tables(d_ref, k_ref):
@@ -180,13 +216,25 @@
         diag[n] = mass[...] * (1.0 + AZIMUTH_WEIGHT * fraction * fraction * values) + count
 
 
+def owner_of(extra_group, place):
+    return 2 * ((extra_group + place % 4 + place // 4) % 4)
+
+
 CHUNKS = ((0, 0, 3), (0, 3, 6), (0, 6, 8), (1, 0, 3))
 
 
-def load_tiles(b_ref, turn, weight, out):
+def load_tiles(b_ref, turn, weight, out, by_owner):
     for slot, start, stop in CHUNKS:
         for h in range(2):
-            tiles = exchange([b_ref[slot, start:stop, 8 * h + at] for at in range(8)])
+            tiles = []
+            for place in range(8 * h, 8 * h + 8):
+                if slot and by_owner:
+                    tiles.append(
+                        jnp.stack([b_ref[1, owner_of(at, place), place] for at in range(start, stop)])
+                    )
+                else:
+                    tiles.append(b_ref[slot, start:stop, place])
+            tiles = exchange(tiles)
             for at in range(8):
                 turn[h, 8 * slot + start : 8 * slot + stop, at * 8 : (at + 1) * 8] = tiles[at]
     for s in range(8):
@@ -200,25 +248,30 @@
                 out[s, rows, lanes] = value
 
 
-OWNED = (((1, 0), (1, 1), (1, 2)), ((0, 0), (0, 2), (0, 4), (0, 6)), ((0, 1), (0, 3), (0, 5), (0, 7)))
+OWNED = (
+    ((1, 0), (1, 1), (1, 2), (0, 0), (0, 2), (0, 4), (0, 6)),
+    ((0, 1), (0, 3), (0, 5), (0, 7)),
+)
 
 
 def store_tiles(value_of, turn, out_ref, emit):
-    for phase in range(3):
+    for core in range(2):
         for s in range(8):
-            for slot, at_group in OWNED[phase]:
+            for slot, at_group in OWNED[core]:
                 group = 8 * slot + at_group
                 for h in range(2):
                     turn[h, group, pl.ds(s, 8, stride=8), :] = value_of(
                         s, slice(group * 8, (group + 1) * 8), slice(h * LANES, (h + 1) * LANES)
                     )
-        for slot, at_group in OWNED[phase]:
+        for slot, at_group in OWNED[core]:
             for h in range(2):
                 group = 8 * slot + at_group
                 tiles = exchange([turn[h, group, at * 8 : (at + 1) * 8] for at in range(8)])
                 for at in range(8):
-                    out_ref[slot, at_group, 8 * h + at] = tiles[at]
-        emit(phase)
+                    place = 8 * h + at
+                    owner = owner_of(at_group, place) if slot else at_group
+                    out_ref[slot, owner, place] = tiles[at]
+        emit(core)
 
 
 def total(parts):
@@ -230,9 +283,9 @@
     return jnp.sum(value.reshape(GROUPS, 8, ELEMENTS), axis=0)
 
 
-def solve(b_ref, out_ref, weigh_in, weigh_out, scratch, emit):
+def solve(b_ref, out_ref, weigh_in, weigh_out, by_owner, scratch, emit):
     mass, diag, faces, k_ref, r, p, q, alphas, turn = scratch
-    load_tiles(b_ref, turn, mass if weigh_in else None, r)
+    load_tiles(b_ref, turn, mass if weigh_in else None, r, by_owner)
     norms = tuple(total(fold(r[n] * r[n]) + fold(r[n + 4] * r[n + 4])) for n in range(4))
     p[ITERS - 1] = jnp.zeros_like(p[ITERS - 1])
     empty = jnp.zeros((8, ELEMENTS), F32)
@@ -540,7 +593,7 @@
     inverse_ref,
     d_ref,
     t_hbm,
-    out_ref,
+    out_hbm,
     cotangent_in,
     t_ref,
     copy_sems,
@@ -556,6 +609,7 @@
     u_planes,
     planes,
     s_planes,
+    ready,
     blank,
     send_sems,
     recv_sems,
@@ -579,17 +633,19 @@
     table_copy.start()
     barrier = pltpu.get_barrier_semaphore()
 
-    def greet(other, core, place):
+    def greet(semaphore, other, place):
         pl.semaphore_signal(
-            barrier,
+            semaphore,
             inc=1,
             device_id={"mode": other, "mer": place},
             device_id_type=pl.DeviceIdType.MESH,
         )
 
-    each_other(mode, mer, (0, 1), greet)
+    each_group(mode, (0, 1), lambda other, core: greet(barrier, other, mer))
+    each_place(mer, lambda place: greet(barrier, mode, place))
     native_to_tiles(state_ref, native_out.at[0], rows, turn)
-    pl.semaphore_wait(barrier, COUNT - 1)
+    pl.semaphore_wait(barrier, N_MODE - 1 + N_MER - 1)
+    each_group(mode, (0, 1), lambda other, core: greet(ready, other, mer))
 
     def each_slot(act):
         def body(k, _):
@@ -600,44 +656,53 @@
 
     def send_to_planes(source, target, at):
         def act(other, core, place):
-            send(source.at[0, other, place], target.at[0, odd, row], other, place, sems, at)
-
-        def act_extra(other, core, place):
-            index = extra(other // 2, place)
-
-            @pl.when(index < SPARE)
+            def single():
+                send(source.at[0, other, place], target.at[0, odd, row], other, place, sems, at)
+
+            if core == 1:
+                single()
+                return
+            owns_two = extra(other // 2, place) < SPARE
+            pl.when(jnp.logical_not(owns_two))(single)
+
+            @pl.when(owns_two)
             def _():
-                send(source.at[1, index, place], target.at[1, odd, row], other, place, sems, at + 1)
-
-        def emit(phase):
-            if phase == 0:
-                target[1, odd, row] = source[1, mine_extra, mer]
-                each_other(mode, mer, (0,), act_extra)
-            else:
-                each_other(mode, mer, (phase - 1,), act)
-            if phase == 2:
-                target[0, odd, row] = source[0, mode, mer]
-
-        sent.append((at, COUNT - 1, COUNT - 1))
-        sent.append((at + 1, 16 * SPARE - 1, 16 * SPARE))
+                send(source.at[:, other, place], target.at[:, odd, row], other, place, sems, at)
+
+        def emit(core):
+            each_other(mode, mer, (core,), act)
+            if core == 1:
+                target[:, odd, row] = source[:, mode, mer]
+
+        sent.append((at, 16 * GROUPS - 2, 16 * GROUPS - 1))
         return emit
 
-    def wait_planes(at, slot):
-        wait(blank, COUNT - 1, recv_sems.at[at + slot])
+    def wait_planes(at):
+        wait_either(double, blank, 2 * (COUNT - 1), COUNT - 1, recv_sems.at[at])
 
     def send_to_modes(source, target, at):
-        def emit(slot):
-            group = jnp.where(slot == 1, mine_extra, mode)
-            target[slot, group, mer] = source[slot, odd, row]
-
-            def act(other, core, place):
-                piece = source.at[slot, place // 8, order_of(other) * 8 + lax.rem(place, 8)]
-                send(piece, target.at[slot, group, mer], other, place, sems, at)
-
+        target[0, mode, mer] = source[0, odd, row]
+
+        def act(other, core, place):
+            index = order_of(other) * 8 + lax.rem(place, 8)
+            piece = source.at[0, place // 8, index]
+            send(piece, target.at[0, mode, mer], other, place, sems, at)
+
+        def act_double(other, core, place):
+            index = order_of(other) * 8 + lax.rem(place, 8)
+            piece = source.at[:, place // 8, index]
+            send(piece, target.at[:, mode, mer], other, place, sems, at)
+
+        @pl.when(double)
+        def _():
+            target[1, mode, mer] = source[1, odd, row]
+            each_other(mode, mer, (0, 1), act_double)
+
+        @pl.when(jnp.logical_not(double))
+        def _():
             each_other(mode, mer, (0, 1), act)
 
         sent.append((at, 2 * (COUNT - 1), COUNT - 1))
-        return emit
 
     def wait_modes(at):
         wait_either(double, blank, 16 * GROUPS - 2, 16 * GROUPS - 1, recv_sems.at[at])
@@ -651,15 +716,14 @@
 
         @pl.when(index < SPARE)
         def _():
-            send(native_out.at[0, 1, index], plane_in.at[0, 1, :, mine], other, mer, sems, 1)
+            send(native_out.at[0, 1, index], plane_in.at[0, 1, :, mine], other, mer, sems, 0)
 
     def send_state(other, core):
         send(native_out.at[0, 0, other], plane_in.at[0, 0, :, mine], other, mer, sems, 0)
 
     each_group(mode, (0,), send_extra_state)
     each_group(mode, (0, 1), send_state)
-    sent.append((0, N_MER * (N_MODE - 1), N_MER * (N_MODE - 1)))
-    sent.append((1, N_MER * (SPARE - 1), N_MER * SPARE))
+    sent.append((0, N_MER * (GROUPS - 2), N_MER * (GROUPS - 1)))
 
     cotangent_copy.wait()
     native_to_tiles(cotangent_in, native_out.at[1], rows, turn)
@@ -688,65 +752,75 @@
     stiffness_tables(d_ref, k_ref)
     table_copy.wait()
 
-    emit_rhs = send_to_modes(plane_out.at[0], mode_in.at[1], 4)
+    wait_either(double, blank, 2 * (N_MODE - 1) * N_MER, (N_MODE - 1) * N_MER, recv_sems.at[0])
 
     def first(slot):
-        wait(blank, (N_MODE - 1) * N_MER, recv_sems.at[slot])
         first_stage(plane_in.at[0, slot], t_ref, u_planes.at[slot], plane_out.at[0, slot])
-        emit_rhs(slot)
 
     each_slot(first)
+    pl.semaphore_wait(ready, N_MODE - 1)
+    send_to_modes(plane_out.at[0], mode_in.at[1], 4)
 
     wait(blank, (N_MER - 1) * 4, recv_sems.at[3])
     metric_tables(metric_in, mode, mer, mass, diag, faces, turn)
     wait(blank, (N_MER - 1) * GROUPS, recv_sems.at[2])
     emit = send_to_planes(mode_out.at[0], plane_in.at[1], 5)
-    solve(mode_in.at[0], mode_out.at[0], False, True, solve_scratch, emit)
+    solve(mode_in.at[0], mode_out.at[0], False, True, False, solve_scratch, emit)
 
     wait_modes(4)
-    emit = send_to_planes(mode_out.at[1], plane_in.at[2], 7)
-    solve(mode_in.at[1], mode_out.at[1], True, False, solve_scratch, emit)
+    emit = send_to_planes(mode_out.at[1], plane_in.at[2], 6)
+    solve(mode_in.at[1], mode_out.at[1], True, False, True, solve_scratch, emit)
 
     def multiplier(slot):
-        wait_planes(5, slot)
         adjoint_planes(plane_in.at[1, slot], t_ref, s_planes.at[slot])
 
+    wait_planes(5)
     each_slot(multiplier)
-    emit_adjoint = send_to_modes(plane_out.at[1], mode_in.at[2], 9)
 
     def second(slot):
-        wait_planes(7, slot)
         state_planes(parts_of(plane_in.at[2, slot]), t_ref, planes)
         finish(t_ref, plane_in.at[1, slot], planes, s_planes.at[slot], plane_out.at[1, slot])
-        emit_adjoint(slot)
-
+
+    wait_planes(6)
     each_slot(second)
-
-    wait_modes(9)
-    emit = send_to_planes(mode_out.at[2], plane_in.at[3], 10)
-    solve(mode_in.at[2], mode_out.at[2], False, True, solve_scratch, emit)
+    send_to_modes(plane_out.at[1], mode_in.at[2], 7)
+
+    wait_modes(7)
+    emit = send_to_planes(mode_out.at[2], plane_in.at[3], 8)
+    solve(mode_in.at[2], mode_out.at[2], False, True, True, solve_scratch, emit)
 
     def third(slot):
-        wait_planes(10, slot)
         adjoint_planes(plane_in.at[3, slot], t_ref, s_planes.at[slot])
         finish(
             t_ref, plane_in.at[3, slot], u_planes.at[slot], s_planes.at[slot], plane_out.at[2, slot]
         )
-        group = jnp.where(slot == 1, mine_extra, mode)
-        native_in[slot, group] = plane_out[2, slot, :, mine]
+        native_in[slot, mode] = plane_out[2, slot, :, mine]
 
         def send_gradient(other, core):
             theirs = pl.ds(pl.multiple_of(order_of(other) * 8, 8), 8)
-            send(plane_out.at[2, slot, :, theirs], native_in.at[slot, group], other, mer, sems, 12)
+            send(plane_out.at[2, slot, :, theirs], native_in.at[slot, mode], other, mer, sems, 9)
 
         each_group(mode, (0, 1), send_gradient)
 
+    wait_planes(8)
     each_slot(third)
-    sent.append((12, 2 * (N_MODE - 1) * N_MER, (N_MODE - 1) * N_MER))
-    wait_either(double, blank, N_MER * (GROUPS - 2), N_MER * (GROUPS - 1), recv_sems.at[12])
-    tiles_to_native(native_in, out_ref, rows, turn)
+    sent.append((9, 2 * (N_MODE - 1) * N_MER, (N_MODE - 1) * N_MER))
+    wait_either(double, blank, N_MER * (GROUPS - 2), N_MER * (GROUPS - 1), recv_sems.at[9])
+    turned = lax.rem(lax.rem(mer, 4) + mer // 4, 4)
+    copies = [pltpu.make_async_copy(native_in.at[0], out_hbm.at[0:N_MODE], copy_sems.at[2])]
+    for index in range(SPARE):
+        owner = 2 * lax.rem(index + turned, 4)
+        copies.append(
+            pltpu.make_async_copy(
+                native_in.at[1, owner], out_hbm.at[N_MODE + index], copy_sems.at[3 + index]
+            )
+        )
+    for copy in copies:
+        copy.start()
     for at, tiles_double, tiles_single in sent:
         wait_either(double, blank, tiles_double, tiles_single, send_sems.at[at])
+    for copy in copies:
+        copy.wait()
 
 
 def program(state, cotangent, mass, inverse, derivative, table):
@@ -761,13 +835,13 @@
 
     return pl.pallas_call(
         program_kernel,
-        out_shape=jax.ShapeDtypeStruct((NODE, NODE, ELEM_DEV * LANES), F32),
+        out_shape=jax.ShapeDtypeStruct((GROUPS, 2, 8, 8, LANES), F32),
         in_specs=[vmem, hbm, vmem, vmem, vmem, hbm],
-        out_specs=vmem,
+        out_specs=hbm,
         scratch_shapes=[
             pltpu.VMEM((NODE, NODE, ELEM_DEV * LANES), F32),
             pltpu.VMEM((8, 2 * HALF, HALF), BF16),
-            pltpu.SemaphoreType.DMA((2,)),
+            pltpu.SemaphoreType.DMA((6,)),
             pltpu.VMEM((PADDED * ELEM_DEV, LANES), F32),
             scratch(2, by_native),
             pltpu.VMEM(by_native, F32),
@@ -780,9 +854,10 @@
             scratch(2, (4, HALF, 2 * LANES)),
             scratch(4, (HALF, 2 * LANES)),
             scratch(2, (4, HALF, LANES)),
+            pltpu.SemaphoreType.REGULAR,
             pltpu.VMEM((2 * COUNT, 8, LANES), F32),
-            pltpu.SemaphoreType.DMA((13,)),
-            pltpu.SemaphoreType.DMA((13,)),
+            pltpu.SemaphoreType.DMA((10,)),
+            pltpu.SemaphoreType.DMA((10,)),
             *SOLVE_SCRATCH,
         ],
         compiler_params=pltpu.CompilerParams(
@@ -794,7 +869,7 @@
 
 def shards(cotangent, checkpoint, mass, inv_radius_sq, derivative):
     table = jnp.asarray(tables())
-    return program(checkpoint, cotangent, mass, inv_radius_sq, derivative, table)
+    return tiles_to_native(program(checkpoint, cotangent, mass, inv_radius_sq, derivative, table))
 
 
 def solution(mesh):

time: 102 us -> 102 us (level)
  Pallas kernels: 99.4 us -> 102 us
  local copies, waits for them, and re-layouts: 2.39 us -> 0 us
    pallas_call x1 -> x2, Pallas kernels: 99.4 us -> 102 us  [the longest x1 99 us: program(): pl.pallas_call(program_kernel, out_shape=jax.ShapeDtypeStruct((GROUPS, 2,...]
    unnamed x1 -> x0, local copies, waits for them, and re-layouts: 2.39 us -> none
where the time goes in v6:
time: 102 us
  Pallas kernels  102 us (100%)
    pallas_call x1, Pallas kernels, program(): pl.pallas_call(program_kernel, out_shape=jax.ShapeDtypeStruct((GROUPS, 2,...  99 us
    pallas_call x1, Pallas kernels, tiles_to_native(): pl.pallas_call(tiles_to_native_kernel, out_shape=jax.ShapeDtypeStruct(sha...  2.93 us

profile of v6, /device:TPU:1, one launch (start us, length us, event | category | flops | bytes accessed | tf_op | source)
XLA Modules:
  0.0 102.1 jit_solution(7747830148595197437)
XLA Ops:
  0.0 99.0 %program.1.t_hbm = f32[11,2,8,8,128]{4,3,2,1,0:T(8,128)} custom-call(f32[9,9,2048]{2,1,0:T(8,128)} %state_ref.1, f32[9,9,2048]{2,1,0:T(8,128)} %cotangent_hbm.1, f32[9,9,16]{2,1,0:T(8,128)} %mass_ref.1, f32[9,9,16]{2,1,0:T(8,128)} %inverse_ref.1, f32[9,9]{1,0:T(8,128)} %d_ref.1, bf16[8,512,256]{2,1,0:T(8,128)(2,1)} %constant.2.clone.t_hbm), custom_call_target="tpu_custom_call" | custom-call | tf_op jit(solution)/shard_map/program/pallas_call | solution.py:836
  99.1 2.9 %tiles_to_native.1 = f32[9,9,2048]{2,1,0:T(8,128)} custom-call(f32[11,2,8,8,128]{4,3,2,1,0:T(8,128)} %program.1.t_hbm), custom_call_target="tpu_custom_call" | custom-call | tf_op jit(solution)/shard_map/tiles_to_native/pallas_call | solution.py:127

commit v7 on v6

--- a/solution.py
+++ b/solution.py
@@ -47,11 +47,11 @@
 
 def mix(first, second):
     shape = first.shape
-    low = lax.broadcasted_iota(jnp.int32, shape, len(shape) - 2) % 8 < 4
     axis = len(shape) - 2
+    low = lax.broadcasted_iota(jnp.int32, shape, axis) % 4 < 2
     return (
-        jnp.where(low, first, pltpu.roll(second, 4, axis)),
-        jnp.where(low, pltpu.roll(first, 4, axis), second),
+        jnp.where(low, first, pltpu.roll(second, 2, axis)),
+        jnp.where(low, pltpu.roll(first, 6, axis), second),
     )
 
 
@@ -91,18 +91,10 @@
 
 
 def tiles_to_native_kernel(t_hbm, out_hbm, tiles_in, rows, turn, native, in_sems, out_sems):
-    loads = [
-        pltpu.make_async_copy(t_hbm.at[group], tiles_in.at[group], in_sems.at[group])
-        for group in range(GROUPS)
-    ]
-    stores = [
-        pltpu.make_async_copy(native.at[i], out_hbm.at[i], out_sems.at[i]) for i in range(NODE)
-    ]
-    for load in loads:
-        load.start()
-    done = 0
+    load = pltpu.make_async_copy(t_hbm, tiles_in, in_sems.at[0])
+    load.start()
+    load.wait()
     for group in range(GROUPS):
-        loads[group].wait()
         for odd in range(2):
             tiles = tiles_in[group, odd].reshape(4, 2, 8, LANES)
             real, imag = mix(tiles[:, 0], tiles[:, 1])
@@ -110,15 +102,14 @@
             turn[1, group, pl.ds(odd, 32, stride=2), :] = imag.reshape(32, LANES)
         both = jnp.concatenate([turn[0, group], turn[1, group]], axis=0)
         rows[group * LANES : (group + 1) * LANES, :] = both.T
-        while done < NODE and (done + 1) * NODE <= (group + 1) * 8:
-            for e in range(ELEM_DEV):
-                native[done, :, e * LANES : (e + 1) * LANES] = rows[
-                    pl.ds(done * NODE * ELEM_DEV + e, NODE, stride=ELEM_DEV), :
-                ]
-            stores[done].start()
-            done += 1
-    for store in stores:
-        store.wait()
+    for i in range(NODE):
+        for e in range(ELEM_DEV):
+            native[i, :, e * LANES : (e + 1) * LANES] = rows[
+                pl.ds(i * NODE * ELEM_DEV + e, NODE, stride=ELEM_DEV), :
+            ]
+    store = pltpu.make_async_copy(native, out_hbm, out_sems.at[0])
+    store.start()
+    store.wait()
 
 
 def tiles_to_native(tiles):
@@ -134,8 +125,8 @@
             pltpu.VMEM((PADDED * ELEM_DEV, LANES), F32),
             pltpu.VMEM((2, GROUPS, 64, LANES), F32),
             pltpu.VMEM(shape, F32),
-            pltpu.SemaphoreType.DMA((GROUPS,)),
-            pltpu.SemaphoreType.DMA((NODE,)),
+            pltpu.SemaphoreType.DMA((1,)),
+            pltpu.SemaphoreType.DMA((1,)),
         ],
         compiler_params=pltpu.CompilerParams(vmem_limit_bytes=62 << 20),
         name="tiles_to_native",
@@ -211,7 +202,8 @@
     count = marks[0] + marks[1] + marks[2] + marks[3]
     values = inverse[...]
     for n in range(4):
-        number = mode_group * 64 + lax.rem(place, 8) * 8 + 2 * n + place // 8
+        offset = lax.rem(place, 8) // 2 * 8 + lax.rem(place, 2) * 2 + n // 2 * 4 + n % 2
+        number = mode_group * 64 + 2 * offset + place // 8
         fraction = number.astype(F32) / MODES
         diag[n] = mass[...] * (1.0 + AZIMUTH_WEIGHT * fraction * fraction * values) + count
 
@@ -220,58 +212,58 @@
     return 2 * ((extra_group + place % 4 + place // 4) % 4)
 
 
-CHUNKS = ((0, 0, 3), (0, 3, 6), (0, 6, 8), (1, 0, 3))
-
-
-def load_tiles(b_ref, turn, weight, out, by_owner):
-    for slot, start, stop in CHUNKS:
+PAIRS = (((0, 2), (4, 6), (8, 9), (10,)), ((1, 3), (5, 7)))
+
+
+def load_tiles(b_ref, half, turn, weight, out, by_owner):
+    rows = slice(4 * half, 4 * half + 4)
+
+    def piece(group, place):
+        if group < 8:
+            return b_ref[0, group, place, rows]
+        return b_ref[1, owner_of(group - 8, place) if by_owner else group - 8, place, rows]
+
+    for at_pair, pair in enumerate(PAIRS[0] + PAIRS[1]):
         for h in range(2):
             tiles = []
             for place in range(8 * h, 8 * h + 8):
-                if slot and by_owner:
-                    tiles.append(
-                        jnp.stack([b_ref[1, owner_of(at, place), place] for at in range(start, stop)])
-                    )
-                else:
-                    tiles.append(b_ref[slot, start:stop, place])
+                tiles.append(
+                    jnp.concatenate([piece(pair[0], place), piece(pair[-1], place)], axis=0)
+                )
             tiles = exchange(tiles)
             for at in range(8):
-                turn[h, 8 * slot + start : 8 * slot + stop, at * 8 : (at + 1) * 8] = tiles[at]
-    for s in range(8):
-        for h in range(2):
+                turn[h, at_pair, at * 8 : (at + 1) * 8] = tiles[at]
             lanes = slice(h * LANES, (h + 1) * LANES)
-            for group in range(GROUPS):
-                rows = slice(group * 8, (group + 1) * 8)
-                value = turn[h, group, pl.ds(s, 8, stride=8), :]
-                if weight is not None:
-                    value = value * weight[rows, lanes]
-                out[s, rows, lanes] = value
-
-
-OWNED = (
-    ((1, 0), (1, 1), (1, 2), (0, 0), (0, 2), (0, 4), (0, 6)),
-    ((0, 1), (0, 3), (0, 5), (0, 7)),
-)
-
-
-def store_tiles(value_of, turn, out_ref, emit):
+            for which, group in enumerate(pair):
+                nodes = slice(group * 8, (group + 1) * 8)
+                for s in range(4):
+                    value = turn[h, at_pair, pl.ds(4 * which + s, 8, stride=8), :]
+                    if weight is not None:
+                        value = value * weight[nodes, lanes]
+                    out[4 * half + s, nodes, lanes] = value
+
+
+def store_tiles(value_of, half, turn, out_ref, emit):
+    rows = slice(4 * half, 4 * half + 4)
     for core in range(2):
-        for s in range(8):
-            for slot, at_group in OWNED[core]:
-                group = 8 * slot + at_group
-                for h in range(2):
-                    turn[h, group, pl.ds(s, 8, stride=8), :] = value_of(
-                        s, slice(group * 8, (group + 1) * 8), slice(h * LANES, (h + 1) * LANES)
-                    )
-        for slot, at_group in OWNED[core]:
+        for at_pair, pair in enumerate(PAIRS[core]):
             for h in range(2):
-                group = 8 * slot + at_group
-                tiles = exchange([turn[h, group, at * 8 : (at + 1) * 8] for at in range(8)])
-                for at in range(8):
-                    place = 8 * h + at
-                    owner = owner_of(at_group, place) if slot else at_group
-                    out_ref[slot, owner, place] = tiles[at]
-        emit(core)
+                lanes = slice(h * LANES, (h + 1) * LANES)
+                for which, group in enumerate(pair):
+                    for s in range(4):
+                        turn[h, 4 * core + at_pair, pl.ds(4 * which + s, 8, stride=8), :] = value_of(
+                            4 * half + s, slice(group * 8, (group + 1) * 8), lanes
+                        )
+                tiles = [turn[h, 4 * core + at_pair, at * 8 : (at + 1) * 8] for at in range(8)]
+                tiles = exchange(tiles)
+                for which, group in enumerate(pair):
+                    for at in range(8):
+                        place = 8 * h + at
+                        owner = owner_of(group - 8, place) if group >= 8 else group
+                        out_ref[group // 8, owner, place, rows] = tiles[at][
+                            4 * which : 4 * which + 4
+                        ]
+        emit(core, half)
 
 
 def total(parts):
@@ -283,16 +275,27 @@
     return jnp.sum(value.reshape(GROUPS, 8, ELEMENTS), axis=0)
 
 
-def solve(b_ref, out_ref, weigh_in, weigh_out, by_owner, scratch, emit):
+def solve(b_ref, out_ref, half, weigh_in, weigh_out, by_owner, scratch, emit):
     mass, diag, faces, k_ref, r, p, q, alphas, turn = scratch
-    load_tiles(b_ref, turn, mass if weigh_in else None, r, by_owner)
-    norms = tuple(total(fold(r[n] * r[n]) + fold(r[n + 4] * r[n + 4])) for n in range(4))
-    p[ITERS - 1] = jnp.zeros_like(p[ITERS - 1])
+    load_tiles(b_ref, half, turn, mass if weigh_in else None, r, by_owner)
+    modes = (2 * half, 2 * half + 1)
+
+    def rows_of(n):
+        return (4 * half + n % 2, 4 * half + 2 + n % 2)
+
+    def square(n):
+        one, two = rows_of(n)
+        return total(fold(r[one] * r[one]) + fold(r[two] * r[two]))
+
+    norms = tuple(square(n) for n in modes)
+    for n in modes:
+        for s in rows_of(n):
+            p[ITERS - 1, s] = jnp.zeros((PADDED, ELEMENTS), F32)
     empty = jnp.zeros((8, ELEMENTS), F32)
 
     def operate(sweep, before, n, beta, norm):
         curve = None
-        for s in (n, n + 4):
+        for s in rows_of(n):
             now = r[s] + beta * p[before, s]
             p[sweep, s] = now
             high = now.astype(BF16).astype(F32)
@@ -326,7 +329,7 @@
 
     def reduce(n, alpha):
         part = None
-        for s in (n, n + 4):
+        for s in rows_of(n):
             value = r[s] - alpha * q[s]
             r[s] = value
             add = fold(value * value)
@@ -336,26 +339,23 @@
     def sweep_body(sweep, carry):
         norms, betas = carry
         before = lax.rem(sweep + ITERS - 1, ITERS)
-        step, after = [None] * 4, [None] * 4
-        for n in range(5):
-            if n < 4:
-                step[n] = operate(sweep, before, n, betas[n], norms[n])
-            if n > 0:
-                after[n - 1] = reduce(n - 1, step[n - 1])
-        return tuple(after), tuple(after[n] / norms[n] for n in range(4))
-
-    none = (jnp.zeros((1, ELEMENTS), F32),) * 4
+        step = [operate(sweep, before, n, betas[n % 2], norms[n % 2]) for n in modes]
+        after = tuple(reduce(n, step[n % 2]) for n in modes)
+        return after, tuple(after[n] / norms[n] for n in range(2))
+
+    none = (jnp.zeros((1, ELEMENTS), F32),) * 2
     norms, betas = lax.fori_loop(0, ITERS - 1, sweep_body, (norms, none))
-    for n in range(4):
-        operate(ITERS - 1, ITERS - 2, n, betas[n], norms[n])
+    for n in modes:
+        operate(ITERS - 1, ITERS - 2, n, betas[n % 2], norms[n % 2])
 
     def value_of(s, rows, lanes):
-        value = alphas[s % 4, :, lanes] * p[0, s, rows, lanes]
+        n = s // 4 * 2 + s % 2
+        value = alphas[n, :, lanes] * p[0, s, rows, lanes]
         for sweep in range(1, ITERS):
-            value = value + alphas[sweep * 4 + s % 4, :, lanes] * p[sweep, s, rows, lanes]
+            value = value + alphas[sweep * 4 + n, :, lanes] * p[sweep, s, rows, lanes]
         return value * mass[rows, lanes] if weigh_out else value
 
-    store_tiles(value_of, turn, out_ref, emit)
+    store_tiles(value_of, half, turn, out_ref, emit)
 
 
 FIELD = pltpu.VMEM((8, PADDED, ELEMENTS), F32)
@@ -519,19 +519,19 @@
     ).start()
 
 
-def wait(blank, tiles, sem):
-    whole = blank.at[pl.ds(0, tiles)]
+def wait(blank, tiles, sem, rows=8):
+    whole = blank.at[pl.ds(0, tiles), pl.ds(0, rows)]
     pltpu.make_async_copy(whole, whole, sem).wait()
 
 
-def wait_either(double, blank, tiles_double, tiles_single, sem):
+def wait_either(double, blank, tiles_double, tiles_single, sem, rows=8):
     @pl.when(double)
     def _():
-        wait(blank, tiles_double, sem)
+        wait(blank, tiles_double, sem, rows)
 
     @pl.when(jnp.logical_not(double))
     def _():
-        wait(blank, tiles_single, sem)
+        wait(blank, tiles_single, sem, rows)
 
 
 def place_at(mer, k):
@@ -655,57 +655,85 @@
         lax.fori_loop(0, slots, body, 0)
 
     def send_to_planes(source, target, at):
-        def act(other, core, place):
-            def single():
-                send(source.at[0, other, place], target.at[0, odd, row], other, place, sems, at)
-
-            if core == 1:
-                single()
-                return
-            owns_two = extra(other // 2, place) < SPARE
-            pl.when(jnp.logical_not(owns_two))(single)
-
-            @pl.when(owns_two)
-            def _():
-                send(source.at[:, other, place], target.at[:, odd, row], other, place, sems, at)
-
-        def emit(core):
+        def emit(core, half):
+            rows = pl.ds(4 * half, 4)
+
+            def act(other, core, place):
+                def single():
+                    send(
+                        source.at[0, other, place, rows],
+                        target.at[0, odd, row, rows],
+                        other,
+                        place,
+                        sems,
+                        at + half,
+                    )
+
+                if core == 1:
+                    single()
+                    return
+                owns_two = extra(other // 2, place) < SPARE
+                pl.when(jnp.logical_not(owns_two))(single)
+
+                @pl.when(owns_two)
+                def _():
+                    send(
+                        source.at[:, other, place, rows],
+                        target.at[:, odd, row, rows],
+                        other,
+                        place,
+                        sems,
+                        at + half,
+                    )
+
             each_other(mode, mer, (core,), act)
             if core == 1:
-                target[:, odd, row] = source[:, mode, mer]
-
-        sent.append((at, 16 * GROUPS - 2, 16 * GROUPS - 1))
+                target[:, odd, row, 4 * half : 4 * half + 4] = source[
+                    :, mode, mer, 4 * half : 4 * half + 4
+                ]
+
+        for half in range(2):
+            sent.append((at + half, 16 * GROUPS - 2, 16 * GROUPS - 1, 4))
         return emit
 
     def wait_planes(at):
-        wait_either(double, blank, 2 * (COUNT - 1), COUNT - 1, recv_sems.at[at])
+        for half in range(2):
+            wait_either(double, blank, 2 * (COUNT - 1), COUNT - 1, recv_sems.at[at + half], 4)
 
     def send_to_modes(source, target, at):
         target[0, mode, mer] = source[0, odd, row]
-
-        def act(other, core, place):
-            index = order_of(other) * 8 + lax.rem(place, 8)
-            piece = source.at[0, place // 8, index]
-            send(piece, target.at[0, mode, mer], other, place, sems, at)
-
-        def act_double(other, core, place):
-            index = order_of(other) * 8 + lax.rem(place, 8)
-            piece = source.at[:, place // 8, index]
-            send(piece, target.at[:, mode, mer], other, place, sems, at)
 
         @pl.when(double)
         def _():
             target[1, mode, mer] = source[1, odd, row]
-            each_other(mode, mer, (0, 1), act_double)
-
-        @pl.when(jnp.logical_not(double))
-        def _():
-            each_other(mode, mer, (0, 1), act)
-
-        sent.append((at, 2 * (COUNT - 1), COUNT - 1))
-
-    def wait_modes(at):
-        wait_either(double, blank, 16 * GROUPS - 2, 16 * GROUPS - 1, recv_sems.at[at])
+
+        for half in range(2):
+            rows = pl.ds(4 * half, 4)
+
+            def act(other, core, place, rows=rows, half=half):
+                index = order_of(other) * 8 + lax.rem(place, 8)
+                piece = source.at[0, place // 8, index, rows]
+                send(piece, target.at[0, mode, mer, rows], other, place, sems, at + half)
+
+            def act_double(other, core, place, rows=rows, half=half):
+                index = order_of(other) * 8 + lax.rem(place, 8)
+                piece = source.at[:, place // 8, index, rows]
+                send(piece, target.at[:, mode, mer, rows], other, place, sems, at + half)
+
+            @pl.when(double)
+            def _(act_double=act_double):
+                each_other(mode, mer, (0, 1), act_double)
+
+            @pl.when(jnp.logical_not(double))
+            def _(act=act):
+                each_other(mode, mer, (0, 1), act)
+
+            sent.append((at + half, 2 * (COUNT - 1), COUNT - 1, 4))
+
+    def wait_modes(at, half):
+        wait_either(
+            double, blank, 16 * GROUPS - 2, 16 * GROUPS - 1, recv_sems.at[at + half], 4
+        )
 
     mine = pl.ds(pl.multiple_of(order_of(mode) * 8, 8), 8)
     plane_in[0, 0, :, mine] = native_out[0, 0, mode]
@@ -723,7 +751,7 @@
 
     each_group(mode, (0,), send_extra_state)
     each_group(mode, (0, 1), send_state)
-    sent.append((0, N_MER * (GROUPS - 2), N_MER * (GROUPS - 1)))
+    sent.append((0, N_MER * (GROUPS - 2), N_MER * (GROUPS - 1), 8))
 
     cotangent_copy.wait()
     native_to_tiles(cotangent_in, native_out.at[1], rows, turn)
@@ -746,8 +774,8 @@
         send(metric_out, metric_in.at[mer], mode, place, sems, 3)
 
     each_place(mer, send_cotangent)
-    sent.append((2, (N_MER - 1) * GROUPS, (N_MER - 1) * GROUPS))
-    sent.append((3, (N_MER - 1) * 4, (N_MER - 1) * 4))
+    sent.append((2, (N_MER - 1) * GROUPS, (N_MER - 1) * GROUPS, 8))
+    sent.append((3, (N_MER - 1) * 4, (N_MER - 1) * 4, 8))
 
     stiffness_tables(d_ref, k_ref)
     table_copy.wait()
@@ -764,30 +792,33 @@
     wait(blank, (N_MER - 1) * 4, recv_sems.at[3])
     metric_tables(metric_in, mode, mer, mass, diag, faces, turn)
     wait(blank, (N_MER - 1) * GROUPS, recv_sems.at[2])
-    emit = send_to_planes(mode_out.at[0], plane_in.at[1], 5)
-    solve(mode_in.at[0], mode_out.at[0], False, True, False, solve_scratch, emit)
-
-    wait_modes(4)
-    emit = send_to_planes(mode_out.at[1], plane_in.at[2], 6)
-    solve(mode_in.at[1], mode_out.at[1], True, False, True, solve_scratch, emit)
+    emit = send_to_planes(mode_out.at[0], plane_in.at[1], 6)
+    for half in range(2):
+        solve(mode_in.at[0], mode_out.at[0], half, False, True, False, solve_scratch, emit)
+
+    emit = send_to_planes(mode_out.at[1], plane_in.at[2], 8)
+    for half in range(2):
+        wait_modes(4, half)
+        solve(mode_in.at[1], mode_out.at[1], half, True, False, True, solve_scratch, emit)
 
     def multiplier(slot):
         adjoint_planes(plane_in.at[1, slot], t_ref, s_planes.at[slot])
 
-    wait_planes(5)
+    wait_planes(6)
     each_slot(multiplier)
 
     def second(slot):
         state_planes(parts_of(plane_in.at[2, slot]), t_ref, planes)
         finish(t_ref, plane_in.at[1, slot], planes, s_planes.at[slot], plane_out.at[1, slot])
 
-    wait_planes(6)
+    wait_planes(8)
     each_slot(second)
-    send_to_modes(plane_out.at[1], mode_in.at[2], 7)
-
-    wait_modes(7)
-    emit = send_to_planes(mode_out.at[2], plane_in.at[3], 8)
-    solve(mode_in.at[2], mode_out.at[2], False, True, True, solve_scratch, emit)
+    send_to_modes(plane_out.at[1], mode_in.at[2], 10)
+
+    emit = send_to_planes(mode_out.at[2], plane_in.at[3], 12)
+    for half in range(2):
+        wait_modes(10, half)
+        solve(mode_in.at[2], mode_out.at[2], half, False, True, True, solve_scratch, emit)
 
     def third(slot):
         adjoint_planes(plane_in.at[3, slot], t_ref, s_planes.at[slot])
@@ -798,14 +829,14 @@
 
         def send_gradient(other, core):
             theirs = pl.ds(pl.multiple_of(order_of(other) * 8, 8), 8)
-            send(plane_out.at[2, slot, :, theirs], native_in.at[slot, mode], other, mer, sems, 9)
+            send(plane_out.at[2, slot, :, theirs], native_in.at[slot, mode], other, mer, sems, 14)
 
         each_group(mode, (0, 1), send_gradient)
 
-    wait_planes(8)
+    wait_planes(12)
     each_slot(third)
-    sent.append((9, 2 * (N_MODE - 1) * N_MER, (N_MODE - 1) * N_MER))
-    wait_either(double, blank, N_MER * (GROUPS - 2), N_MER * (GROUPS - 1), recv_sems.at[9])
+    sent.append((14, 2 * (N_MODE - 1) * N_MER, (N_MODE - 1) * N_MER, 8))
+    wait_either(double, blank, N_MER * (GROUPS - 2), N_MER * (GROUPS - 1), recv_sems.at[14])
     turned = lax.rem(lax.rem(mer, 4) + mer // 4, 4)
     copies = [pltpu.make_async_copy(native_in.at[0], out_hbm.at[0:N_MODE], copy_sems.at[2])]
     for index in range(SPARE):
@@ -817,8 +848,8 @@
         )
     for copy in copies:
         copy.start()
-    for at, tiles_double, tiles_single in sent:
-        wait_either(double, blank, tiles_double, tiles_single, send_sems.at[at])
+    for at, tiles_double, tiles_single, rows_each in sent:
+        wait_either(double, blank, tiles_double, tiles_single, send_sems.at[at], rows_each)
     for copy in copies:
         copy.wait()
 
@@ -856,8 +887,8 @@
             scratch(2, (4, HALF, LANES)),
             pltpu.SemaphoreType.REGULAR,
             pltpu.VMEM((2 * COUNT, 8, LANES), F32),
-            pltpu.SemaphoreType.DMA((10,)),
-            pltpu.SemaphoreType.DMA((10,)),
+            pltpu.SemaphoreType.DMA((15,)),
+            pltpu.SemaphoreType.DMA((15,)),
             *SOLVE_SCRATCH,
         ],
         compiler_params=pltpu.CompilerParams(

time: 102 us -> 101 us (level)
  no operation moved by 1% of the time
where the time goes in v7:
time: 101 us
  Pallas kernels  101 us (100%)
    pallas_call x1, Pallas kernels, program(): pl.pallas_call(program_kernel, out_shape=jax.ShapeDtypeStruct((GROUPS, 2,...  98.2 us
    pallas_call x1, Pallas kernels, tiles_to_native(): pl.pallas_call(tiles_to_native_kernel, out_shape=jax.ShapeDtypeStruct(sha...  2.53 us

profile of v7, /device:TPU:1, one launch (start us, length us, event | category | flops | bytes accessed | tf_op | source)
XLA Modules:
  0.0 100.9 jit_solution(47070738030842340)
XLA Ops:
  0.0 98.2 %program.1.t_hbm = f32[11,2,8,8,128]{4,3,2,1,0:T(8,128)} custom-call(f32[9,9,2048]{2,1,0:T(8,128)} %state_ref.1, f32[9,9,2048]{2,1,0:T(8,128)} %cotangent_hbm.1, f32[9,9,16]{2,1,0:T(8,128)} %mass_ref.1, f32[9,9,16]{2,1,0:T(8,128)} %inverse_ref.1, f32[9,9]{1,0:T(8,128)} %d_ref.1, bf16[8,512,256]{2,1,0:T(8,128)(2,1)} %constant.2.clone.t_hbm), custom_call_target="tpu_custom_call" | custom-call | tf_op jit(solution)/shard_map/program/pallas_call | solution.py:867
  98.2 2.5 %tiles_to_native.1 = f32[9,9,2048]{2,1,0:T(8,128)} custom-call(f32[11,2,8,8,128]{4,3,2,1,0:T(8,128)} %program.1.t_hbm), custom_call_target="tpu_custom_call" | custom-call | tf_op jit(solution)/shard_map/tiles_to_native/pallas_call | solution.py:118

commit v8 on v7

--- a/solution.py
+++ b/solution.py
@@ -178,16 +178,7 @@
         out_ref[kind, GROUPS:] = jnp.zeros((16 - GROUPS, LANES), F32)
 
 
-def metric_tables(m_ref, mode_group, place, mass, diag, faces, turn):
-    inverse = diag.at[0]
-    for kind, out in ((0, mass), (1, inverse)):
-        for h in range(2):
-            rows = exchange([m_ref[8 * h + at, kind] for at in range(8)])
-            for at in range(8):
-                for group in range(GROUPS):
-                    turn[h, group, at : at + 1] = rows[at][group : group + 1]
-            for group in range(GROUPS):
-                out[group * 8 : (group + 1) * 8, h * LANES : (h + 1) * LANES] = turn[h, group, 0:8]
+def face_tables(faces, count):
     shape = (PADDED, ELEMENTS)
     node = lax.broadcasted_iota(jnp.int32, shape, 0)
     element = lax.broadcasted_iota(jnp.int32, shape, 1)
@@ -199,13 +190,25 @@
     marks = [jnp.where(mark, 1.0, 0.0).astype(F32) for mark in (upper, lower, outer, inner)]
     for at in range(4):
         faces[at] = marks[at]
-    count = marks[0] + marks[1] + marks[2] + marks[3]
+    count[...] = marks[0] + marks[1] + marks[2] + marks[3]
+
+
+def metric_tables(m_ref, mode_group, place, mass, diag, count, turn):
+    inverse = diag.at[0]
+    for kind, out in ((0, mass), (1, inverse)):
+        for h in range(2):
+            rows = exchange([m_ref[8 * h + at, kind] for at in range(8)])
+            for at in range(8):
+                for group in range(GROUPS):
+                    turn[h, group, at : at + 1] = rows[at][group : group + 1]
+            for group in range(GROUPS):
+                out[group * 8 : (group + 1) * 8, h * LANES : (h + 1) * LANES] = turn[h, group, 0:8]
     values = inverse[...]
     for n in range(4):
         offset = lax.rem(place, 8) // 2 * 8 + lax.rem(place, 2) * 2 + n // 2 * 4 + n % 2
         number = mode_group * 64 + 2 * offset + place // 8
         fraction = number.astype(F32) / MODES
-        diag[n] = mass[...] * (1.0 + AZIMUTH_WEIGHT * fraction * fraction * values) + count
+        diag[n] = mass[...] * (1.0 + AZIMUTH_WEIGHT * fraction * fraction * values) + count[...]
 
 
 def owner_of(extra_group, place):
@@ -277,27 +280,28 @@
 
 def solve(b_ref, out_ref, half, weigh_in, weigh_out, by_owner, scratch, emit):
     mass, diag, faces, k_ref, r, p, q, alphas, turn = scratch
-    load_tiles(b_ref, half, turn, mass if weigh_in else None, r, by_owner)
+    load_tiles(b_ref, half, turn, mass if weigh_in else None, p.at[0], by_owner)
     modes = (2 * half, 2 * half + 1)
-
-    def rows_of(n):
-        return (4 * half + n % 2, 4 * half + 2 + n % 2)
-
-    def square(n):
-        one, two = rows_of(n)
-        return total(fold(r[one] * r[one]) + fold(r[two] * r[two]))
-
-    norms = tuple(square(n) for n in modes)
-    for n in modes:
-        for s in rows_of(n):
-            p[ITERS - 1, s] = jnp.zeros((PADDED, ELEMENTS), F32)
     empty = jnp.zeros((8, ELEMENTS), F32)
 
-    def operate(sweep, before, n, beta, norm):
-        curve = None
-        for s in rows_of(n):
-            now = r[s] + beta * p[before, s]
-            p[sweep, s] = now
+    def add(whole, part):
+        part = fold(part)
+        return part if whole is None else whole + part
+
+    def operate(sweep, n, alpha, beta):
+        last = sweep == ITERS - 1
+        norm = curve = bend = None
+        for s in (4 * half + n % 2, 4 * half + 2 + n % 2):
+            if sweep == 0:
+                rest = now = p[0, s]
+            else:
+                before = p[sweep - 1, s]
+                rest = (before if sweep == 1 else r[s]) - alpha * q[s]
+                now = rest + beta * before
+                p[sweep, s] = now
+                if not last:
+                    r[s] = rest
+            norm = add(norm, rest * rest)
             high = now.astype(BF16).astype(F32)
             halves = jnp.concatenate([high, now - high], axis=0).astype(BF16)
             image = jnp.dot(k_ref[...], halves, preferred_element_type=F32)
@@ -320,33 +324,20 @@
                 ],
                 axis=0,
             )
-            q[s] = image
-            part = fold(now * image)
-            curve = part if curve is None else curve + part
-        alpha = norm / total(curve)
+            curve = add(curve, now * image)
+            if not last:
+                q[s] = image
+                bend = add(bend, image * image)
+        curve = total(curve)
+        alpha = total(norm) / curve
         alphas[sweep * 4 + n] = alpha
-        return alpha
-
-    def reduce(n, alpha):
-        part = None
-        for s in rows_of(n):
-            value = r[s] - alpha * q[s]
-            r[s] = value
-            add = fold(value * value)
-            part = add if part is None else part + add
-        return total(part)
-
-    def sweep_body(sweep, carry):
-        norms, betas = carry
-        before = lax.rem(sweep + ITERS - 1, ITERS)
-        step = [operate(sweep, before, n, betas[n % 2], norms[n % 2]) for n in modes]
-        after = tuple(reduce(n, step[n % 2]) for n in modes)
-        return after, tuple(after[n] / norms[n] for n in range(2))
-
-    none = (jnp.zeros((1, ELEMENTS), F32),) * 2
-    norms, betas = lax.fori_loop(0, ITERS - 1, sweep_body, (norms, none))
-    for n in modes:
-        operate(ITERS - 1, ITERS - 2, n, betas[n % 2], norms[n % 2])
+        if last:
+            return alpha, None
+        return alpha, jnp.maximum(alpha * (total(bend) / curve) - 1.0, 0.0)
+
+    steps = [(None, None)] * 2
+    for sweep in range(ITERS):
+        steps = [operate(sweep, n, *steps[n % 2]) for n in modes]
 
     def value_of(s, rows, lanes):
         n = s // 4 * 2 + s % 2
@@ -405,21 +396,26 @@
         out_ref[odd] = jnp.stack([one, two], axis=1).reshape(64, 8, LANES)
 
 
-def mode_rows(odd):
+def column_tables(c_ref):
     row = lax.broadcasted_iota(jnp.int32, (HALF, LANES), 0)
-    mode = 2 * ((row // 32 % 4 * 2 + row // 128) * 32 + row % 32) + odd
-    fraction = mode.astype(F32) / MODES
-    weight = jnp.where(mode == 0, 1.0 / PLANES, 2.0 / PLANES).astype(F32)
-    sign = jnp.where(row % 2 == 0, 1.0, -1.0).astype(F32)
-    return fraction, weight, sign
-
-
-def first_row(shape):
-    return lax.broadcasted_iota(jnp.int32, shape, 0) == 0
-
-
-def to_planes(t_ref, cos_fields, sin_fields, out_ref):
-    sign = mode_rows(0)[2][:, :1]
+    for odd in range(2):
+        mode = 2 * ((row // 32 % 4 * 2 + row // 128) * 32 + row % 32) + odd
+        c_ref[odd] = mode.astype(F32) / MODES
+        c_ref[2 + odd] = jnp.where(mode == 0, 1.0 / PLANES, 2.0 / PLANES).astype(F32)
+    c_ref[4] = jnp.where(row % 2 == 0, 1.0, -1.0).astype(F32)
+
+
+def signs(c_ref, width):
+    return jnp.concatenate([c_ref[4]] * (width // LANES), axis=1)
+
+
+def without_first(value):
+    head = lax.broadcasted_iota(jnp.int32, (8, value.shape[1]), 0) == 0
+    return jnp.concatenate([jnp.where(head, 0.0, value[:8]), value[8:]], axis=0)
+
+
+def to_planes(t_ref, c_ref, cos_fields, sin_fields, out_ref):
+    sign = signs(c_ref, cos_fields[0].shape[1])
     cos_even, cos_odd = apply(t_ref, 0, cos_fields[0]), apply(t_ref, 1, cos_fields[1])
     sin_even, sin_odd = apply(t_ref, 2, sin_fields[0]), apply(t_ref, 3, sin_fields[1])
     quarter_cos = jnp.sum(sign * cos_fields[0], axis=0, keepdims=True)
@@ -434,14 +430,11 @@
     out_ref[3, 0:1] = quarter_cos + quarter_sin
 
 
-def from_planes(t_ref, values):
-    shape = values[0].shape
-    sign = mode_rows(0)[2][:, :1]
-    first = first_row(shape)
+def from_planes(t_ref, c_ref, values):
+    sign = signs(c_ref, values[0].shape[1])
     quarter, three = values[1][0:1], values[3][0:1]
     one = values[0]
-    two = jnp.where(first, 0.0, values[1])
-    four = jnp.where(first, 0.0, values[3])
+    two, four = without_first(values[1]), without_first(values[3])
     plus, minus = one + two, one - two
     plus_far, minus_far = values[2] + four, values[2] - four
     a_even = apply(t_ref, 4, plus + plus_far) + sign * (quarter + three)
@@ -451,49 +444,50 @@
     return (a_even, b_even), (a_odd, b_odd)
 
 
-def state_planes(parts, t_ref, out_ref):
+def state_planes(parts, t_ref, c_ref, out_ref):
     cos_fields, sin_fields = [], []
     for odd in range(2):
         real, imag = parts[odd]
-        fraction = mode_rows(odd)[0]
+        fraction = c_ref[odd]
         cos_fields.append(jnp.concatenate([real, -fraction * imag], axis=1))
         sin_fields.append(jnp.concatenate([imag, fraction * real], axis=1))
-    to_planes(t_ref, cos_fields, sin_fields, out_ref)
-
-
-def first_stage(u_ref, t_ref, planes, out_ref):
+    to_planes(t_ref, c_ref, cos_fields, sin_fields, out_ref)
+
+
+def first_stage(u_ref, t_ref, c_ref, planes, out_ref):
     parts = parts_of(u_ref)
-    state_planes(parts, t_ref, planes)
+    state_planes(parts, t_ref, c_ref, planes)
     values = [planes[at, :, :LANES] * planes[at, :, LANES:] for at in range(4)]
-    found = from_planes(t_ref, values)
+    found = from_planes(t_ref, c_ref, values)
     out = []
     for odd in range(2):
-        weight = mode_rows(odd)[1]
+        weight = c_ref[2 + odd]
         out.append(tuple(parts[odd][c] - weight * found[odd][c] for c in range(2)))
     parts_to(out_ref, out)
 
 
-def adjoint_planes(s_ref, t_ref, out_ref):
+def adjoint_planes(s_ref, t_ref, c_ref, out_ref):
     parts = parts_of(s_ref)
-    weights = [mode_rows(odd)[1] for odd in range(2)]
+    weights = [c_ref[2 + odd] for odd in range(2)]
     to_planes(
         t_ref,
+        c_ref,
         [weights[odd] * parts[odd][0] for odd in range(2)],
         [weights[odd] * parts[odd][1] for odd in range(2)],
         out_ref,
     )
 
 
-def finish(t_ref, s_ref, planes, adjoint, out_ref):
+def finish(t_ref, c_ref, s_ref, planes, adjoint, out_ref):
     values = []
     for at in range(4):
         factor = adjoint[at]
         values.append(planes[at] * jnp.concatenate([factor, factor], axis=1))
-    found = from_planes(t_ref, values)
+    found = from_planes(t_ref, c_ref, values)
     parts = parts_of(s_ref)
     out = []
     for odd in range(2):
-        fraction = mode_rows(odd)[0]
+        fraction = c_ref[odd]
         a, b = found[odd]
         out.append(
             (
@@ -609,6 +603,8 @@
     u_planes,
     planes,
     s_planes,
+    c_ref,
+    count,
     ready,
     blank,
     send_sems,
@@ -778,19 +774,21 @@
     sent.append((3, (N_MER - 1) * 4, (N_MER - 1) * 4, 8))
 
     stiffness_tables(d_ref, k_ref)
+    column_tables(c_ref)
+    face_tables(faces, count)
+    wait(blank, (N_MER - 1) * 4, recv_sems.at[3])
+    metric_tables(metric_in, mode, mer, mass, diag, count, turn)
     table_copy.wait()
 
     wait_either(double, blank, 2 * (N_MODE - 1) * N_MER, (N_MODE - 1) * N_MER, recv_sems.at[0])
 
     def first(slot):
-        first_stage(plane_in.at[0, slot], t_ref, u_planes.at[slot], plane_out.at[0, slot])
+        first_stage(plane_in.at[0, slot], t_ref, c_ref, u_planes.at[slot], plane_out.at[0, slot])
 
     each_slot(first)
     pl.semaphore_wait(ready, N_MODE - 1)
     send_to_modes(plane_out.at[0], mode_in.at[1], 4)
 
-    wait(blank, (N_MER - 1) * 4, recv_sems.at[3])
-    metric_tables(metric_in, mode, mer, mass, diag, faces, turn)
     wait(blank, (N_MER - 1) * GROUPS, recv_sems.at[2])
     emit = send_to_planes(mode_out.at[0], plane_in.at[1], 6)
     for half in range(2):
@@ -802,14 +800,14 @@
         solve(mode_in.at[1], mode_out.at[1], half, True, False, True, solve_scratch, emit)
 
     def multiplier(slot):
-        adjoint_planes(plane_in.at[1, slot], t_ref, s_planes.at[slot])
+        adjoint_planes(plane_in.at[1, slot], t_ref, c_ref, s_planes.at[slot])
 
     wait_planes(6)
     each_slot(multiplier)
 
     def second(slot):
-        state_planes(parts_of(plane_in.at[2, slot]), t_ref, planes)
-        finish(t_ref, plane_in.at[1, slot], planes, s_planes.at[slot], plane_out.at[1, slot])
+        state_planes(parts_of(plane_in.at[2, slot]), t_ref, c_ref, planes)
+        finish(t_ref, c_ref, plane_in.at[1, slot], planes, s_planes.at[slot], plane_out.at[1, slot])
 
     wait_planes(8)
     each_slot(second)
@@ -821,9 +819,10 @@
         solve(mode_in.at[2], mode_out.at[2], half, False, True, True, solve_scratch, emit)
 
     def third(slot):
-        adjoint_planes(plane_in.at[3, slot], t_ref, s_planes.at[slot])
+        s_in = plane_in.at[3, slot]
+        adjoint_planes(s_in, t_ref, c_ref, s_planes.at[slot])
         finish(
-            t_ref, plane_in.at[3, slot], u_planes.at[slot], s_planes.at[slot], plane_out.at[2, slot]
+            t_ref, c_ref, s_in, u_planes.at[slot], s_planes.at[slot], plane_out.at[2, slot]
         )
         native_in[slot, mode] = plane_out[2, slot, :, mine]
 
@@ -885,6 +884,8 @@
             scratch(2, (4, HALF, 2 * LANES)),
             scratch(4, (HALF, 2 * LANES)),
             scratch(2, (4, HALF, LANES)),
+            scratch(5, (HALF, LANES)),
+            pltpu.VMEM((PADDED, ELEMENTS), F32),
             pltpu.SemaphoreType.REGULAR,
             pltpu.VMEM((2 * COUNT, 8, LANES), F32),
             pltpu.SemaphoreType.DMA((15,)),

time: 101 us -> 102 us (level)
  no operation moved by 1% of the time
where the time goes in v8:
time: 102 us
  Pallas kernels  101 us (99%)
    pallas_call x1, Pallas kernels, program(): pl.pallas_call(program_kernel, out_shape=jax.ShapeDtypeStruct((GROUPS, 2,...  98.9 us
    pallas_call x1, Pallas kernels, tiles_to_native(): pl.pallas_call(tiles_to_native_kernel, out_shape=jax.ShapeDtypeStruct(sha...  2.53 us

profile of v8, /device:TPU:1, one launch (start us, length us, event | category | flops | bytes accessed | tf_op | source)
XLA Modules:
  0.0 101.6 jit_solution(10655180603235165927)
XLA Ops:
  0.0 98.9 %program.1.t_hbm = f32[11,2,8,8,128]{4,3,2,1,0:T(8,128)} custom-call(f32[9,9,2048]{2,1,0:T(8,128)} %state_ref.1, f32[9,9,2048]{2,1,0:T(8,128)} %cotangent_hbm.1, f32[9,9,16]{2,1,0:T(8,128)} %mass_ref.1, f32[9,9,16]{2,1,0:T(8,128)} %inverse_ref.1, f32[9,9]{1,0:T(8,128)} %d_ref.1, bf16[8,512,256]{2,1,0:T(8,128)(2,1)} %constant.2.clone.t_hbm), custom_call_target="tpu_custom_call" | custom-call | tf_op jit(solution)/shard_map/program/pallas_call | solution.py:866
  98.9 2.5 %tiles_to_native.1 = f32[9,9,2048]{2,1,0:T(8,128)} custom-call(f32[11,2,8,8,128]{4,3,2,1,0:T(8,128)} %program.1.t_hbm), custom_call_target="tpu_custom_call" | custom-call | tf_op jit(solution)/shard_map/tiles_to_native/pallas_call | solution.py:118

commit v9 on v6

--- a/solution.py
+++ b/solution.py
@@ -47,11 +47,11 @@
 
 def mix(first, second):
     shape = first.shape
-    low = lax.broadcasted_iota(jnp.int32, shape, len(shape) - 2) % 8 < 4
     axis = len(shape) - 2
+    low = lax.broadcasted_iota(jnp.int32, shape, axis) % 4 < 2
     return (
-        jnp.where(low, first, pltpu.roll(second, 4, axis)),
-        jnp.where(low, pltpu.roll(first, 4, axis), second),
+        jnp.where(low, first, pltpu.roll(second, 2, axis)),
+        jnp.where(low, pltpu.roll(first, 6, axis), second),
     )
 
 
@@ -91,32 +91,31 @@
 
 
 def tiles_to_native_kernel(t_hbm, out_hbm, tiles_in, rows, turn, native, in_sems, out_sems):
-    loads = [
-        pltpu.make_async_copy(t_hbm.at[group], tiles_in.at[group], in_sems.at[group])
-        for group in range(GROUPS)
-    ]
-    stores = [
-        pltpu.make_async_copy(native.at[i], out_hbm.at[i], out_sems.at[i]) for i in range(NODE)
-    ]
-    for load in loads:
-        load.start()
-    done = 0
-    for group in range(GROUPS):
-        loads[group].wait()
-        for odd in range(2):
-            tiles = tiles_in[group, odd].reshape(4, 2, 8, LANES)
-            real, imag = mix(tiles[:, 0], tiles[:, 1])
-            turn[0, group, pl.ds(odd, 32, stride=2), :] = real.reshape(32, LANES)
-            turn[1, group, pl.ds(odd, 32, stride=2), :] = imag.reshape(32, LANES)
-        both = jnp.concatenate([turn[0, group], turn[1, group]], axis=0)
-        rows[group * LANES : (group + 1) * LANES, :] = both.T
-        while done < NODE and (done + 1) * NODE <= (group + 1) * 8:
+    parts = ((0, 6, 0, 5), (6, GROUPS, 5, NODE))
+    loads, stores = [], []
+    for at, (start, stop, first, last) in enumerate(parts):
+        groups, nodes = pl.ds(start, stop - start), pl.ds(first, last - first)
+        loads.append(
+            pltpu.make_async_copy(t_hbm.at[groups], tiles_in.at[groups], in_sems.at[at])
+        )
+        stores.append(pltpu.make_async_copy(native.at[nodes], out_hbm.at[nodes], out_sems.at[at]))
+        loads[at].start()
+    for at, (start, stop, first, last) in enumerate(parts):
+        loads[at].wait()
+        for group in range(start, stop):
+            for odd in range(2):
+                tiles = tiles_in[group, odd].reshape(4, 2, 8, LANES)
+                real, imag = mix(tiles[:, 0], tiles[:, 1])
+                turn[0, group, pl.ds(odd, 32, stride=2), :] = real.reshape(32, LANES)
+                turn[1, group, pl.ds(odd, 32, stride=2), :] = imag.reshape(32, LANES)
+            both = jnp.concatenate([turn[0, group], turn[1, group]], axis=0)
+            rows[group * LANES : (group + 1) * LANES, :] = both.T
+        for i in range(first, last):
             for e in range(ELEM_DEV):
-                native[done, :, e * LANES : (e + 1) * LANES] = rows[
-                    pl.ds(done * NODE * ELEM_DEV + e, NODE, stride=ELEM_DEV), :
+                native[i, :, e * LANES : (e + 1) * LANES] = rows[
+                    pl.ds(i * NODE * ELEM_DEV + e, NODE, stride=ELEM_DEV), :
                 ]
-            stores[done].start()
-            done += 1
+        stores[at].start()
     for store in stores:
         store.wait()
 
@@ -134,8 +133,8 @@
             pltpu.VMEM((PADDED * ELEM_DEV, LANES), F32),
             pltpu.VMEM((2, GROUPS, 64, LANES), F32),
             pltpu.VMEM(shape, F32),
-            pltpu.SemaphoreType.DMA((GROUPS,)),
-            pltpu.SemaphoreType.DMA((NODE,)),
+            pltpu.SemaphoreType.DMA((2,)),
+            pltpu.SemaphoreType.DMA((2,)),
         ],
         compiler_params=pltpu.CompilerParams(vmem_limit_bytes=62 << 20),
         name="tiles_to_native",
@@ -187,16 +186,7 @@
         out_ref[kind, GROUPS:] = jnp.zeros((16 - GROUPS, LANES), F32)
 
 
-def metric_tables(m_ref, mode_group, place, mass, diag, faces, turn):
-    inverse = diag.at[0]
-    for kind, out in ((0, mass), (1, inverse)):
-        for h in range(2):
-            rows = exchange([m_ref[8 * h + at, kind] for at in range(8)])
-            for at in range(8):
-                for group in range(GROUPS):
-                    turn[h, group, at : at + 1] = rows[at][group : group + 1]
-            for group in range(GROUPS):
-                out[group * 8 : (group + 1) * 8, h * LANES : (h + 1) * LANES] = turn[h, group, 0:8]
+def face_tables(faces, count):
     shape = (PADDED, ELEMENTS)
     node = lax.broadcasted_iota(jnp.int32, shape, 0)
     element = lax.broadcasted_iota(jnp.int32, shape, 1)
@@ -208,12 +198,25 @@
     marks = [jnp.where(mark, 1.0, 0.0).astype(F32) for mark in (upper, lower, outer, inner)]
     for at in range(4):
         faces[at] = marks[at]
-    count = marks[0] + marks[1] + marks[2] + marks[3]
+    count[...] = marks[0] + marks[1] + marks[2] + marks[3]
+
+
+def metric_tables(m_ref, mode_group, place, mass, diag, count, turn):
+    inverse = diag.at[0]
+    for kind, out in ((0, mass), (1, inverse)):
+        for h in range(2):
+            rows = exchange([m_ref[8 * h + at, kind] for at in range(8)])
+            for at in range(8):
+                for group in range(GROUPS):
+                    turn[h, group, at : at + 1] = rows[at][group : group + 1]
+            for group in range(GROUPS):
+                out[group * 8 : (group + 1) * 8, h * LANES : (h + 1) * LANES] = turn[h, group, 0:8]
     values = inverse[...]
     for n in range(4):
-        number = mode_group * 64 + lax.rem(place, 8) * 8 + 2 * n + place // 8
+        offset = lax.rem(place, 8) // 2 * 8 + lax.rem(place, 2) * 2 + n // 2 * 4 + n % 2
+        number = mode_group * 64 + 2 * offset + place // 8
         fraction = number.astype(F32) / MODES
-        diag[n] = mass[...] * (1.0 + AZIMUTH_WEIGHT * fraction * fraction * values) + count
+        diag[n] = mass[...] * (1.0 + AZIMUTH_WEIGHT * fraction * fraction * values) + count[...]
 
 
 def owner_of(extra_group, place):
@@ -286,15 +289,20 @@
 def solve(b_ref, out_ref, weigh_in, weigh_out, by_owner, scratch, emit):
     mass, diag, faces, k_ref, r, p, q, alphas, turn = scratch
     load_tiles(b_ref, turn, mass if weigh_in else None, r, by_owner)
-    norms = tuple(total(fold(r[n] * r[n]) + fold(r[n + 4] * r[n + 4])) for n in range(4))
-    p[ITERS - 1] = jnp.zeros_like(p[ITERS - 1])
     empty = jnp.zeros((8, ELEMENTS), F32)
 
-    def operate(sweep, before, n, beta, norm):
-        curve = None
-        for s in (n, n + 4):
-            now = r[s] + beta * p[before, s]
+    def add(whole, part):
+        part = fold(part)
+        return part if whole is None else whole + part
+
+    def operate(sweep, n, alpha, beta):
+        norm = curve = bend = None
+        for s in (n // 2 * 4 + n % 2, n // 2 * 4 + 2 + n % 2):
+            rest = r[s] - alpha * q[s]
+            now = rest + beta * p[lax.rem(sweep + ITERS - 1, ITERS), s]
+            r[s] = rest
             p[sweep, s] = now
+            norm = add(norm, rest * rest)
             high = now.astype(BF16).astype(F32)
             halves = jnp.concatenate([high, now - high], axis=0).astype(BF16)
             image = jnp.dot(k_ref[...], halves, preferred_element_type=F32)
@@ -318,41 +326,26 @@
                 axis=0,
             )
             q[s] = image
-            part = fold(now * image)
-            curve = part if curve is None else curve + part
-        alpha = norm / total(curve)
+            curve = add(curve, now * image)
+            bend = add(bend, image * image)
+        curve = total(curve)
+        alpha = total(norm) / curve
         alphas[sweep * 4 + n] = alpha
-        return alpha
-
-    def reduce(n, alpha):
-        part = None
-        for s in (n, n + 4):
-            value = r[s] - alpha * q[s]
-            r[s] = value
-            add = fold(value * value)
-            part = add if part is None else part + add
-        return total(part)
-
-    def sweep_body(sweep, carry):
-        norms, betas = carry
-        before = lax.rem(sweep + ITERS - 1, ITERS)
-        step, after = [None] * 4, [None] * 4
-        for n in range(5):
-            if n < 4:
-                step[n] = operate(sweep, before, n, betas[n], norms[n])
-            if n > 0:
-                after[n - 1] = reduce(n - 1, step[n - 1])
-        return tuple(after), tuple(after[n] / norms[n] for n in range(4))
-
-    none = (jnp.zeros((1, ELEMENTS), F32),) * 4
-    norms, betas = lax.fori_loop(0, ITERS - 1, sweep_body, (norms, none))
-    for n in range(4):
-        operate(ITERS - 1, ITERS - 2, n, betas[n], norms[n])
+        return alpha, jnp.maximum(alpha * (total(bend) / curve) - 1.0, 0.0)
+
+    none = jnp.zeros((1, ELEMENTS), F32)
+    lax.fori_loop(
+        0,
+        ITERS,
+        lambda sweep, steps: tuple(operate(sweep, n, *steps[n]) for n in range(4)),
+        ((none, none),) * 4,
+    )
 
     def value_of(s, rows, lanes):
-        value = alphas[s % 4, :, lanes] * p[0, s, rows, lanes]
+        n = s // 4 * 2 + s % 2
+        value = alphas[n, :, lanes] * p[0, s, rows, lanes]
         for sweep in range(1, ITERS):
-            value = value + alphas[sweep * 4 + s % 4, :, lanes] * p[sweep, s, rows, lanes]
+            value = value + alphas[sweep * 4 + n, :, lanes] * p[sweep, s, rows, lanes]
         return value * mass[rows, lanes] if weigh_out else value
 
     store_tiles(value_of, turn, out_ref, emit)
@@ -405,21 +398,26 @@
         out_ref[odd] = jnp.stack([one, two], axis=1).reshape(64, 8, LANES)
 
 
-def mode_rows(odd):
+def column_tables(c_ref):
     row = lax.broadcasted_iota(jnp.int32, (HALF, LANES), 0)
-    mode = 2 * ((row // 32 % 4 * 2 + row // 128) * 32 + row % 32) + odd
-    fraction = mode.astype(F32) / MODES
-    weight = jnp.where(mode == 0, 1.0 / PLANES, 2.0 / PLANES).astype(F32)
-    sign = jnp.where(row % 2 == 0, 1.0, -1.0).astype(F32)
-    return fraction, weight, sign
-
-
-def first_row(shape):
-    return lax.broadcasted_iota(jnp.int32, shape, 0) == 0
-
-
-def to_planes(t_ref, cos_fields, sin_fields, out_ref):
-    sign = mode_rows(0)[2][:, :1]
+    for odd in range(2):
+        mode = 2 * ((row // 32 % 4 * 2 + row // 128) * 32 + row % 32) + odd
+        c_ref[odd] = mode.astype(F32) / MODES
+        c_ref[2 + odd] = jnp.where(mode == 0, 1.0 / PLANES, 2.0 / PLANES).astype(F32)
+    c_ref[4] = jnp.where(row % 2 == 0, 1.0, -1.0).astype(F32)
+
+
+def signs(c_ref, width):
+    return jnp.concatenate([c_ref[4]] * (width // LANES), axis=1)
+
+
+def without_first(value):
+    head = lax.broadcasted_iota(jnp.int32, (8, value.shape[1]), 0) == 0
+    return jnp.concatenate([jnp.where(head, 0.0, value[:8]), value[8:]], axis=0)
+
+
+def to_planes(t_ref, c_ref, cos_fields, sin_fields, out_ref):
+    sign = signs(c_ref, cos_fields[0].shape[1])
     cos_even, cos_odd = apply(t_ref, 0, cos_fields[0]), apply(t_ref, 1, cos_fields[1])
     sin_even, sin_odd = apply(t_ref, 2, sin_fields[0]), apply(t_ref, 3, sin_fields[1])
     quarter_cos = jnp.sum(sign * cos_fields[0], axis=0, keepdims=True)
@@ -434,14 +432,11 @@
     out_ref[3, 0:1] = quarter_cos + quarter_sin
 
 
-def from_planes(t_ref, values):
-    shape = values[0].shape
-    sign = mode_rows(0)[2][:, :1]
-    first = first_row(shape)
+def from_planes(t_ref, c_ref, values):
+    sign = signs(c_ref, values[0].shape[1])
     quarter, three = values[1][0:1], values[3][0:1]
     one = values[0]
-    two = jnp.where(first, 0.0, values[1])
-    four = jnp.where(first, 0.0, values[3])
+    two, four = without_first(values[1]), without_first(values[3])
     plus, minus = one + two, one - two
     plus_far, minus_far = values[2] + four, values[2] - four
     a_even = apply(t_ref, 4, plus + plus_far) + sign * (quarter + three)
@@ -451,49 +446,50 @@
     return (a_even, b_even), (a_odd, b_odd)
 
 
-def state_planes(parts, t_ref, out_ref):
+def state_planes(parts, t_ref, c_ref, out_ref):
     cos_fields, sin_fields = [], []
     for odd in range(2):
         real, imag = parts[odd]
-        fraction = mode_rows(odd)[0]
+        fraction = c_ref[odd]
         cos_fields.append(jnp.concatenate([real, -fraction * imag], axis=1))
         sin_fields.append(jnp.concatenate([imag, fraction * real], axis=1))
-    to_planes(t_ref, cos_fields, sin_fields, out_ref)
-
-
-def first_stage(u_ref, t_ref, planes, out_ref):
+    to_planes(t_ref, c_ref, cos_fields, sin_fields, out_ref)
+
+
+def first_stage(u_ref, t_ref, c_ref, planes, out_ref):
     parts = parts_of(u_ref)
-    state_planes(parts, t_ref, planes)
+    state_planes(parts, t_ref, c_ref, planes)
     values = [planes[at, :, :LANES] * planes[at, :, LANES:] for at in range(4)]
-    found = from_planes(t_ref, values)
+    found = from_planes(t_ref, c_ref, values)
     out = []
     for odd in range(2):
-        weight = mode_rows(odd)[1]
+        weight = c_ref[2 + odd]
         out.append(tuple(parts[odd][c] - weight * found[odd][c] for c in range(2)))
     parts_to(out_ref, out)
 
 
-def adjoint_planes(s_ref, t_ref, out_ref):
+def adjoint_planes(s_ref, t_ref, c_ref, out_ref):
     parts = parts_of(s_ref)
-    weights = [mode_rows(odd)[1] for odd in range(2)]
+    weights = [c_ref[2 + odd] for odd in range(2)]
     to_planes(
         t_ref,
+        c_ref,
         [weights[odd] * parts[odd][0] for odd in range(2)],
         [weights[odd] * parts[odd][1] for odd in range(2)],
         out_ref,
     )
 
 
-def finish(t_ref, s_ref, planes, adjoint, out_ref):
+def finish(t_ref, c_ref, s_ref, planes, adjoint, out_ref):
     values = []
     for at in range(4):
         factor = adjoint[at]
         values.append(planes[at] * jnp.concatenate([factor, factor], axis=1))
-    found = from_planes(t_ref, values)
+    found = from_planes(t_ref, c_ref, values)
     parts = parts_of(s_ref)
     out = []
     for odd in range(2):
-        fraction = mode_rows(odd)[0]
+        fraction = c_ref[odd]
         a, b = found[odd]
         out.append(
             (
@@ -519,19 +515,19 @@
     ).start()
 
 
-def wait(blank, tiles, sem):
-    whole = blank.at[pl.ds(0, tiles)]
+def wait(blank, tiles, sem, rows=8):
+    whole = blank.at[pl.ds(0, tiles), pl.ds(0, rows)]
     pltpu.make_async_copy(whole, whole, sem).wait()
 
 
-def wait_either(double, blank, tiles_double, tiles_single, sem):
+def wait_either(double, blank, tiles_double, tiles_single, sem, rows=8):
     @pl.when(double)
     def _():
-        wait(blank, tiles_double, sem)
+        wait(blank, tiles_double, sem, rows)
 
     @pl.when(jnp.logical_not(double))
     def _():
-        wait(blank, tiles_single, sem)
+        wait(blank, tiles_single, sem, rows)
 
 
 def place_at(mer, k):
@@ -609,6 +605,8 @@
     u_planes,
     planes,
     s_planes,
+    c_ref,
+    count,
     ready,
     blank,
     send_sems,
@@ -674,7 +672,7 @@
             if core == 1:
                 target[:, odd, row] = source[:, mode, mer]
 
-        sent.append((at, 16 * GROUPS - 2, 16 * GROUPS - 1))
+        sent.append((at, 16 * GROUPS - 2, 16 * GROUPS - 1, 8))
         return emit
 
     def wait_planes(at):
@@ -702,7 +700,7 @@
         def _():
             each_other(mode, mer, (0, 1), act)
 
-        sent.append((at, 2 * (COUNT - 1), COUNT - 1))
+        sent.append((at, 2 * (COUNT - 1), COUNT - 1, 8))
 
     def wait_modes(at):
         wait_either(double, blank, 16 * GROUPS - 2, 16 * GROUPS - 1, recv_sems.at[at])
@@ -723,7 +721,7 @@
 
     each_group(mode, (0,), send_extra_state)
     each_group(mode, (0, 1), send_state)
-    sent.append((0, N_MER * (GROUPS - 2), N_MER * (GROUPS - 1)))
+    sent.append((0, N_MER * (GROUPS - 2), N_MER * (GROUPS - 1), 8))
 
     cotangent_copy.wait()
     native_to_tiles(cotangent_in, native_out.at[1], rows, turn)
@@ -746,23 +744,28 @@
         send(metric_out, metric_in.at[mer], mode, place, sems, 3)
 
     each_place(mer, send_cotangent)
-    sent.append((2, (N_MER - 1) * GROUPS, (N_MER - 1) * GROUPS))
-    sent.append((3, (N_MER - 1) * 4, (N_MER - 1) * 4))
-
+    sent.append((2, (N_MER - 1) * GROUPS, (N_MER - 1) * GROUPS, 8))
+    sent.append((3, (N_MER - 1) * 4, (N_MER - 1) * 4, 8))
+
+    p_ref, q_ref = solve_scratch[5:7]
+    p_ref[ITERS - 1] = jnp.zeros((8, PADDED, ELEMENTS), F32)
+    q_ref[...] = jnp.zeros((8, PADDED, ELEMENTS), F32)
     stiffness_tables(d_ref, k_ref)
+    column_tables(c_ref)
+    face_tables(faces, count)
+    wait(blank, (N_MER - 1) * 4, recv_sems.at[3])
+    metric_tables(metric_in, mode, mer, mass, diag, count, turn)
     table_copy.wait()
 
     wait_either(double, blank, 2 * (N_MODE - 1) * N_MER, (N_MODE - 1) * N_MER, recv_sems.at[0])
 
     def first(slot):
-        first_stage(plane_in.at[0, slot], t_ref, u_planes.at[slot], plane_out.at[0, slot])
+        first_stage(plane_in.at[0, slot], t_ref, c_ref, u_planes.at[slot], plane_out.at[0, slot])
 
     each_slot(first)
     pl.semaphore_wait(ready, N_MODE - 1)
     send_to_modes(plane_out.at[0], mode_in.at[1], 4)
 
-    wait(blank, (N_MER - 1) * 4, recv_sems.at[3])
-    metric_tables(metric_in, mode, mer, mass, diag, faces, turn)
     wait(blank, (N_MER - 1) * GROUPS, recv_sems.at[2])
     emit = send_to_planes(mode_out.at[0], plane_in.at[1], 5)
     solve(mode_in.at[0], mode_out.at[0], False, True, False, solve_scratch, emit)
@@ -772,14 +775,14 @@
     solve(mode_in.at[1], mode_out.at[1], True, False, True, solve_scratch, emit)
 
     def multiplier(slot):
-        adjoint_planes(plane_in.at[1, slot], t_ref, s_planes.at[slot])
+        adjoint_planes(plane_in.at[1, slot], t_ref, c_ref, s_planes.at[slot])
 
     wait_planes(5)
     each_slot(multiplier)
 
     def second(slot):
-        state_planes(parts_of(plane_in.at[2, slot]), t_ref, planes)
-        finish(t_ref, plane_in.at[1, slot], planes, s_planes.at[slot], plane_out.at[1, slot])
+        state_planes(parts_of(plane_in.at[2, slot]), t_ref, c_ref, planes)
+        finish(t_ref, c_ref, plane_in.at[1, slot], planes, s_planes.at[slot], plane_out.at[1, slot])
 
     wait_planes(6)
     each_slot(second)
@@ -790,9 +793,10 @@
     solve(mode_in.at[2], mode_out.at[2], False, True, True, solve_scratch, emit)
 
     def third(slot):
-        adjoint_planes(plane_in.at[3, slot], t_ref, s_planes.at[slot])
+        s_in = plane_in.at[3, slot]
+        adjoint_planes(s_in, t_ref, c_ref, s_planes.at[slot])
         finish(
-            t_ref, plane_in.at[3, slot], u_planes.at[slot], s_planes.at[slot], plane_out.at[2, slot]
+            t_ref, c_ref, s_in, u_planes.at[slot], s_planes.at[slot], plane_out.at[2, slot]
         )
         native_in[slot, mode] = plane_out[2, slot, :, mine]
 
@@ -804,7 +808,7 @@
 
     wait_planes(8)
     each_slot(third)
-    sent.append((9, 2 * (N_MODE - 1) * N_MER, (N_MODE - 1) * N_MER))
+    sent.append((9, 2 * (N_MODE - 1) * N_MER, (N_MODE - 1) * N_MER, 8))
     wait_either(double, blank, N_MER * (GROUPS - 2), N_MER * (GROUPS - 1), recv_sems.at[9])
     turned = lax.rem(lax.rem(mer, 4) + mer // 4, 4)
     copies = [pltpu.make_async_copy(native_in.at[0], out_hbm.at[0:N_MODE], copy_sems.at[2])]
@@ -817,8 +821,8 @@
         )
     for copy in copies:
         copy.start()
-    for at, tiles_double, tiles_single in sent:
-        wait_either(double, blank, tiles_double, tiles_single, send_sems.at[at])
+    for at, tiles_double, tiles_single, rows_each in sent:
+        wait_either(double, blank, tiles_double, tiles_single, send_sems.at[at], rows_each)
     for copy in copies:
         copy.wait()
 
@@ -854,6 +858,8 @@
             scratch(2, (4, HALF, 2 * LANES)),
             scratch(4, (HALF, 2 * LANES)),
             scratch(2, (4, HALF, LANES)),
+            scratch(5, (HALF, LANES)),
+            pltpu.VMEM((PADDED, ELEMENTS), F32),
             pltpu.SemaphoreType.REGULAR,
             pltpu.VMEM((2 * COUNT, 8, LANES), F32),
             pltpu.SemaphoreType.DMA((10,)),

time: 102 us -> 105 us (1.029)
  Pallas kernels: 102 us -> 104 us
    pallas_call x1, Pallas kernels: 99 us -> 102 us  [program(): pl.pallas_call(program_kernel, out_shape=jax.ShapeDtypeStruct((GROUPS, 2,...]
where the time goes in v9:
time: 105 us
  Pallas kernels  104 us (99%)
    pallas_call x1, Pallas kernels, program(): pl.pallas_call(program_kernel, out_shape=jax.ShapeDtypeStruct((GROUPS, 2,...  102 us
    pallas_call x1, Pallas kernels, tiles_to_native(): pl.pallas_call(tiles_to_native_kernel, out_shape=jax.ShapeDtypeStruct(sha...  2.28 us

profile of v9, /device:TPU:1, one launch (start us, length us, event | category | flops | bytes accessed | tf_op | source)
XLA Modules:
  0.0 104.6 jit_solution(1817138492483548515)
XLA Ops:
  0.0 102.2 %program.1.t_hbm = f32[11,2,8,8,128]{4,3,2,1,0:T(8,128)} custom-call(f32[9,9,2048]{2,1,0:T(8,128)} %state_ref.1, f32[9,9,2048]{2,1,0:T(8,128)} %cotangent_hbm.1, f32[9,9,16]{2,1,0:T(8,128)} %mass_ref.1, f32[9,9,16]{2,1,0:T(8,128)} %inverse_ref.1, f32[9,9]{1,0:T(8,128)} %d_ref.1, bf16[8,512,256]{2,1,0:T(8,128)(2,1)} %constant.2.clone.t_hbm), custom_call_target="tpu_custom_call" | custom-call | tf_op jit(solution)/shard_map/program/pallas_call | solution.py:840
  102.2 2.3 %tiles_to_native.1 = f32[9,9,2048]{2,1,0:T(8,128)} custom-call(f32[11,2,8,8,128]{4,3,2,1,0:T(8,128)} %program.1.t_hbm), custom_call_target="tpu_custom_call" | custom-call | tf_op jit(solution)/shard_map/tiles_to_native/pallas_call | solution.py:126

commit v10 on v9

--- a/solution.py
+++ b/solution.py
@@ -162,8 +162,13 @@
     whole = whole + dot(dot(inner, stiffness), inner_t) * dot(outer, outer_t)
     high = whole.astype(BF16).astype(F32)
     low = whole - high
-    top = jnp.concatenate([high, high], axis=1)
-    bottom = jnp.concatenate([low, jnp.zeros_like(low)], axis=1)
+    shape = (PADDED, 2 * PADDED)
+    node = lax.broadcasted_iota(jnp.int32, shape, 0)
+    column = lax.broadcasted_iota(jnp.int32, shape, 1)
+    either = (node // 8 == column // 16) & (node % 8 == column % 8)
+    first = either & (column % 16 < 8)
+    top = dot(high, jnp.where(either, 1.0, 0.0).astype(F32))
+    bottom = dot(low, jnp.where(first, 1.0, 0.0).astype(F32))
     k_ref[...] = jnp.concatenate([top, bottom], axis=0).astype(BF16)
 
 
@@ -282,52 +287,45 @@
     return jnp.broadcast_to(jnp.sum(half, axis=(0, 1), keepdims=True), (1, ELEMENTS))
 
 
-def fold(value):
-    return jnp.sum(value.reshape(GROUPS, 8, ELEMENTS), axis=0)
-
-
 def solve(b_ref, out_ref, weigh_in, weigh_out, by_owner, scratch, emit):
-    mass, diag, faces, k_ref, r, p, q, alphas, turn = scratch
+    mass, diag, faces, k_ref, r, p, q, alphas, turn, units = scratch
     load_tiles(b_ref, turn, mass if weigh_in else None, r, by_owner)
-    empty = jnp.zeros((8, ELEMENTS), F32)
-
-    def add(whole, part):
-        part = fold(part)
-        return part if whole is None else whole + part
 
     def operate(sweep, n, alpha, beta):
-        norm = curve = bend = None
+        norm = curve = bend = jnp.zeros((8, ELEMENTS), F32)
+        before = lax.rem(sweep + ITERS - 1, ITERS)
         for s in (n // 2 * 4 + n % 2, n // 2 * 4 + 2 + n % 2):
-            rest = r[s] - alpha * q[s]
-            now = rest + beta * p[lax.rem(sweep + ITERS - 1, ITERS), s]
-            r[s] = rest
-            p[sweep, s] = now
-            norm = add(norm, rest * rest)
-            high = now.astype(BF16).astype(F32)
-            halves = jnp.concatenate([high, now - high], axis=0).astype(BF16)
-            image = jnp.dot(k_ref[...], halves, preferred_element_type=F32)
-            ahead = pltpu.roll(now[: PADDED - 8], ELEMENTS - RADIAL, 1)
-            behind = pltpu.roll(now[8:], RADIAL, 1)
-            image = (
-                image[:PADDED]
-                + image[PADDED:]
-                + diag[n] * now
-                - faces[0] * jnp.concatenate([empty, ahead], axis=0)
-                - faces[1] * jnp.concatenate([behind, empty], axis=0)
-            )
-            outward = pltpu.roll(now[:16], ELEMENTS - 1, 1)
-            inward = pltpu.roll(now[72:], 1, 1)
-            image = jnp.concatenate(
-                [
-                    image[:16] - faces[3, :16] * inward,
-                    image[16:72],
-                    image[72:] - faces[2, 72:] * outward,
-                ],
-                axis=0,
-            )
-            q[s] = image
-            curve = add(curve, now * image)
-            bend = add(bend, image * image)
+            for tile in range(GROUPS):
+                rows = slice(8 * tile, 8 * tile + 8)
+                rest = r[s, rows] - alpha * q[s, rows]
+                now = rest + beta * p[before, s, rows]
+                r[s, rows] = rest
+                p[sweep, s, rows] = now
+                norm = norm + rest * rest
+                high = now.astype(BF16).astype(F32)
+                unit = jnp.concatenate([high, now - high], axis=0).astype(BF16)
+                units[s, 16 * tile : 16 * tile + 16] = unit
+            image = jnp.dot(k_ref[...], units[s], preferred_element_type=F32)
+
+            def moved(tile, shift, s=s):
+                return pltpu.roll(p[sweep, s, 8 * tile : 8 * tile + 8], shift, 1)
+
+            for tile in range(GROUPS):
+                rows = slice(8 * tile, 8 * tile + 8)
+                now = p[sweep, s, rows]
+                value = image[rows] + image[PADDED + 8 * tile : PADDED + 8 * tile + 8]
+                value = value + diag[n, rows] * now
+                if tile not in (0, 9):
+                    value = value - faces[0, rows] * moved(tile - 1, ELEMENTS - RADIAL)
+                if tile not in (8, 10):
+                    value = value - faces[1, rows] * moved(tile + 1, RADIAL)
+                if tile < 2:
+                    value = value - faces[3, rows] * moved(tile + 9, 1)
+                if tile > 8:
+                    value = value - faces[2, rows] * moved(tile - 9, ELEMENTS - 1)
+                q[s, rows] = value
+                curve = curve + now * value
+                bend = bend + value * value
         curve = total(curve)
         alpha = total(norm) / curve
         alphas[sweep * 4 + n] = alpha
@@ -362,6 +360,7 @@
     FIELD,
     pltpu.VMEM((ITERS * 4, 1, ELEMENTS), F32),
     pltpu.VMEM((2, GROUPS, 64, LANES), F32),
+    pltpu.VMEM((8, 2 * PADDED, ELEMENTS), BF16),
 ]
 
 

time: 105 us -> 105 us (level)
  no operation moved by 1% of the time
where the time goes in v10:
time: 105 us
  Pallas kernels  105 us (100%)
    pallas_call x1, Pallas kernels, program(): pl.pallas_call(program_kernel, out_shape=jax.ShapeDtypeStruct((GROUPS, 2,...  102 us
    pallas_call x1, Pallas kernels, tiles_to_native(): pl.pallas_call(tiles_to_native_kernel, out_shape=jax.ShapeDtypeStruct(sha...  2.28 us

profile of v10, /device:TPU:1, one launch (start us, length us, event | category | flops | bytes accessed | tf_op | source)
XLA Modules:
  0.0 104.7 jit_solution(13990462424962974633)
XLA Ops:
  0.0 102.2 %program.1.t_hbm = f32[11,2,8,8,128]{4,3,2,1,0:T(8,128)} custom-call(f32[9,9,2048]{2,1,0:T(8,128)} %state_ref.1, f32[9,9,2048]{2,1,0:T(8,128)} %cotangent_hbm.1, f32[9,9,16]{2,1,0:T(8,128)} %mass_ref.1, f32[9,9,16]{2,1,0:T(8,128)} %inverse_ref.1, f32[9,9]{1,0:T(8,128)} %d_ref.1, bf16[8,512,256]{2,1,0:T(8,128)(2,1)} %constant.2.clone.t_hbm), custom_call_target="tpu_custom_call" | custom-call | tf_op jit(solution)/shard_map/program/pallas_call | solution.py:839
  102.3 2.3 %tiles_to_native.1 = f32[9,9,2048]{2,1,0:T(8,128)} custom-call(f32[11,2,8,8,128]{4,3,2,1,0:T(8,128)} %program.1.t_hbm), custom_call_target="tpu_custom_call" | custom-call | tf_op jit(solution)/shard_map/tiles_to_native/pallas_call | solution.py:126

commit v11 on v10

--- a/solution.py
+++ b/solution.py
@@ -191,22 +191,21 @@
         out_ref[kind, GROUPS:] = jnp.zeros((16 - GROUPS, LANES), F32)
 
 
-def face_tables(faces, count):
-    shape = (PADDED, ELEMENTS)
-    node = lax.broadcasted_iota(jnp.int32, shape, 0)
-    element = lax.broadcasted_iota(jnp.int32, shape, 1)
+def face_tables():
+    node = np.arange(PADDED)[:, None]
+    element = np.arange(ELEMENTS)[None, :]
     inside = node < NODES
-    upper = (node % NODE == NODE - 1) & (element < ELEMENTS - RADIAL) & inside
-    lower = (node % NODE == 0) & (element >= RADIAL) & inside
-    outer = (node // NODE == NODE - 1) & (element % RADIAL != RADIAL - 1) & inside
-    inner = (node // NODE == 0) & (element % RADIAL != 0)
-    marks = [jnp.where(mark, 1.0, 0.0).astype(F32) for mark in (upper, lower, outer, inner)]
-    for at in range(4):
-        faces[at] = marks[at]
-    count[...] = marks[0] + marks[1] + marks[2] + marks[3]
-
-
-def metric_tables(m_ref, mode_group, place, mass, diag, count, turn):
+    marks = [
+        (node % NODE == NODE - 1) & (element < ELEMENTS - RADIAL) & inside,
+        (node % NODE == 0) & (element >= RADIAL) & inside,
+        (node // NODE == NODE - 1) & (element % RADIAL != RADIAL - 1) & inside,
+        (node // NODE == 0) & (element % RADIAL != 0) & inside,
+    ]
+    marks = np.stack(marks).astype(np.float32)
+    return np.concatenate([marks, marks.sum(axis=0, keepdims=True)])
+
+
+def metric_tables(m_ref, mode_group, place, mass, diag, faces, turn):
     inverse = diag.at[0]
     for kind, out in ((0, mass), (1, inverse)):
         for h in range(2):
@@ -221,7 +220,7 @@
         offset = lax.rem(place, 8) // 2 * 8 + lax.rem(place, 2) * 2 + n // 2 * 4 + n % 2
         number = mode_group * 64 + 2 * offset + place // 8
         fraction = number.astype(F32) / MODES
-        diag[n] = mass[...] * (1.0 + AZIMUTH_WEIGHT * fraction * fraction * values) + count[...]
+        diag[n] = mass[...] * (1.0 + AZIMUTH_WEIGHT * fraction * fraction * values) + faces[4]
 
 
 def owner_of(extra_group, place):
@@ -289,18 +288,23 @@
 
 def solve(b_ref, out_ref, weigh_in, weigh_out, by_owner, scratch, emit):
     mass, diag, faces, k_ref, r, p, q, alphas, turn, units = scratch
-    load_tiles(b_ref, turn, mass if weigh_in else None, r, by_owner)
+    load_tiles(b_ref, turn, mass if weigh_in else None, p.at[0], by_owner)
 
     def operate(sweep, n, alpha, beta):
         norm = curve = bend = jnp.zeros((8, ELEMENTS), F32)
-        before = lax.rem(sweep + ITERS - 1, ITERS)
+        last = sweep == ITERS - 1
         for s in (n // 2 * 4 + n % 2, n // 2 * 4 + 2 + n % 2):
             for tile in range(GROUPS):
                 rows = slice(8 * tile, 8 * tile + 8)
-                rest = r[s, rows] - alpha * q[s, rows]
-                now = rest + beta * p[before, s, rows]
-                r[s, rows] = rest
-                p[sweep, s, rows] = now
+                if sweep == 0:
+                    rest = now = p[0, s, rows]
+                else:
+                    before = p[sweep - 1, s, rows]
+                    rest = (before if sweep == 1 else r[s, rows]) - alpha * q[s, rows]
+                    now = rest + beta * before
+                    p[sweep, s, rows] = now
+                    if not last:
+                        r[s, rows] = rest
                 norm = norm + rest * rest
                 high = now.astype(BF16).astype(F32)
                 unit = jnp.concatenate([high, now - high], axis=0).astype(BF16)
@@ -323,21 +327,20 @@
                     value = value - faces[3, rows] * moved(tile + 9, 1)
                 if tile > 8:
                     value = value - faces[2, rows] * moved(tile - 9, ELEMENTS - 1)
-                q[s, rows] = value
                 curve = curve + now * value
-                bend = bend + value * value
+                if not last:
+                    q[s, rows] = value
+                    bend = bend + value * value
         curve = total(curve)
         alpha = total(norm) / curve
         alphas[sweep * 4 + n] = alpha
+        if last:
+            return alpha, None
         return alpha, jnp.maximum(alpha * (total(bend) / curve) - 1.0, 0.0)
 
-    none = jnp.zeros((1, ELEMENTS), F32)
-    lax.fori_loop(
-        0,
-        ITERS,
-        lambda sweep, steps: tuple(operate(sweep, n, *steps[n]) for n in range(4)),
-        ((none, none),) * 4,
-    )
+    steps = [(None, None)] * 4
+    for sweep in range(ITERS):
+        steps = [operate(sweep, n, *steps[n]) for n in range(4)]
 
     def value_of(s, rows, lanes):
         n = s // 4 * 2 + s % 2
@@ -353,7 +356,7 @@
 SOLVE_SCRATCH = [
     pltpu.VMEM((PADDED, ELEMENTS), F32),
     pltpu.VMEM((4, PADDED, ELEMENTS), F32),
-    pltpu.VMEM((4, PADDED, ELEMENTS), F32),
+    pltpu.VMEM((5, PADDED, ELEMENTS), F32),
     pltpu.VMEM((2 * PADDED, 2 * PADDED), BF16),
     FIELD,
     pltpu.VMEM((ITERS, 8, PADDED, ELEMENTS), F32),
@@ -397,13 +400,13 @@
         out_ref[odd] = jnp.stack([one, two], axis=1).reshape(64, 8, LANES)
 
 
-def column_tables(c_ref):
-    row = lax.broadcasted_iota(jnp.int32, (HALF, LANES), 0)
-    for odd in range(2):
-        mode = 2 * ((row // 32 % 4 * 2 + row // 128) * 32 + row % 32) + odd
-        c_ref[odd] = mode.astype(F32) / MODES
-        c_ref[2 + odd] = jnp.where(mode == 0, 1.0 / PLANES, 2.0 / PLANES).astype(F32)
-    c_ref[4] = jnp.where(row % 2 == 0, 1.0, -1.0).astype(F32)
+def column_tables():
+    row = np.arange(HALF)
+    modes = [2 * ((row // 32 % 4 * 2 + row // 128) * 32 + row % 32) + odd for odd in range(2)]
+    columns = [mode / MODES for mode in modes]
+    columns += [np.where(mode == 0, 1.0 / PLANES, 2.0 / PLANES) for mode in modes]
+    columns.append(np.where(row % 2 == 0, 1.0, -1.0))
+    return np.repeat(np.stack(columns).astype(np.float32)[:, :, None], LANES, axis=2)
 
 
 def signs(c_ref, width):
@@ -588,6 +591,8 @@
     inverse_ref,
     d_ref,
     t_hbm,
+    c_hbm,
+    f_hbm,
     out_hbm,
     cotangent_in,
     t_ref,
@@ -605,7 +610,6 @@
     planes,
     s_planes,
     c_ref,
-    count,
     ready,
     blank,
     send_sems,
@@ -628,6 +632,12 @@
     table_copy = pltpu.make_async_copy(t_hbm, t_ref, copy_sems.at[1])
     cotangent_copy.start()
     table_copy.start()
+    constant_copies = [
+        pltpu.make_async_copy(c_hbm, c_ref, copy_sems.at[6]),
+        pltpu.make_async_copy(f_hbm, faces, copy_sems.at[7]),
+    ]
+    for copy in constant_copies:
+        copy.start()
     barrier = pltpu.get_barrier_semaphore()
 
     def greet(semaphore, other, place):
@@ -722,12 +732,17 @@
     each_group(mode, (0, 1), send_state)
     sent.append((0, N_MER * (GROUPS - 2), N_MER * (GROUPS - 1), 8))
 
+    metric_rows(mass_ref, inverse_ref, rows, metric_out)
+    metric_in[mer] = metric_out[...]
+
+    def send_metric(place):
+        send(metric_out, metric_in.at[mer], mode, place, sems, 3)
+
+    each_place(mer, send_metric)
     cotangent_copy.wait()
     native_to_tiles(cotangent_in, native_out.at[1], rows, turn)
     mode_in[0, 0, :, mer] = native_out[1, 0, :, odd, eighth]
     mode_in[0, 1, 0:SPARE, mer] = native_out[1, 1, 0:SPARE, odd, eighth]
-    metric_rows(mass_ref, inverse_ref, rows, metric_out)
-    metric_in[mer] = metric_out[...]
 
     def send_cotangent(place):
         which, at = place // 8, lax.rem(place, 8)
@@ -740,20 +755,16 @@
             sems,
             2,
         )
-        send(metric_out, metric_in.at[mer], mode, place, sems, 3)
 
     each_place(mer, send_cotangent)
     sent.append((2, (N_MER - 1) * GROUPS, (N_MER - 1) * GROUPS, 8))
     sent.append((3, (N_MER - 1) * 4, (N_MER - 1) * 4, 8))
 
-    p_ref, q_ref = solve_scratch[5:7]
-    p_ref[ITERS - 1] = jnp.zeros((8, PADDED, ELEMENTS), F32)
-    q_ref[...] = jnp.zeros((8, PADDED, ELEMENTS), F32)
     stiffness_tables(d_ref, k_ref)
-    column_tables(c_ref)
-    face_tables(faces, count)
+    for copy in constant_copies:
+        copy.wait()
     wait(blank, (N_MER - 1) * 4, recv_sems.at[3])
-    metric_tables(metric_in, mode, mer, mass, diag, count, turn)
+    metric_tables(metric_in, mode, mer, mass, diag, faces, turn)
     table_copy.wait()
 
     wait_either(double, blank, 2 * (N_MODE - 1) * N_MER, (N_MODE - 1) * N_MER, recv_sems.at[0])
@@ -826,7 +837,7 @@
         copy.wait()
 
 
-def program(state, cotangent, mass, inverse, derivative, table):
+def program(state, cotangent, mass, inverse, derivative, *constants):
     by_mode = (2, N_MODE, N_MER, 8, LANES)
     by_native = (2, N_MODE, 2, 8, 8, LANES)
     by_plane = (2, 2, COUNT // 2, 8, LANES)
@@ -839,12 +850,12 @@
     return pl.pallas_call(
         program_kernel,
         out_shape=jax.ShapeDtypeStruct((GROUPS, 2, 8, 8, LANES), F32),
-        in_specs=[vmem, hbm, vmem, vmem, vmem, hbm],
+        in_specs=[vmem, hbm, vmem, vmem, vmem, hbm, hbm, hbm],
         out_specs=hbm,
         scratch_shapes=[
             pltpu.VMEM((NODE, NODE, ELEM_DEV * LANES), F32),
             pltpu.VMEM((8, 2 * HALF, HALF), BF16),
-            pltpu.SemaphoreType.DMA((6,)),
+            pltpu.SemaphoreType.DMA((8,)),
             pltpu.VMEM((PADDED * ELEM_DEV, LANES), F32),
             scratch(2, by_native),
             pltpu.VMEM(by_native, F32),
@@ -858,7 +869,6 @@
             scratch(4, (HALF, 2 * LANES)),
             scratch(2, (4, HALF, LANES)),
             scratch(5, (HALF, LANES)),
-            pltpu.VMEM((PADDED, ELEMENTS), F32),
             pltpu.SemaphoreType.REGULAR,
             pltpu.VMEM((2 * COUNT, 8, LANES), F32),
             pltpu.SemaphoreType.DMA((10,)),
@@ -869,12 +879,14 @@
             collective_id=0, has_side_effects=True, vmem_limit_bytes=60 << 20
         ),
         name="program",
-    )(state, cotangent, mass, inverse, derivative, table)
+    )(state, cotangent, mass, inverse, derivative, *constants)
 
 
 def shards(cotangent, checkpoint, mass, inv_radius_sq, derivative):
-    table = jnp.asarray(tables())
-    return tiles_to_native(program(checkpoint, cotangent, mass, inv_radius_sq, derivative, table))
+    constants = [jnp.asarray(values()) for values in (tables, column_tables, face_tables)]
+    return tiles_to_native(
+        program(checkpoint, cotangent, mass, inv_radius_sq, derivative, *constants)
+    )
 
 
 def solution(mesh):

time: 105 us -> 103 us (0.981)
  Pallas kernels: 105 us -> 103 us
    pallas_call x1, Pallas kernels: 102 us -> 101 us  [program(): pl.pallas_call(program_kernel, out_shape=jax.ShapeDtypeStruct((GROUPS, 2,...]
where the time goes in v11:
time: 103 us
  Pallas kernels  103 us (100%)
    pallas_call x1, Pallas kernels, program(): pl.pallas_call(program_kernel, out_shape=jax.ShapeDtypeStruct((GROUPS, 2,...  101 us
    pallas_call x1, Pallas kernels, tiles_to_native(): pl.pallas_call(tiles_to_native_kernel, out_shape=jax.ShapeDtypeStruct(sha...  2.28 us

profile of v11, /device:TPU:1, one launch (start us, length us, event | category | flops | bytes accessed | tf_op | source)
XLA Modules:
  0.0 103.2 jit_solution(9996524634131412980)
XLA Ops:
  0.0 100.7 %program.1.t_hbm = f32[11,2,8,8,128]{4,3,2,1,0:T(8,128)} custom-call(f32[9,9,2048]{2,1,0:T(8,128)} %state_ref.1, f32[9,9,2048]{2,1,0:T(8,128)} %cotangent_hbm.1, f32[9,9,16]{2,1,0:T(8,128)} %mass_ref.1, f32[9,9,16]{2,1,0:T(8,128)} %inverse_ref.1, f32[9,9]{1,0:T(8,128)} %d_ref.1, bf16[8,512,256]{2,1,0:T(8,128)(2,1)} %constant.6.clone.t_hbm, ...), custom_call_target="tpu_custom_call" | custom-call | tf_op jit(solution)/shard_map/program/pallas_call | solution.py:850
  100.7 2.3 %tiles_to_native.1 = f32[9,9,2048]{2,1,0:T(8,128)} custom-call(f32[11,2,8,8,128]{4,3,2,1,0:T(8,128)} %program.1.t_hbm), custom_call_target="tpu_custom_call" | custom-call | tf_op jit(solution)/shard_map/tiles_to_native/pallas_call | solution.py:126

commit v12 on v7

--- a/solution.py
+++ b/solution.py
@@ -91,25 +91,33 @@
 
 
 def tiles_to_native_kernel(t_hbm, out_hbm, tiles_in, rows, turn, native, in_sems, out_sems):
-    load = pltpu.make_async_copy(t_hbm, tiles_in, in_sems.at[0])
-    load.start()
-    load.wait()
-    for group in range(GROUPS):
-        for odd in range(2):
-            tiles = tiles_in[group, odd].reshape(4, 2, 8, LANES)
-            real, imag = mix(tiles[:, 0], tiles[:, 1])
-            turn[0, group, pl.ds(odd, 32, stride=2), :] = real.reshape(32, LANES)
-            turn[1, group, pl.ds(odd, 32, stride=2), :] = imag.reshape(32, LANES)
-        both = jnp.concatenate([turn[0, group], turn[1, group]], axis=0)
-        rows[group * LANES : (group + 1) * LANES, :] = both.T
-    for i in range(NODE):
-        for e in range(ELEM_DEV):
-            native[i, :, e * LANES : (e + 1) * LANES] = rows[
-                pl.ds(i * NODE * ELEM_DEV + e, NODE, stride=ELEM_DEV), :
-            ]
-    store = pltpu.make_async_copy(native, out_hbm, out_sems.at[0])
-    store.start()
-    store.wait()
+    parts = ((0, 6, 0, 5), (6, GROUPS, 5, NODE))
+    loads, stores = [], []
+    for at, (start, stop, first, last) in enumerate(parts):
+        groups, nodes = pl.ds(start, stop - start), pl.ds(first, last - first)
+        loads.append(
+            pltpu.make_async_copy(t_hbm.at[groups], tiles_in.at[groups], in_sems.at[at])
+        )
+        stores.append(pltpu.make_async_copy(native.at[nodes], out_hbm.at[nodes], out_sems.at[at]))
+        loads[at].start()
+    for at, (start, stop, first, last) in enumerate(parts):
+        loads[at].wait()
+        for group in range(start, stop):
+            for odd in range(2):
+                tiles = tiles_in[group, odd].reshape(4, 2, 8, LANES)
+                real, imag = mix(tiles[:, 0], tiles[:, 1])
+                turn[0, group, pl.ds(odd, 32, stride=2), :] = real.reshape(32, LANES)
+                turn[1, group, pl.ds(odd, 32, stride=2), :] = imag.reshape(32, LANES)
+            both = jnp.concatenate([turn[0, group], turn[1, group]], axis=0)
+            rows[group * LANES : (group + 1) * LANES, :] = both.T
+        for i in range(first, last):
+            for e in range(ELEM_DEV):
+                native[i, :, e * LANES : (e + 1) * LANES] = rows[
+                    pl.ds(i * NODE * ELEM_DEV + e, NODE, stride=ELEM_DEV), :
+                ]
+        stores[at].start()
+    for store in stores:
+        store.wait()
 
 
 def tiles_to_native(tiles):
@@ -125,8 +133,8 @@
             pltpu.VMEM((PADDED * ELEM_DEV, LANES), F32),
             pltpu.VMEM((2, GROUPS, 64, LANES), F32),
             pltpu.VMEM(shape, F32),
-            pltpu.SemaphoreType.DMA((1,)),
-            pltpu.SemaphoreType.DMA((1,)),
+            pltpu.SemaphoreType.DMA((2,)),
+            pltpu.SemaphoreType.DMA((2,)),
         ],
         compiler_params=pltpu.CompilerParams(vmem_limit_bytes=62 << 20),
         name="tiles_to_native",
@@ -654,9 +662,11 @@
 
         lax.fori_loop(0, slots, body, 0)
 
-    def send_to_planes(source, target, at):
+    def send_to_planes(source, target, at, whole=False):
         def emit(core, half):
-            rows = pl.ds(4 * half, 4)
+            if whole and half == 0:
+                return
+            rows = pl.ds(0, 8) if whole else pl.ds(4 * half, 4)
 
             def act(other, core, place):
                 def single():
@@ -688,27 +698,27 @@
 
             each_other(mode, mer, (core,), act)
             if core == 1:
-                target[:, odd, row, 4 * half : 4 * half + 4] = source[
-                    :, mode, mer, 4 * half : 4 * half + 4
-                ]
-
-        for half in range(2):
-            sent.append((at + half, 16 * GROUPS - 2, 16 * GROUPS - 1, 4))
+                own = slice(0, 8) if whole else slice(4 * half, 4 * half + 4)
+                target[:, odd, row, own] = source[:, mode, mer, own]
+
+        for half in range(1 if whole else 0, 2):
+            sent.append((at + half, 16 * GROUPS - 2, 16 * GROUPS - 1, 8 if whole else 4))
         return emit
 
-    def wait_planes(at):
-        for half in range(2):
-            wait_either(double, blank, 2 * (COUNT - 1), COUNT - 1, recv_sems.at[at + half], 4)
-
-    def send_to_modes(source, target, at):
+    def wait_planes(at, whole=False):
+        for half in range(1 if whole else 0, 2):
+            sem = recv_sems.at[at + half]
+            wait_either(double, blank, 2 * (COUNT - 1), COUNT - 1, sem, 8 if whole else 4)
+
+    def send_to_modes(source, target, at, whole=False):
         target[0, mode, mer] = source[0, odd, row]
 
         @pl.when(double)
         def _():
             target[1, mode, mer] = source[1, odd, row]
 
-        for half in range(2):
-            rows = pl.ds(4 * half, 4)
+        for half in range(1 if whole else 0, 2):
+            rows = pl.ds(0, 8) if whole else pl.ds(4 * half, 4)
 
             def act(other, core, place, rows=rows, half=half):
                 index = order_of(other) * 8 + lax.rem(place, 8)
@@ -728,11 +738,11 @@
             def _(act=act):
                 each_other(mode, mer, (0, 1), act)
 
-            sent.append((at + half, 2 * (COUNT - 1), COUNT - 1, 4))
-
-    def wait_modes(at, half):
+            sent.append((at + half, 2 * (COUNT - 1), COUNT - 1, 8 if whole else 4))
+
+    def wait_modes(at, half, rows=4):
         wait_either(
-            double, blank, 16 * GROUPS - 2, 16 * GROUPS - 1, recv_sems.at[at + half], 4
+            double, blank, 16 * GROUPS - 2, 16 * GROUPS - 1, recv_sems.at[at + half], rows
         )
 
     mine = pl.ds(pl.multiple_of(order_of(mode) * 8, 8), 8)
@@ -787,24 +797,24 @@
 
     each_slot(first)
     pl.semaphore_wait(ready, N_MODE - 1)
-    send_to_modes(plane_out.at[0], mode_in.at[1], 4)
+    send_to_modes(plane_out.at[0], mode_in.at[1], 4, whole=True)
 
     wait(blank, (N_MER - 1) * 4, recv_sems.at[3])
     metric_tables(metric_in, mode, mer, mass, diag, faces, turn)
     wait(blank, (N_MER - 1) * GROUPS, recv_sems.at[2])
-    emit = send_to_planes(mode_out.at[0], plane_in.at[1], 6)
+    emit = send_to_planes(mode_out.at[0], plane_in.at[1], 6, whole=True)
     for half in range(2):
         solve(mode_in.at[0], mode_out.at[0], half, False, True, False, solve_scratch, emit)
 
     emit = send_to_planes(mode_out.at[1], plane_in.at[2], 8)
+    wait_modes(4, 1, 8)
     for half in range(2):
-        wait_modes(4, half)
         solve(mode_in.at[1], mode_out.at[1], half, True, False, True, solve_scratch, emit)
 
     def multiplier(slot):
         adjoint_planes(plane_in.at[1, slot], t_ref, s_planes.at[slot])
 
-    wait_planes(6)
+    wait_planes(6, whole=True)
     each_slot(multiplier)
 
     def second(slot):

time: 101 us -> 99.2 us (0.982)
  Pallas kernels: 101 us -> 98.9 us
    pallas_call x1, Pallas kernels: 98.2 us -> 96.6 us  [program(): pl.pallas_call(program_kernel, out_shape=jax.ShapeDtypeStruct((GROUPS, 2,...]
where the time goes in v12:
time: 99.2 us; the launch traced here: 99 us
  Pallas kernels  98.9 us (100%)
    pallas_call x1, Pallas kernels, program(): pl.pallas_call(program_kernel, out_shape=jax.ShapeDtypeStruct((GROUPS, 2,...  96.6 us
    pallas_call x1, Pallas kernels, tiles_to_native(): pl.pallas_call(tiles_to_native_kernel, out_shape=jax.ShapeDtypeStruct(sha...  2.28 us

profile of v12, /device:TPU:1, one launch (start us, length us, event | category | flops | bytes accessed | tf_op | source)
XLA Modules:
  0.0 99.0 jit_solution(17011940403985614839)
XLA Ops:
  0.0 96.6 %program.1.t_hbm = f32[11,2,8,8,128]{4,3,2,1,0:T(8,128)} custom-call(f32[9,9,2048]{2,1,0:T(8,128)} %state_ref.1, f32[9,9,2048]{2,1,0:T(8,128)} %cotangent_hbm.1, f32[9,9,16]{2,1,0:T(8,128)} %mass_ref.1, f32[9,9,16]{2,1,0:T(8,128)} %inverse_ref.1, f32[9,9]{1,0:T(8,128)} %d_ref.1, bf16[8,512,256]{2,1,0:T(8,128)(2,1)} %constant.2.clone.t_hbm), custom_call_target="tpu_custom_call" | custom-call | tf_op jit(solution)/shard_map/program/pallas_call | solution.py:877
  96.6 2.3 %tiles_to_native.1 = f32[9,9,2048]{2,1,0:T(8,128)} custom-call(f32[11,2,8,8,128]{4,3,2,1,0:T(8,128)} %program.1.t_hbm), custom_call_target="tpu_custom_call" | custom-call | tf_op jit(solution)/shard_map/tiles_to_native/pallas_call | solution.py:126

commit v13 on v12

--- a/solution.py
+++ b/solution.py
@@ -186,6 +186,20 @@
         out_ref[kind, GROUPS:] = jnp.zeros((16 - GROUPS, LANES), F32)
 
 
+def face_tables():
+    node = np.arange(PADDED)[:, None]
+    element = np.arange(ELEMENTS)[None, :]
+    inside = node < NODES
+    marks = [
+        (node % NODE == NODE - 1) & (element < ELEMENTS - RADIAL) & inside,
+        (node % NODE == 0) & (element >= RADIAL) & inside,
+        (node // NODE == NODE - 1) & (element % RADIAL != RADIAL - 1) & inside,
+        (node // NODE == 0) & (element % RADIAL != 0) & inside,
+    ]
+    marks = np.stack(marks).astype(np.float32)
+    return np.concatenate([marks, marks.sum(axis=0, keepdims=True)])
+
+
 def metric_tables(m_ref, mode_group, place, mass, diag, faces, turn):
     inverse = diag.at[0]
     for kind, out in ((0, mass), (1, inverse)):
@@ -196,24 +210,12 @@
                     turn[h, group, at : at + 1] = rows[at][group : group + 1]
             for group in range(GROUPS):
                 out[group * 8 : (group + 1) * 8, h * LANES : (h + 1) * LANES] = turn[h, group, 0:8]
-    shape = (PADDED, ELEMENTS)
-    node = lax.broadcasted_iota(jnp.int32, shape, 0)
-    element = lax.broadcasted_iota(jnp.int32, shape, 1)
-    inside = node < NODES
-    upper = (node % NODE == NODE - 1) & (element < ELEMENTS - RADIAL) & inside
-    lower = (node % NODE == 0) & (element >= RADIAL) & inside
-    outer = (node // NODE == NODE - 1) & (element % RADIAL != RADIAL - 1) & inside
-    inner = (node // NODE == 0) & (element % RADIAL != 0)
-    marks = [jnp.where(mark, 1.0, 0.0).astype(F32) for mark in (upper, lower, outer, inner)]
-    for at in range(4):
-        faces[at] = marks[at]
-    count = marks[0] + marks[1] + marks[2] + marks[3]
     values = inverse[...]
     for n in range(4):
         offset = lax.rem(place, 8) // 2 * 8 + lax.rem(place, 2) * 2 + n // 2 * 4 + n % 2
         number = mode_group * 64 + 2 * offset + place // 8
         fraction = number.astype(F32) / MODES
-        diag[n] = mass[...] * (1.0 + AZIMUTH_WEIGHT * fraction * fraction * values) + count
+        diag[n] = mass[...] * (1.0 + AZIMUTH_WEIGHT * fraction * fraction * values) + faces[4]
 
 
 def owner_of(extra_group, place):
@@ -370,7 +372,7 @@
 SOLVE_SCRATCH = [
     pltpu.VMEM((PADDED, ELEMENTS), F32),
     pltpu.VMEM((4, PADDED, ELEMENTS), F32),
-    pltpu.VMEM((4, PADDED, ELEMENTS), F32),
+    pltpu.VMEM((5, PADDED, ELEMENTS), F32),
     pltpu.VMEM((2 * PADDED, 2 * PADDED), BF16),
     FIELD,
     pltpu.VMEM((ITERS, 8, PADDED, ELEMENTS), F32),
@@ -413,21 +415,26 @@
         out_ref[odd] = jnp.stack([one, two], axis=1).reshape(64, 8, LANES)
 
 
-def mode_rows(odd):
-    row = lax.broadcasted_iota(jnp.int32, (HALF, LANES), 0)
-    mode = 2 * ((row // 32 % 4 * 2 + row // 128) * 32 + row % 32) + odd
-    fraction = mode.astype(F32) / MODES
-    weight = jnp.where(mode == 0, 1.0 / PLANES, 2.0 / PLANES).astype(F32)
-    sign = jnp.where(row % 2 == 0, 1.0, -1.0).astype(F32)
-    return fraction, weight, sign
-
-
-def first_row(shape):
-    return lax.broadcasted_iota(jnp.int32, shape, 0) == 0
-
-
-def to_planes(t_ref, cos_fields, sin_fields, out_ref):
-    sign = mode_rows(0)[2][:, :1]
+def column_tables():
+    row = np.arange(HALF)
+    modes = [2 * ((row // 32 % 4 * 2 + row // 128) * 32 + row % 32) + odd for odd in range(2)]
+    columns = [mode / MODES for mode in modes]
+    columns += [np.where(mode == 0, 1.0 / PLANES, 2.0 / PLANES) for mode in modes]
+    columns.append(np.where(row % 2 == 0, 1.0, -1.0))
+    return np.repeat(np.stack(columns).astype(np.float32)[:, :, None], LANES, axis=2)
+
+
+def signs(c_ref, width):
+    return jnp.concatenate([c_ref[4]] * (width // LANES), axis=1)
+
+
+def without_first(value):
+    head = lax.broadcasted_iota(jnp.int32, (8, value.shape[1]), 0) == 0
+    return jnp.concatenate([jnp.where(head, 0.0, value[:8]), value[8:]], axis=0)
+
+
+def to_planes(t_ref, c_ref, cos_fields, sin_fields, out_ref):
+    sign = signs(c_ref, cos_fields[0].shape[1])
     cos_even, cos_odd = apply(t_ref, 0, cos_fields[0]), apply(t_ref, 1, cos_fields[1])
     sin_even, sin_odd = apply(t_ref, 2, sin_fields[0]), apply(t_ref, 3, sin_fields[1])
     quarter_cos = jnp.sum(sign * cos_fields[0], axis=0, keepdims=True)
@@ -442,14 +449,11 @@
     out_ref[3, 0:1] = quarter_cos + quarter_sin
 
 
-def from_planes(t_ref, values):
-    shape = values[0].shape
-    sign = mode_rows(0)[2][:, :1]
-    first = first_row(shape)
+def from_planes(t_ref, c_ref, values):
+    sign = signs(c_ref, values[0].shape[1])
     quarter, three = values[1][0:1], values[3][0:1]
     one = values[0]
-    two = jnp.where(first, 0.0, values[1])
-    four = jnp.where(first, 0.0, values[3])
+    two, four = without_first(values[1]), without_first(values[3])
     plus, minus = one + two, one - two
     plus_far, minus_far = values[2] + four, values[2] - four
     a_even = apply(t_ref, 4, plus + plus_far) + sign * (quarter + three)
@@ -459,49 +463,50 @@
     return (a_even, b_even), (a_odd, b_odd)
 
 
-def state_planes(parts, t_ref, out_ref):
+def state_planes(parts, t_ref, c_ref, out_ref):
     cos_fields, sin_fields = [], []
     for odd in range(2):
         real, imag = parts[odd]
-        fraction = mode_rows(odd)[0]
+        fraction = c_ref[odd]
         cos_fields.append(jnp.concatenate([real, -fraction * imag], axis=1))
         sin_fields.append(jnp.concatenate([imag, fraction * real], axis=1))
-    to_planes(t_ref, cos_fields, sin_fields, out_ref)
-
-
-def first_stage(u_ref, t_ref, planes, out_ref):
+    to_planes(t_ref, c_ref, cos_fields, sin_fields, out_ref)
+
+
+def first_stage(u_ref, t_ref, c_ref, planes, out_ref):
     parts = parts_of(u_ref)
-    state_planes(parts, t_ref, planes)
+    state_planes(parts, t_ref, c_ref, planes)
     values = [planes[at, :, :LANES] * planes[at, :, LANES:] for at in range(4)]
-    found = from_planes(t_ref, values)
+    found = from_planes(t_ref, c_ref, values)
     out = []
     for odd in range(2):
-        weight = mode_rows(odd)[1]
+        weight = c_ref[2 + odd]
         out.append(tuple(parts[odd][c] - weight * found[odd][c] for c in range(2)))
     parts_to(out_ref, out)
 
 
-def adjoint_planes(s_ref, t_ref, out_ref):
+def adjoint_planes(s_ref, t_ref, c_ref, out_ref):
     parts = parts_of(s_ref)
-    weights = [mode_rows(odd)[1] for odd in range(2)]
+    weights = [c_ref[2 + odd] for odd in range(2)]
     to_planes(
         t_ref,
+        c_ref,
         [weights[odd] * parts[odd][0] for odd in range(2)],
         [weights[odd] * parts[odd][1] for odd in range(2)],
         out_ref,
     )
 
 
-def finish(t_ref, s_ref, planes, adjoint, out_ref):
+def finish(t_ref, c_ref, s_ref, planes, adjoint, out_ref):
     values = []
     for at in range(4):
         factor = adjoint[at]
         values.append(planes[at] * jnp.concatenate([factor, factor], axis=1))
-    found = from_planes(t_ref, values)
+    found = from_planes(t_ref, c_ref, values)
     parts = parts_of(s_ref)
     out = []
     for odd in range(2):
-        fraction = mode_rows(odd)[0]
+        fraction = c_ref[odd]
         a, b = found[odd]
         out.append(
             (
@@ -601,6 +606,8 @@
     inverse_ref,
     d_ref,
     t_hbm,
+    c_hbm,
+    f_hbm,
     out_hbm,
     cotangent_in,
     t_ref,
@@ -617,6 +624,7 @@
     u_planes,
     planes,
     s_planes,
+    c_ref,
     ready,
     blank,
     send_sems,
@@ -639,6 +647,12 @@
     table_copy = pltpu.make_async_copy(t_hbm, t_ref, copy_sems.at[1])
     cotangent_copy.start()
     table_copy.start()
+    constant_copies = [
+        pltpu.make_async_copy(c_hbm, c_ref, copy_sems.at[6]),
+        pltpu.make_async_copy(f_hbm, faces, copy_sems.at[7]),
+    ]
+    for copy in constant_copies:
+        copy.start()
     barrier = pltpu.get_barrier_semaphore()
 
     def greet(semaphore, other, place):
@@ -789,11 +803,13 @@
 
     stiffness_tables(d_ref, k_ref)
     table_copy.wait()
+    for copy in constant_copies:
+        copy.wait()
 
     wait_either(double, blank, 2 * (N_MODE - 1) * N_MER, (N_MODE - 1) * N_MER, recv_sems.at[0])
 
     def first(slot):
-        first_stage(plane_in.at[0, slot], t_ref, u_planes.at[slot], plane_out.at[0, slot])
+        first_stage(plane_in.at[0, slot], t_ref, c_ref, u_planes.at[slot], plane_out.at[0, slot])
 
     each_slot(first)
     pl.semaphore_wait(ready, N_MODE - 1)
@@ -812,14 +828,14 @@
         solve(mode_in.at[1], mode_out.at[1], half, True, False, True, solve_scratch, emit)
 
     def multiplier(slot):
-        adjoint_planes(plane_in.at[1, slot], t_ref, s_planes.at[slot])
+        adjoint_planes(plane_in.at[1, slot], t_ref, c_ref, s_planes.at[slot])
 
     wait_planes(6, whole=True)
     each_slot(multiplier)
 
     def second(slot):
-        state_planes(parts_of(plane_in.at[2, slot]), t_ref, planes)
-        finish(t_ref, plane_in.at[1, slot], planes, s_planes.at[slot], plane_out.at[1, slot])
+        state_planes(parts_of(plane_in.at[2, slot]), t_ref, c_ref, planes)
+        finish(t_ref, c_ref, plane_in.at[1, slot], planes, s_planes.at[slot], plane_out.at[1, slot])
 
     wait_planes(8)
     each_slot(second)
@@ -831,9 +847,9 @@
         solve(mode_in.at[2], mode_out.at[2], half, False, True, True, solve_scratch, emit)
 
     def third(slot):
-        adjoint_planes(plane_in.at[3, slot], t_ref, s_planes.at[slot])
+        adjoint_planes(plane_in.at[3, slot], t_ref, c_ref, s_planes.at[slot])
         finish(
-            t_ref, plane_in.at[3, slot], u_planes.at[slot], s_planes.at[slot], plane_out.at[2, slot]
+            t_ref, c_ref, plane_in.at[3, slot], u_planes.at[slot], s_planes.at[slot], plane_out.at[2, slot]
         )
         native_in[slot, mode] = plane_out[2, slot, :, mine]
 
@@ -864,7 +880,7 @@
         copy.wait()
 
 
-def program(state, cotangent, mass, inverse, derivative, table):
+def program(state, cotangent, mass, inverse, derivative, *constants):
     by_mode = (2, N_MODE, N_MER, 8, LANES)
     by_native = (2, N_MODE, 2, 8, 8, LANES)
     by_plane = (2, 2, COUNT // 2, 8, LANES)
@@ -877,12 +893,12 @@
     return pl.pallas_call(
         program_kernel,
         out_shape=jax.ShapeDtypeStruct((GROUPS, 2, 8, 8, LANES), F32),
-        in_specs=[vmem, hbm, vmem, vmem, vmem, hbm],
+        in_specs=[vmem, hbm, vmem, vmem, vmem, hbm, hbm, hbm],
         out_specs=hbm,
         scratch_shapes=[
             pltpu.VMEM((NODE, NODE, ELEM_DEV * LANES), F32),
             pltpu.VMEM((8, 2 * HALF, HALF), BF16),
-            pltpu.SemaphoreType.DMA((6,)),
+            pltpu.SemaphoreType.DMA((8,)),
             pltpu.VMEM((PADDED * ELEM_DEV, LANES), F32),
             scratch(2, by_native),
             pltpu.VMEM(by_native, F32),
@@ -895,6 +911,7 @@
             scratch(2, (4, HALF, 2 * LANES)),
             scratch(4, (HALF, 2 * LANES)),
             scratch(2, (4, HALF, LANES)),
+            scratch(5, (HALF, LANES)),
             pltpu.SemaphoreType.REGULAR,
             pltpu.VMEM((2 * COUNT, 8, LANES), F32),
             pltpu.SemaphoreType.DMA((15,)),
@@ -905,12 +922,14 @@
             collective_id=0, has_side_effects=True, vmem_limit_bytes=60 << 20
         ),
         name="program",
-    )(state, cotangent, mass, inverse, derivative, table)
+    )(state, cotangent, mass, inverse, derivative, *constants)
 
 
 def shards(cotangent, checkpoint, mass, inv_radius_sq, derivative):
-    table = jnp.asarray(tables())
-    return tiles_to_native(program(checkpoint, cotangent, mass, inv_radius_sq, derivative, table))
+    constants = [jnp.asarray(values()) for values in (tables, column_tables, face_tables)]
+    return tiles_to_native(
+        program(checkpoint, cotangent, mass, inv_radius_sq, derivative, *constants)
+    )
 
 
 def solution(mesh):

time: 99.2 us -> 100 us (level)
  Pallas kernels: 98.9 us -> 99.9 us
where the time goes in v13:
time: 100 us
  Pallas kernels  99.9 us (100%)
    pallas_call x1, Pallas kernels, program(): pl.pallas_call(program_kernel, out_shape=jax.ShapeDtypeStruct((GROUPS, 2,...  97.6 us
    pallas_call x1, Pallas kernels, tiles_to_native(): pl.pallas_call(tiles_to_native_kernel, out_shape=jax.ShapeDtypeStruct(sha...  2.28 us

profile of v13, /device:TPU:1, one launch (start us, length us, event | category | flops | bytes accessed | tf_op | source)
XLA Modules:
  0.0 100.0 jit_solution(6980404926647737749)
XLA Ops:
  0.0 97.6 %program.1.t_hbm = f32[11,2,8,8,128]{4,3,2,1,0:T(8,128)} custom-call(f32[9,9,2048]{2,1,0:T(8,128)} %state_ref.1, f32[9,9,2048]{2,1,0:T(8,128)} %cotangent_hbm.1, f32[9,9,16]{2,1,0:T(8,128)} %mass_ref.1, f32[9,9,16]{2,1,0:T(8,128)} %inverse_ref.1, f32[9,9]{1,0:T(8,128)} %d_ref.1, bf16[8,512,256]{2,1,0:T(8,128)(2,1)} %constant.6.clone.t_hbm, ...), custom_call_target="tpu_custom_call" | custom-call | tf_op jit(solution)/shard_map/program/pallas_call | solution.py:893
  97.6 2.3 %tiles_to_native.1 = f32[9,9,2048]{2,1,0:T(8,128)} custom-call(f32[11,2,8,8,128]{4,3,2,1,0:T(8,128)} %program.1.t_hbm), custom_call_target="tpu_custom_call" | custom-call | tf_op jit(solution)/shard_map/tiles_to_native/pallas_call | solution.py:126
